TPU v7x, 32 devices: a whole 2x2x4 slice. The times are simulated.
32 devices in a mesh: vol: 8 (over z, y), dsg: 4 (over x, core).
Axes of the slice: x: 2, y: 2, z: 4, core: 2. Of those that a mesh axis runs over, the one named last changes fastest.
Arguments:
- fields: float32 [32768, 128], P('vol'), may hold values from -6 to 6
- far_geom: float32 [8, 16384], P(None, ('vol', 'dsg')), may hold values from -6 to 6, as said below
- far_block: int32 [16384, 1], P(('vol', 'dsg')), may hold values from 0 to 7; in each aligned block of 512 rows (0 to 511, 512 to 1023, ...) at most 160 rows name the same one
- far_cell: int32 [16384], P(('vol', 'dsg')), may hold values from 0 to 4095
- far_patch: int32 [16384], P(('vol', 'dsg')), may hold values from 0 to 95, as said below
- near_geom: float32 [8, 65536], P(None, ('vol', 'dsg')), may hold values from -6 to 6, as said below
- near_cell: int32 [65536], P(('vol', 'dsg')), may hold values from 0 to 4095
- near_patch: int32 [65536], P(('vol', 'dsg')), may hold values from 0 to 95, as said below
- adjacency: int32 [96, 4], replicated, may hold values from -1 to 95, as said below
Outputs:
- far_density: float32 [16384], P(('vol', 'dsg'))
- design_grad: float32 [96, 64, 64], P('dsg')
Inputs may be any that keep to these rules, and one draw needn't show every extreme that they name: `far_geom`: rows 0-2 and 6-7 lie in [0, 1). `near_geom`: rows 0-2 and 6-7 lie in [0, 1). `far_block`: the 512 far points of one device name each block at most 160 times. `far_patch`: the far and near points of one device lie on at most 4 design patches, the same set for both. `near_patch`: the far and near points of one device lie on at most 4 design patches, the same set for both. -1 marks a free side; where adjacency[k, s] = m >= 0, adjacency[m, s xor 1] = k.
All inputs are finite; a program needn't handle non-finite values.
Results may differ from a plain program's by a relative error of at most 0.0003.
Values sent between devices are 32-bit elements; how exact they have to be, the bound alone decides.
No kernel may reach another device: no remote copies, remote signals or barrier semaphores. Data moves between devices by JAX's collectives and lax.ppermute only.
A program may use at most 128 MiB of HBM per device.

v0:
```python
import functools

import jax
import jax.numpy as jnp
import numpy as np
from jax import lax
from jax.experimental import pallas as pl
from jax.experimental.pallas import tpu as pltpu
from jax.sharding import PartitionSpec as P

CTRL = 64
GROUP = 4
LANES = 128
PENALTY = 4.0
SMOOTHING = 16.0
NO_PATCH = 1.0e6
GRID_ROWS = GROUP // 2 * CTRL
PAYLOAD_ROWS = GRID_ROWS + GROUP * 8
F32 = jnp.float32
BF16 = jnp.bfloat16
EXACT = lax.Precision.HIGHEST
VMEM = pl.BlockSpec(memory_space=pltpu.VMEM)
SMEM = pl.BlockSpec(memory_space=pltpu.SMEM)
ANY = pl.BlockSpec(memory_space=pl.ANY)


def params(megabytes):
    return pltpu.CompilerParams(vmem_limit_bytes=megabytes << 20)


def constants():
    order = np.arange(1, CTRL + 1)
    basis = np.sqrt(2.0 / (CTRL + 1)) * np.sin(np.pi * np.outer(order, order) / (CTRL + 1))
    eigen = 1.0 + SMOOTHING * (2.0 - 2.0 * np.cos(np.pi * order / (CTRL + 1)))
    damp = 1.0 / eigen
    keep = 1.0 - damp
    powers = [keep**k * damp for k in range(3)]
    ends = [basis[:, 0], basis[:, CTRL - 1]]
    edge_rows = np.zeros((8, CTRL))
    scale_rows = np.zeros((8, CTRL))
    for k in range(3):
        for side in range(2):
            edge_rows[2 * k + side] = powers[k] * ends[side]
            scale_rows[2 * k + side] = powers[k]
    series = sum(np.outer(keep**k * damp, keep**k * damp) for k in range(4))

    def coupling(k):
        f = powers[k]
        lane = [0, 2, 1, 3]
        out = np.zeros((4 * CTRL, 4 * CTRL))
        for a, side_in in enumerate(lane):
            for b, side_out in enumerate(lane):
                q_in, q_out = ends[side_in % 2], ends[side_out % 2]
                if side_in // 2 == side_out // 2:
                    block = np.diag(f * np.sum(q_in * q_out * f))
                else:
                    block = np.outer(q_out * f, q_in * f)
                out[a * CTRL : (a + 1) * CTRL, b * CTRL : (b + 1) * CTRL] = SMOOTHING * block
        return out

    return dict(
        basis=np.float32(basis),
        basis_pair=np.float32(np.kron(np.eye(2), basis)),
        edge_rows=np.float32(edge_rows),
        scale_rows=np.float32(scale_rows),
        series=np.float32(series),
        coupling=np.float32(np.concatenate([coupling(0), coupling(1)], 1)),
    )


def split3(x):
    high = x.astype(BF16).astype(F32)
    rest = x - high
    mid = rest.astype(BF16).astype(F32)
    return high, mid, rest - mid


def nt(a, b, **kw):
    return lax.dot_general(a, b, (((1,), (1,)), ((), ())), preferred_element_type=F32, **kw)


def nn(a, b, **kw):
    return lax.dot_general(a, b, (((1,), (0,)), ((), ())), preferred_element_type=F32, **kw)


def tn(a, b, **kw):
    return lax.dot_general(a, b, (((0,), (0,)), ((), ())), preferred_element_type=F32, **kw)


def iota(shape, axis):
    return lax.broadcasted_iota(jnp.int32, shape, axis)


def pack_kernel(capacity, geom_ref, block_ref, cell_ref, request_ref, place_ref):
    owners = request_ref.shape[0]
    count = geom_ref.shape[1]
    block = block_ref[...]
    owner_id = iota((owners, count), 0)
    chosen = jnp.where(owner_id == block, 1.0, 0.0).astype(F32)
    earlier = jnp.where(iota((count, count), 0) < iota((count, count), 1), 1.0, 0.0).astype(BF16)
    rank = nn(chosen.astype(BF16), earlier)
    place = jnp.sum(chosen * (rank + (capacity * owner_id).astype(F32)), axis=0, keepdims=True)
    place = place.astype(jnp.int32)
    place_ref[...] = place
    row = iota((8, count), 0)
    values = jnp.where(row < 6, geom_ref[...], jnp.where(row == 6, cell_ref[...].astype(F32), 0.0))
    high, mid, low = split3(values)
    parts = jnp.concatenate([high, mid, low], 0).astype(BF16)
    put = jnp.where(iota((owners * capacity, count), 0) == place, 1.0, 0.0).astype(BF16)
    packed = nt(parts, put)
    packed = (packed[16:24] + packed[8:16]) + packed[0:8]
    for owner in range(owners):
        request_ref[owner] = packed[:, owner * capacity : (owner + 1) * capacity]


def pack_requests(far_geom, far_block, far_cell, owners, capacity):
    count = far_geom.shape[1]
    return pl.pallas_call(
        functools.partial(pack_kernel, capacity),
        out_shape=(
            jax.ShapeDtypeStruct((owners, 8, capacity), F32),
            jax.ShapeDtypeStruct((1, count), jnp.int32),
        ),
        in_specs=[VMEM] * 3,
        out_specs=(VMEM, VMEM),
        compiler_params=params(16),
        name="pack_requests",
    )(far_geom, far_block, far_cell)


def gather_rows(cells, fields_ref, rows_ref, count):
    unroll = 16

    def step(i, carry):
        for u in range(unroll):
            p = i * unroll + u
            rows_ref[pl.ds(p, 1), :] = fields_ref[pl.ds(cells(p), 1), :]
        return carry

    lax.fori_loop(0, count // unroll, step, 0)


def bernstein(t):
    u = 1.0 - t
    uu, tt = u * u, t * t
    values = [uu * u, 3.0 * t * uu, 3.0 * tt * u, tt * t]
    tu = 6.0 * t * u
    slopes = [-3.0 * uu, 3.0 * uu - tu, tu - 3.0 * tt, 3.0 * tt]
    return values, slopes


def tile_density(columns, geom):
    row = iota((8, LANES), 0)
    wide = [jnp.broadcast_to(geom[r : r + 1], (8, LANES)) for r in range(3)]
    x_val, x_der = bernstein(wide[0])
    y_val, y_der = bernstein(wide[1])
    z_val, z_der = bernstein(wide[2])
    k = row % 4

    def by_k(v):
        return jnp.where(k == 0, v[0], jnp.where(k == 1, v[1], jnp.where(k == 2, v[2], v[3])))

    def by_j(v, m):
        return jnp.where(row < 4, v[2 * m], v[2 * m + 1])

    z_v, z_d = by_k(z_val), by_k(z_der)
    yz = [by_j(y_val, m) * z_v for m in range(2)]
    dyz = [by_j(y_der, m) * z_v for m in range(2)]
    ydz = [by_j(y_val, m) * z_d for m in range(2)]
    sums = []
    for half in range(2):
        total = [None] * 4
        for i in range(4):
            at = half * 64 + i * 16
            first, second = columns[at : at + 8], columns[at + 8 : at + 16]
            plain = first * yz[0] + second * yz[1]
            along_y = first * dyz[0] + second * dyz[1]
            along_z = first * ydz[0] + second * ydz[1]
            terms = [x_val[i] * plain, x_der[i] * plain, x_val[i] * along_y, x_val[i] * along_z]
            total = [t if s is None else s + t for s, t in zip(total, terms)]
        sums.append([jnp.sum(t, axis=0, keepdims=True) for t in total])
    state, adjoint = sums
    n = [geom[3 + r : 4 + r] for r in range(3)]
    normal_sq = n[0] * n[0] + n[1] * n[1] + n[2] * n[2]
    inner = state[1] * adjoint[1] + state[2] * adjoint[2] + state[3] * adjoint[3]
    along_s = state[1] * n[0] + state[2] * n[1] + state[3] * n[2]
    along_a = adjoint[1] * n[0] + adjoint[2] * n[1] + adjoint[3] * n[2]
    return normal_sq * inner - 2.0 * along_s * along_a + PENALTY * normal_sq * state[0] * adjoint[0]


def densities(rows_ref, geom_ref, out_ref, count):
    def step(tile, carry):
        at = pl.multiple_of(tile * LANES, LANES)
        columns = rows_ref[pl.ds(at, LANES), :].T
        out_ref[:, pl.ds(at, LANES)] = tile_density(columns, geom_ref[:, pl.ds(at, LANES)])
        return carry

    lax.fori_loop(0, count // LANES, step, 0)


def near_kernel(cell_ref, fields_ref, geom_ref, out_ref, rows_ref):
    count = geom_ref.shape[1]
    gather_rows(lambda p: cell_ref[p], fields_ref, rows_ref, count)
    densities(rows_ref, geom_ref, out_ref, count)


def near_densities(near_cell, fields, near_geom):
    count = near_geom.shape[1]
    return pl.pallas_call(
        near_kernel,
        out_shape=jax.ShapeDtypeStruct((1, count), F32),
        in_specs=[SMEM, VMEM, VMEM],
        out_specs=VMEM,
        scratch_shapes=[pltpu.VMEM((count, LANES), F32)],
        compiler_params=params(24),
        cost_estimate=pl.CostEstimate(flops=40_000_000, bytes_accessed=4_000_000, transcendentals=0),
        name="near_densities",
    )(near_cell, fields, near_geom)


def far_kernel(request_ref, fields_ref, out_ref, query_ref, cell_v, cell_s, rows_ref, dens_ref, sem):
    owners, _, capacity = request_ref.shape
    count = owners * capacity
    for o in range(owners):
        query_ref[:, o * capacity : (o + 1) * capacity] = request_ref[o]
    cell_v[...] = query_ref[6:7, :].astype(jnp.int32)
    copy = pltpu.make_async_copy(cell_v, cell_s, sem)
    copy.start()
    copy.wait()
    gather_rows(lambda p: cell_s[0, p], fields_ref, rows_ref, count)
    densities(rows_ref, query_ref, dens_ref, count)
    for o in range(owners):
        out_ref[o] = dens_ref[:, o * capacity : (o + 1) * capacity]


def far_answers(requests, fields):
    owners, _, capacity = requests.shape
    count = owners * capacity
    return pl.pallas_call(
        far_kernel,
        out_shape=jax.ShapeDtypeStruct((owners, 1, capacity), F32),
        in_specs=[VMEM, VMEM],
        out_specs=VMEM,
        scratch_shapes=[
            pltpu.VMEM((8, count), F32),
            pltpu.VMEM((1, count), jnp.int32),
            pltpu.SMEM((1, count), jnp.int32),
            pltpu.VMEM((count, LANES), F32),
            pltpu.VMEM((1, count), F32),
            pltpu.SemaphoreType.DMA,
        ],
        compiler_params=params(24),
        name="far_answers",
    )(requests, fields)


def spline_columns(param):
    scaled = param * float(CTRL - 3)
    start = jnp.clip(jnp.floor(scaled), 0.0, float(CTRL - 4))
    x = scaled - start
    u = 1.0 - x
    cubed, squared = x * x * x, x * x
    weights = [
        u * u * u * (1.0 / 6.0),
        (3.0 * cubed - 6.0 * squared + 4.0) * (1.0 / 6.0),
        (-3.0 * cubed + 3.0 * squared + 3.0 * x + 1.0) * (1.0 / 6.0),
        cubed * (1.0 / 6.0),
    ]
    off = iota((CTRL, param.shape[1]), 0) - start.astype(jnp.int32)
    out = jnp.zeros(off.shape, F32)
    for m in range(4):
        out = jnp.where(off == m, weights[m], out)
    return out


def halves(x):
    high = x.astype(BF16)
    return high, (x - high.astype(F32)).astype(BF16)


def slot_grids(density, s, t, patch, slots):
    left_high, left_low = halves(spline_columns(s))
    right_high, right_low = halves(spline_columns(t) * density)
    masks = [jnp.where(patch == slot, 1.0, 0.0).astype(BF16) for slot in slots]
    high = jnp.concatenate([left_high * m for m in masks], 0)
    low = jnp.concatenate([left_low * m for m in masks], 0)
    return nt(high, right_high) + (nt(high, right_low) + nt(low, right_high))


def near_grid_kernel(dens_ref, geom_ref, near_ref, far_ref, grid_ref, slot_ref):
    near, far = near_ref[...].astype(F32), far_ref[...].astype(F32)
    slots = []
    last = jnp.full((1, 1), -1.0, F32)
    for _ in range(GROUP):
        a = jnp.min(jnp.where(near > last, near, NO_PATCH), axis=1, keepdims=True)
        b = jnp.min(jnp.where(far > last, far, NO_PATCH), axis=1, keepdims=True)
        last = jnp.minimum(a, b)
        slots.append(last)
    slot_ref[...] = jnp.concatenate([jnp.broadcast_to(s, (1, LANES)) for s in slots + slots], 0)
    grid_ref[...] = slot_grids(dens_ref[...], geom_ref[6:7, :], geom_ref[7:8, :], near, slots)


def near_grids(dens, near_geom, near_patch, far_patch):
    return pl.pallas_call(
        near_grid_kernel,
        out_shape=(
            jax.ShapeDtypeStruct((GROUP * CTRL, CTRL), F32),
            jax.ShapeDtypeStruct((8, LANES), F32),
        ),
        in_specs=[VMEM] * 4,
        out_specs=(VMEM, VMEM),
        compiler_params=params(24),
        cost_estimate=pl.CostEstimate(flops=80_000_000, bytes_accessed=1_000_000, transcendentals=0),
        name="near_grids",
    )(dens, near_geom, near_patch, far_patch)


def payload_kernel(
    reply_ref, place_ref, geom_ref, far_ref, slot_ref, near_ref,
    basis_ref, pair_ref, edge_ref, scale_ref,
    dens_ref, out_ref, flat_ref,
):
    owners, _, capacity = reply_ref.shape
    count = geom_ref.shape[1]
    for o in range(owners):
        flat_ref[:, o * capacity : (o + 1) * capacity] = reply_ref[o]
    high, mid, low = split3(flat_ref[...])
    parts = jnp.concatenate([high, mid, low, jnp.zeros((5, owners * capacity), F32)], 0).astype(BF16)
    put = jnp.where(iota((owners * capacity, count), 0) == place_ref[...], 1.0, 0.0).astype(BF16)
    got = nn(parts, put)
    dens = (got[2:3] + got[1:2]) + got[0:1]
    dens_ref[...] = dens
    slots = [slot_ref[s : s + 1, 0:1] for s in range(GROUP)]
    grids = near_ref[...] + slot_grids(
        dens, geom_ref[6:7, :], geom_ref[7:8, :], far_ref[...].astype(F32), slots
    )
    lane = iota((1, LANES), 1)
    names = jnp.zeros((1, LANES), F32)
    for s in range(GROUP):
        names = jnp.where(lane == s, slot_ref[s : s + 1, :], names)
    edge = edge_ref[...]
    scale = scale_ref[...]
    blank = jnp.zeros((8, CTRL), F32)
    both = jnp.concatenate(
        [jnp.concatenate([edge, blank], 1), jnp.concatenate([blank, edge], 1)], 0
    )
    row = iota((8, LANES), 0)
    for pair in range(GROUP // 2):
        a, b = 2 * pair, 2 * pair + 1
        both_grids = jnp.concatenate(
            [grids[a * CTRL : (a + 1) * CTRL], grids[b * CTRL : (b + 1) * CTRL]], 1
        )
        spectral = nn(nn(basis_ref[...], both_grids, precision=EXACT), pair_ref[...], precision=EXACT)
        out_ref[pair * CTRL : (pair + 1) * CTRL, :] = spectral
        along_rows = nn(edge, spectral, precision=EXACT)
        along_cols = nt(both, spectral, precision=EXACT)
        for side, slot in enumerate((a, b)):
            block = jnp.concatenate(
                [
                    along_rows[:, side * CTRL : (side + 1) * CTRL] * scale,
                    along_cols[8 * side : 8 * side + 8] * scale,
                ],
                1,
            )
            block = jnp.where(row == 6, slot_ref[slot : slot + 1, :], jnp.where(row == 7, names, block))
            out_ref[GRID_ROWS + slot * 8 : GRID_ROWS + slot * 8 + 8, :] = block


def make_payload(reply, place, far_geom, far_patch, slots, near_grid, const):
    owners, _, capacity = reply.shape
    count = far_geom.shape[1]
    return pl.pallas_call(
        payload_kernel,
        out_shape=(
            jax.ShapeDtypeStruct((1, count), F32),
            jax.ShapeDtypeStruct((PAYLOAD_ROWS, LANES), F32),
        ),
        in_specs=[VMEM] * 10,
        out_specs=(VMEM, VMEM),
        scratch_shapes=[pltpu.VMEM((1, owners * capacity), F32)],
        compiler_params=params(24),
        name="make_payload",
    )(
        reply, place, far_geom, far_patch, slots, near_grid,
        const["basis"], const["basis_pair"], const["edge_rows"], const["scale_rows"],
    )


def smooth_kernel(
    sources, per_owner, where_ref, adj_ref, coupling_ref, basis_ref, series_ref, edge_ref, scale_ref, *rest
):
    n_in = len(sources)
    payload = rest[:n_in]
    out_ref, buf, name_v, name_s, own, halo_rows, sem, name_sem = rest[n_in:]
    devices = buf.shape[0] // PAYLOAD_ROWS
    copies = []
    for a, (source, ref) in enumerate(zip(sources, payload)):
        rows = ref.shape[0]
        copies.append(
            pltpu.make_async_copy(
                ref, buf.at[pl.ds(pl.multiple_of(where_ref[1 + a] * PAYLOAD_ROWS, 8), rows)], sem.at[a]
            )
        )
        copies[-1].start()
    own[...] = jnp.zeros(own.shape, F32)
    for copy in copies:
        copy.wait()
    name_v[...] = buf[pl.ds(PAYLOAD_ROWS - 1, devices, stride=PAYLOAD_ROWS), :].astype(jnp.int32)
    names = pltpu.make_async_copy(name_v, name_s, name_sem)
    names.start()

    patches = adj_ref.shape[0]
    lane = iota((devices, LANES), 1)

    def edge_rows(r):
        return [
            buf[pl.ds(GRID_ROWS + 8 * s + r, devices, stride=PAYLOAD_ROWS), :] for s in range(GROUP)
        ]

    places = [jnp.where(lane == n.astype(jnp.int32), 1.0, 0.0) for n in edge_rows(6)]
    place = jnp.concatenate(places, 0).astype(BF16)
    sums = []
    for r in range(6):
        parts = [p.astype(BF16) for p in split3(jnp.concatenate(edge_rows(r), 0))]
        sums.append(tn(place, parts[0]) + (tn(place, parts[1]) + tn(place, parts[2])))
    base = [jnp.concatenate([sums[2 * k], sums[2 * k + 1]], 1)[:patches] for k in range(3)]

    adjacency = adj_ref[...]
    column = iota((patches, patches), 1)
    facing = [
        jnp.where(adjacency[:, s : s + 1] == column, 1.0, 0.0).astype(BF16) for s in range(4)
    ]
    low_lane = iota((patches, LANES), 1) < CTRL

    def halo(edges):
        parts = [p.astype(BF16) for p in split3(edges)]

        def look(side, at):
            pieces = [nn(facing[side], p[:, at : at + LANES]) for p in parts]
            return pieces[0] + (pieces[1] + pieces[2])

        first = jnp.where(low_lane, look(0, LANES), look(2, LANES))
        second = jnp.where(low_lane, look(1, 0), look(3, 0))
        return jnp.concatenate([first, second], 1)

    wide = 4 * CTRL
    halo0 = halo(base[0])
    effect0 = nn(halo0, coupling_ref[...], precision=EXACT)
    edges1 = base[0] + base[1] + effect0[:, :wide]
    halo1 = halo(edges1)
    effect1 = nn(halo1, coupling_ref[:, :wide], precision=EXACT)
    edges2 = base[0] + base[1] + base[2] + effect0[:, wide:] + effect1
    halo2 = halo(edges2)

    first_own = where_ref[0] * per_owner
    mine = jnp.where(
        iota((per_owner, patches), 1) == iota((per_owner, patches), 0) + first_own, 1.0, 0.0
    ).astype(BF16)
    scale = scale_ref[...]
    for k, h in enumerate((halo2, halo1, halo0)):
        picked = [nn(mine, p.astype(BF16)) for p in split3(h)]
        picked = picked[0] + (picked[1] + picked[2])
        factor = SMOOTHING * jnp.concatenate([scale[2 * k : 2 * k + 1]] * 2, 1)
        for side in range(2):
            halo_rows[pl.ds(2 * k + side, per_owner, stride=8), :] = (
                picked[:, side * LANES : (side + 1) * LANES] * factor
            )
    zero = jnp.zeros((per_owner, LANES), F32)
    for r in (6, 7):
        halo_rows[pl.ds(r, per_owner, stride=8), :] = zero

    names.wait()

    def add_slot(device, carry):
        for s in range(GROUP):
            patch = name_s[device, s] - first_own

            @pl.when((patch >= 0) & (patch < per_owner))
            def _():
                at = pl.multiple_of(device * PAYLOAD_ROWS + (s // 2) * CTRL, 8)
                block = buf[pl.ds(at, CTRL), :]
                if s % 2:
                    block = pltpu.roll(block, CTRL, 1)
                own_at = pl.multiple_of(patch * CTRL, CTRL)
                own[pl.ds(own_at, CTRL), :] = own[pl.ds(own_at, CTRL), :] + block

        return carry

    lax.fori_loop(0, devices, add_slot, 0)

    basis = basis_ref[...]
    series = series_ref[...]
    edge = edge_ref[...]

    def finish(patch, carry):
        at = pl.multiple_of(patch * CTRL, CTRL)
        rows = halo_rows[pl.ds(pl.multiple_of(patch * 8, 8), 8), :]
        left = jnp.concatenate([edge, rows[:, CTRL:]], 0)
        right = jnp.concatenate([rows[:, :CTRL], edge], 0)
        spectral = own[pl.ds(at, CTRL), :][:, :CTRL] * series + tn(left, right, precision=EXACT)
        out_ref[patch] = nn(nn(basis, spectral, precision=EXACT), basis, precision=EXACT)
        return carry

    lax.fori_loop(0, per_owner, finish, 0, unroll=4)


def smooth(payloads, sources, where, adjacency, owners, devices, const):
    per_owner = adjacency.shape[0] // owners
    return pl.pallas_call(
        functools.partial(smooth_kernel, sources, per_owner),
        out_shape=jax.ShapeDtypeStruct((per_owner, CTRL, CTRL), F32),
        in_specs=[SMEM] + [VMEM] * 6 + [ANY] * len(payloads),
        out_specs=VMEM,
        scratch_shapes=[
            pltpu.VMEM((devices * PAYLOAD_ROWS, LANES), F32),
            pltpu.VMEM((devices, LANES), jnp.int32),
            pltpu.SMEM((devices, LANES), jnp.int32),
            pltpu.VMEM((per_owner * CTRL, LANES), F32),
            pltpu.VMEM((per_owner * 8, LANES), F32),
            pltpu.SemaphoreType.DMA((len(payloads),)),
            pltpu.SemaphoreType.DMA,
        ],
        compiler_params=params(48),
        name="smooth",
    )(
        where, adjacency, const["coupling"], const["basis"], const["series"], const["edge_rows"],
        const["scale_rows"], *payloads,
    )


def spread_payload(payload, vol_count, dsg_count):
    if vol_count > 8 or dsg_count != 4:
        whole = lax.all_gather(payload, ("vol", "dsg"), axis=0, tiled=True)
        return [None], [whole]
    sources, arrays = [(0, 0)], [payload]
    for k in range(1, vol_count):
        sources.append((k, 0))
        arrays.append(lax.ppermute(payload, "vol", [(i, i ^ k) for i in range(vol_count)]))
    for offset in (2, 1):
        pairs = [(i, i ^ offset) for i in range(dsg_count)]
        for (a, b), array in list(zip(sources, arrays)):
            sources.append((a, b ^ offset))
            arrays.append(lax.ppermute(array, "dsg", pairs))
    return sources, arrays


def per_device(
    fields, far_geom, far_block, far_cell, far_patch, near_geom, near_cell, near_patch, adjacency
):
    vol_count, dsg_count = lax.axis_size("vol"), lax.axis_size("dsg")
    vol_at, dsg_at = lax.axis_index("vol"), lax.axis_index("dsg")
    far_count = far_cell.shape[0]
    capacity = 5 * far_count // (2 * vol_count)
    const = {name: jnp.asarray(value) for name, value in constants().items()}

    request, place = pack_requests(
        far_geom, far_block.reshape(1, -1), far_cell.reshape(1, -1), vol_count, capacity
    )
    asked = lax.all_to_all(request, "vol", split_axis=0, concat_axis=0, tiled=True)
    near_dens = near_densities(near_cell, fields, near_geom)
    answer = far_answers(asked, fields)
    reply = lax.all_to_all(answer, "vol", split_axis=0, concat_axis=0, tiled=True)
    near_patch, far_patch = near_patch.reshape(1, -1), far_patch.reshape(1, -1)
    near_grid, slots = near_grids(near_dens, near_geom, near_patch, far_patch)
    far_dens, payload = make_payload(reply, place, far_geom, far_patch, slots, near_grid, const)

    sources, arrays = spread_payload(payload, vol_count, dsg_count)
    where = [dsg_at]
    for source in sources:
        if source is None:
            where.append(jnp.int32(0))
        else:
            where.append((vol_at ^ source[0]) * dsg_count + (dsg_at ^ source[1]))
    where = jnp.stack([w.astype(jnp.int32) for w in where])
    design = smooth(arrays, sources, where, adjacency, dsg_count, vol_count * dsg_count, const)
    return far_dens.reshape(-1), design


def solution(mesh):
    return jax.shard_map(
        per_device,
        mesh=mesh,
        in_specs=(
            P("vol", None),
            P(None, ("vol", "dsg")),
            P(("vol", "dsg"), None),
            P(("vol", "dsg")),
            P(("vol", "dsg")),
            P(None, ("vol", "dsg")),
            P(("vol", "dsg")),
            P(("vol", "dsg")),
            P(),
        ),
        out_specs=(P(("vol", "dsg")), P("dsg", None, None)),
        check_vma=False,
    )
```

profile of v0, /device:TPU:0, one launch (start us, length us, event | category | flops | bytes accessed | tf_op | source)
XLA Modules:
  0.0 90.6 jit_solution(17228924240916409779)
XLA Ops:
  0.6 0.0 copy-start.5
  0.7 0.7 copy-done.5
  1.4 0.7 copy-done.13
  2.1 0.7 copy-done.14
  2.8 0.8 pack_requests.1
  3.5 14.0 %all_to_all.10.request_ref = f32[8,8,160]{2,1,0:T(8,128)S(1)} all-to-all(f32[8,8,160]{2,1,0:T(8,128)S(1)} %get-tuple-element.8), channel_id=1, replica_groups=mesh['vol'=8,'dsg'=4] {'vol'}, dimensions={0} | all-to-all | bytes 81920 | tf_op jit(solution)/shard_map/all_to_all | solution.py:559
  17.5 1.6 %copy-done = f32[4096,128]{1,0:T(8,128)S(1)} copy-done((f32[4096,128]{1,0:T(8,128)S(1)}, f32[4096,128]{1,0:T(8,128)}, u32[]{:S(2)}) %copy-start) | copy-done | bytes 2097176
  19.1 0.0 copy-start.6
  19.1 0.0 copy-start.7
  19.1 0.0 copy-start.9
  19.1 0.0 copy-start.10
  19.2 0.0 copy-start.16
  19.2 0.0 copy-start.2
  19.2 0.0 copy-start.8
  19.2 4.0 %far_answers.1 = f32[8,1,160]{2,1,0:T(1,128)} custom-call(f32[8,8,160]{2,1,0:T(8,128)S(1)} %all_to_all.10.request_ref, f32[4096,128]{1,0:T(8,128)S(1)} %copy-done), custom_call_target="tpu_custom_call" | custom-call | tf_op jit(solution)/shard_map/far_answers/pallas_call | solution.py:239
  23.2 3.3 %all-to-all-start.1 = ((f32[8,1,160]{2,1,0:T(1,128)}), f32[8,1,160]{2,1,0:T(1,128)S(1)}, u32[]{:S(2)}, u32[]{:S(2)}) async-start(f32[8,1,160]{2,1,0:T(1,128)} %far_answers.1), calls=%async_computation.1 | async-start | bytes 16384 | tf_op jit(solution)/shard_map/all_to_all | solution.py:562
  26.6 4.9 %near_densities.1.dens_ref = f32[1,2048]{1,0:T(1,128)S(1)} custom-call(s32[2048]{0:T(1024)S(1)} %copy-done.11, f32[4096,128]{1,0:T(8,128)S(1)} %copy-done.1, f32[8,2048]{1,0:T(8,128)S(1)} %copy-done.4), custom_call_target="tpu_custom_call" | custom-call | flops 40000000 | bytes 4000000 | tf_op jit(solution)/shard_map/near_densities/pallas_call | solution.py:209
  31.5 1.4 %near_grids.1 = (f32[256,64]{1,0:T(8,128)S(1)}, f32[8,128]{1,0:T(8,128)S(1)}) custom-call(f32[1,2048]{1,0:T(1,128)S(1)} %near_densities.1.dens_ref, f32[8,2048]{1,0:T(8,128)S(1)} %copy-done.4, s32[1,2048]{1,0:T(1,128)S(1)} %bitcast.42, s32[1,512]{1,0:T(1,128)S(1)} %bitcast.38), custom_call_target="tpu_custom_call" | custom-call | flops 80000000 | bytes 1000000 | tf_op jit(solution)/shard_map/near_grids/pallas_call | solution.py:304
  32.9 0.2 all-to-all-done.1.reply_ref
  33.1 1.9 %make_payload.1 = (f32[1,512]{1,0:T(1,128)}, f32[160,128]{1,0:T(8,128)S(1)}) custom-call(f32[8,1,160]{2,1,0:T(1,128)S(1)} %all-to-all-done.1.reply_ref, s32[1,512]{1,0:T(1,128)S(1)} %get-tuple-element.9.place_ref, f32[8,512]{1,0:T(8,128)S(1)} %copy-done.6, s32[1,512]{1,0:T(1,128)S(1)} %bitcast.39, f32[8,128]{1,0:T(8,128)S(1)} %get-tuple-element.10.slot_ref, ...), custom_call_target="tpu_custom_call" | custom-call | tf_op jit(solution)/shard_map/make_payload/pallas_call | solution.py:372
  35.0 0.1 collective-permute-start.15
  35.0 1.6 %collective-permute-start.7 = (f32[160,128]{1,0:T(8,128)S(1)}, f32[160,128]{1,0:T(8,128)S(1)}, u32[]{:S(2)}, u32[]{:S(2)}) collective-permute-start(f32[160,128]{1,0:T(8,128)S(1)} %get-tuple-element.13.rest_0_), channel_id=1, source_target_pairs={{0,2},{1,3},{2,0},{3,1},{4,6},{5,7},{6,4},{7,5},{8,10},{9,11},{10,... | collective-permute-start | bytes 245768 | tf_op jit(solution)/shard_map/ppermute | solution.py:543
  36.6 4.5 %collective-permute-start.6 = (f32[160,128]{1,0:T(8,128)S(1)}, f32[160,128]{1,0:T(8,128)S(1)}, u32[]{:S(2)}, u32[]{:S(2)}) collective-permute-start(f32[160,128]{1,0:T(8,128)S(1)} %get-tuple-element.13.rest_0_), channel_id=1, source_target_pairs={{0,28},{4,24},{8,20},{12,16},{16,12},{20,8},{24,4},{28,0},{1,29},{... | collective-permute-start | bytes 245768 | tf_op jit(solution)/shard_map/ppermute | solution.py:538
  41.1 0.5 collective-permute-start.5
  41.6 0.6 collective-permute-start.4
  42.2 0.0 collective-permute-done.15.rest_16_
  42.2 2.0 %collective-permute-start.3 = (f32[160,128]{1,0:T(8,128)S(1)}, f32[160,128]{1,0:T(8,128)S(1)}, u32[]{:S(2)}, u32[]{:S(2)}) collective-permute-start(f32[160,128]{1,0:T(8,128)S(1)} %get-tuple-element.13.rest_0_), channel_id=1, source_target_pairs={{0,16},{4,20},{8,24},{12,28},{16,0},{20,4},{24,8},{28,12},{1,17},{... | collective-permute-start | bytes 245768 | tf_op jit(solution)/shard_map/ppermute | solution.py:538
  44.2 0.0 collective-permute-done.7.rest_8_
  44.3 2.2 %collective-permute-start.2 = (f32[160,128]{1,0:T(8,128)S(1)}, f32[160,128]{1,0:T(8,128)S(1)}, u32[]{:S(2)}, u32[]{:S(2)}) collective-permute-start(f32[160,128]{1,0:T(8,128)S(1)} %get-tuple-element.13.rest_0_), channel_id=1, source_target_pairs={{0,12},{4,8},{8,4},{12,0},{16,28},{20,24},{24,20},{28,16},{1,13},{... | collective-permute-start | bytes 245768 | tf_op jit(solution)/shard_map/ppermute | solution.py:538
  46.5 0.0 collective-permute-done.6.rest_7_
  46.5 4.2 %collective-permute-start.1 = (f32[160,128]{1,0:T(8,128)S(1)}, f32[160,128]{1,0:T(8,128)S(1)}, u32[]{:S(2)}, u32[]{:S(2)}) collective-permute-start(f32[160,128]{1,0:T(8,128)S(1)} %get-tuple-element.13.rest_0_), channel_id=1, source_target_pairs={{0,8},{4,12},{8,0},{12,4},{16,24},{20,28},{24,16},{28,20},{1,9},{5... | collective-permute-start | bytes 245768 | tf_op jit(solution)/shard_map/ppermute | solution.py:538
  50.7 0.0 collective-permute-done.5.rest_6_
  50.7 1.7 %collective-permute-start = (f32[160,128]{1,0:T(8,128)S(1)}, f32[160,128]{1,0:T(8,128)S(1)}, u32[]{:S(2)}, u32[]{:S(2)}) collective-permute-start(f32[160,128]{1,0:T(8,128)S(1)} %get-tuple-element.13.rest_0_), channel_id=1, source_target_pairs={{0,4},{4,0},{8,12},{12,8},{16,20},{20,16},{24,28},{28,24},{1,5},{5... | collective-permute-start | bytes 245768 | tf_op jit(solution)/shard_map/ppermute | solution.py:538
  52.3 2.2 %collective-permute-done.4.rest_5_ = f32[160,128]{1,0:T(8,128)S(1)} collective-permute-done((f32[160,128]{1,0:T(8,128)S(1)}, f32[160,128]{1,0:T(8,128)S(1)}, u32[]{:S(2)}, u32[]{:S(2)}) %collective-permute-start.4) | collective-permute-done | bytes 81952 | tf_op jit(solution)/shard_map/ppermute | solution.py:538
  54.6 1.0 %collective-permute-done.3.rest_4_ = f32[160,128]{1,0:T(8,128)S(1)} collective-permute-done((f32[160,128]{1,0:T(8,128)S(1)}, f32[160,128]{1,0:T(8,128)S(1)}, u32[]{:S(2)}, u32[]{:S(2)}) %collective-permute-start.3) | collective-permute-done | bytes 81952 | tf_op jit(solution)/shard_map/ppermute | solution.py:538
  55.6 0.0 collective-permute-start.22
  55.6 0.0 collective-permute-done.2.rest_3_
  55.6 0.5 collective-permute-start.14
  56.2 0.0 collective-permute-done.1.rest_2_
  56.2 0.2 collective-permute-start.21
  56.4 1.5 %collective-permute-start.13 = (f32[160,128]{1,0:T(8,128)S(1)}, f32[160,128]{1,0:T(8,128)S(1)}, u32[]{:S(2)}, u32[]{:S(2)}) collective-permute-start(f32[160,128]{1,0:T(8,128)S(1)} %collective-permute-done.5.rest_6_), channel_id=1, source_target_pairs={{0,2},{1,3},{2,0},{3,1},{4,6},{5,7},{6,4},{7,5},{8,10},{9,11},{10,... | collective-permute-start | bytes 245768 | tf_op jit(solution)/shard_map/ppermute | solution.py:543
  57.9 0.0 collective-permute-start.20
  57.9 0.6 collective-permute-start.12
  58.5 2.4 %collective-permute-done.14.rest_15_ = f32[160,128]{1,0:T(8,128)S(1)} collective-permute-done((f32[160,128]{1,0:T(8,128)S(1)}, f32[160,128]{1,0:T(8,128)S(1)}, u32[]{:S(2)}, u32[]{:S(2)}) %collective-permute-start.14) | collective-permute-done | bytes 81952 | tf_op jit(solution)/shard_map/ppermute | solution.py:543
  60.9 0.4 collective-permute-start.11
  61.3 1.3 %collective-permute-done.13.rest_14_ = f32[160,128]{1,0:T(8,128)S(1)} collective-permute-done((f32[160,128]{1,0:T(8,128)S(1)}, f32[160,128]{1,0:T(8,128)S(1)}, u32[]{:S(2)}, u32[]{:S(2)}) %collective-permute-start.13) | collective-permute-done | bytes 81952 | tf_op jit(solution)/shard_map/ppermute | solution.py:543
  62.6 0.5 collective-permute-start.10
  63.2 0.8 collective-permute-done.12.rest_13_
  64.0 0.9 collective-permute-start.9
  64.9 0.9 collective-permute-done.11.rest_12_
  65.8 0.5 collective-permute-start.8
  66.3 1.6 %collective-permute-done.10.rest_11_ = f32[160,128]{1,0:T(8,128)S(1)} collective-permute-done((f32[160,128]{1,0:T(8,128)S(1)}, f32[160,128]{1,0:T(8,128)S(1)}, u32[]{:S(2)}, u32[]{:S(2)}) %collective-permute-start.10) | collective-permute-done | bytes 81952 | tf_op jit(solution)/shard_map/ppermute | solution.py:543
  67.9 0.5 collective-permute-start.29
  68.4 1.2 %collective-permute-done.9.rest_10_ = f32[160,128]{1,0:T(8,128)S(1)} collective-permute-done((f32[160,128]{1,0:T(8,128)S(1)}, f32[160,128]{1,0:T(8,128)S(1)}, u32[]{:S(2)}, u32[]{:S(2)}) %collective-permute-start.9) | collective-permute-done | bytes 81952 | tf_op jit(solution)/shard_map/ppermute | solution.py:543
  69.7 0.5 collective-permute-start.27
  70.2 0.9 collective-permute-done.8.rest_9_
  71.0 0.5 collective-permute-start.25
  71.6 0.1 collective-permute-start.24
  71.6 0.1 copy.17.adj_ref
  71.7 0.1 stack.135.where_ref
  71.9 0.4 collective-permute-done.26.rest_27_
  72.3 0.2 collective-permute-done.25.rest_26_
  72.5 0.4 collective-permute-done.24.rest_25_
  72.8 17.8 %smooth.1 = f32[24,64,64]{2,1,0:T(8,128)} custom-call(s32[33]{0:T(128)S(1)} %stack.135.where_ref, s32[96,4]{1,0:T(8,128)S(1)} %copy.17.adj_ref, f32[256,512]{1,0:T(8,128)S(1)} %copy-done.2, f32[64,64]{1,0:T(8,128)S(1)} %copy-done.3, f32[64,64]{1,0:T(8,128)S(1)} %copy-done.8, f32[8,64]{1,0:T(8,128)S(1)} %copy-done.10, f32[8,64]{1,0:T(8,128)S(1)} %copy-done.9, ...), custom_call_target="tpu_custom_call" | custom-call | tf_op jit(solution)/shard_map/smooth/pallas_call | solution.py:509
  (43 shorter events, 0.1 us)
Async XLA Ops:
  0.6 26.0 %copy-start.4 = (f32[8,2048]{1,0:T(8,128)S(1)}, f32[8,2048]{1,0:T(8,128)}, u32[]{:S(2)}) copy-start(f32[8,2048]{1,0:T(8,128)} %geom_ref.6) | copy-start | bytes 196612
  0.6 0.8 copy-start.5
  1.4 0.7 copy-start.13
  2.1 0.7 copy-start.14
  2.8 23.8 %copy-start.11 = (s32[2048]{0:T(1024)S(1)}, s32[2048]{0:T(1024)}, u32[]{:S(2)}) copy-start(s32[2048]{0:T(1024)} %cell_ref.1) | copy-start | bytes 24580
  17.5 1.6 %copy-start = (f32[4096,128]{1,0:T(8,128)S(1)}, f32[4096,128]{1,0:T(8,128)}, u32[]{:S(2)}) copy-start(f32[4096,128]{1,0:T(8,128)} %fields_ref.3) | copy-start | bytes 6291460
  19.1 7.5 %copy-start.1 = (f32[4096,128]{1,0:T(8,128)S(1)}, f32[4096,128]{1,0:T(8,128)}, u32[]{:S(2)}) copy-start(f32[4096,128]{1,0:T(8,128)} %fields_ref.3) | copy-start | bytes 6291460
  19.1 12.4 %copy-start.12 = (s32[512]{0:T(512)S(1)}, s32[512]{0:T(512)}, u32[]{:S(2)}) copy-start(s32[512]{0:T(512)} %param.19) | copy-start | bytes 6148
  19.1 12.4 %copy-start.15 = (s32[2048]{0:T(1024)S(1)}, s32[2048]{0:T(1024)}, u32[]{:S(2)}) copy-start(s32[2048]{0:T(1024)} %param.22) | copy-start | bytes 24580
  19.1 13.9 %copy-start.3 = (f32[64,64]{1,0:T(8,128)S(1)}, f32[64,64]{1,0:T(8,128)}, u32[]{:S(2)}) copy-start(f32[64,64]{1,0:T(8,128)} %constant.35.clone.basis_ref) | copy-start | bytes 49156
  19.1 13.9 %copy-start.6 = (f32[8,512]{1,0:T(8,128)S(1)}, f32[8,512]{1,0:T(8,128)}, u32[]{:S(2)}) copy-start(f32[8,512]{1,0:T(8,128)} %geom_ref.7) | copy-start | bytes 49156
  19.1 13.9 %copy-start.7 = (f32[128,128]{1,0:T(8,128)S(1)}, f32[128,128]{1,0:T(8,128)}, u32[]{:S(2)}) copy-start(f32[128,128]{1,0:T(8,128)} %constant.36.clone.pair_ref) | copy-start | bytes 196612
  19.1 13.9 %copy-start.9 = (f32[8,64]{1,0:T(8,128)S(1)}, f32[8,64]{1,0:T(8,128)}, u32[]{:S(2)}) copy-start(f32[8,64]{1,0:T(8,128)} %constant.38.clone.scale_ref) | copy-start | bytes 6148
  19.1 13.9 %copy-start.10 = (f32[8,64]{1,0:T(8,128)S(1)}, f32[8,64]{1,0:T(8,128)}, u32[]{:S(2)}) copy-start(f32[8,64]{1,0:T(8,128)} %constant.37.clone.edge_ref) | copy-start | bytes 6148
  19.2 52.5 %copy-start.16 = (s32[96,4]{0,1:T(4,128)S(1)}, s32[96,4]{0,1:T(4,128)}, u32[]{:S(2)}) copy-start(s32[96,4]{0,1:T(4,128)} %param.23) | copy-start | bytes 4612
  19.2 53.7 %copy-start.2 = (f32[256,512]{1,0:T(8,128)S(1)}, f32[256,512]{1,0:T(8,128)}, u32[]{:S(2)}) copy-start(f32[256,512]{1,0:T(8,128)} %constant.40.clone.coupling_ref) | copy-start | bytes 1572868
  19.2 53.6 %copy-start.8 = (f32[64,64]{1,0:T(8,128)S(1)}, f32[64,64]{1,0:T(8,128)}, u32[]{:S(2)}) copy-start(f32[64,64]{1,0:T(8,128)} %constant.39.clone.series_ref) | copy-start | bytes 49156
  23.2 9.8 %all-to-all-start.1 = ((f32[8,1,160]{2,1,0:T(1,128)}), f32[8,1,160]{2,1,0:T(1,128)S(1)}, u32[]{:S(2)}, u32[]{:S(2)}) async-start(f32[8,1,160]{2,1,0:T(1,128)} %far_answers.1), calls=%async_computation.1 | async-start | bytes 16384 | tf_op jit(solution)/shard_map/all_to_all | solution.py:562
  35.0 7.3 %collective-permute-start.15 = (f32[160,128]{1,0:T(8,128)S(1)}, f32[160,128]{1,0:T(8,128)S(1)}, u32[]{:S(2)}, u32[]{:S(2)}) collective-permute-start(f32[160,128]{1,0:T(8,128)S(1)} %get-tuple-element.13.rest_0_), channel_id=1, source_target_pairs={{0,1},{1,0},{2,3},{3,2},{4,5},{5,4},{6,7},{7,6},{8,9},{9,8},{10,11... | collective-permute-start | bytes 245768 | tf_op jit(solution)/shard_map/ppermute | solution.py:543
  35.0 9.2 %collective-permute-start.7 = (f32[160,128]{1,0:T(8,128)S(1)}, f32[160,128]{1,0:T(8,128)S(1)}, u32[]{:S(2)}, u32[]{:S(2)}) collective-permute-start(f32[160,128]{1,0:T(8,128)S(1)} %get-tuple-element.13.rest_0_), channel_id=1, source_target_pairs={{0,2},{1,3},{2,0},{3,1},{4,6},{5,7},{6,4},{7,5},{8,10},{9,11},{10,... | collective-permute-start | bytes 245768 | tf_op jit(solution)/shard_map/ppermute | solution.py:543
  36.6 9.9 %collective-permute-start.6 = (f32[160,128]{1,0:T(8,128)S(1)}, f32[160,128]{1,0:T(8,128)S(1)}, u32[]{:S(2)}, u32[]{:S(2)}) collective-permute-start(f32[160,128]{1,0:T(8,128)S(1)} %get-tuple-element.13.rest_0_), channel_id=1, source_target_pairs={{0,28},{4,24},{8,20},{12,16},{16,12},{20,8},{24,4},{28,0},{1,29},{... | collective-permute-start | bytes 245768 | tf_op jit(solution)/shard_map/ppermute | solution.py:538
  41.1 9.6 %collective-permute-start.5 = (f32[160,128]{1,0:T(8,128)S(1)}, f32[160,128]{1,0:T(8,128)S(1)}, u32[]{:S(2)}, u32[]{:S(2)}) collective-permute-start(f32[160,128]{1,0:T(8,128)S(1)} %get-tuple-element.13.rest_0_), channel_id=1, source_target_pairs={{0,24},{4,28},{8,16},{12,20},{16,8},{20,12},{24,0},{28,4},{1,25},{... | collective-permute-start | bytes 245768 | tf_op jit(solution)/shard_map/ppermute | solution.py:538
  41.6 12.9 %collective-permute-start.4 = (f32[160,128]{1,0:T(8,128)S(1)}, f32[160,128]{1,0:T(8,128)S(1)}, u32[]{:S(2)}, u32[]{:S(2)}) collective-permute-start(f32[160,128]{1,0:T(8,128)S(1)} %get-tuple-element.13.rest_0_), channel_id=1, source_target_pairs={{0,20},{4,16},{8,28},{12,24},{16,4},{20,0},{24,12},{28,8},{1,21},{... | collective-permute-start | bytes 245768 | tf_op jit(solution)/shard_map/ppermute | solution.py:538
  42.2 13.4 %collective-permute-start.3 = (f32[160,128]{1,0:T(8,128)S(1)}, f32[160,128]{1,0:T(8,128)S(1)}, u32[]{:S(2)}, u32[]{:S(2)}) collective-permute-start(f32[160,128]{1,0:T(8,128)S(1)} %get-tuple-element.13.rest_0_), channel_id=1, source_target_pairs={{0,16},{4,20},{8,24},{12,28},{16,0},{20,4},{24,8},{28,12},{1,17},{... | collective-permute-start | bytes 245768 | tf_op jit(solution)/shard_map/ppermute | solution.py:538
  44.3 11.4 %collective-permute-start.2 = (f32[160,128]{1,0:T(8,128)S(1)}, f32[160,128]{1,0:T(8,128)S(1)}, u32[]{:S(2)}, u32[]{:S(2)}) collective-permute-start(f32[160,128]{1,0:T(8,128)S(1)} %get-tuple-element.13.rest_0_), channel_id=1, source_target_pairs={{0,12},{4,8},{8,4},{12,0},{16,28},{20,24},{24,20},{28,16},{1,13},{... | collective-permute-start | bytes 245768 | tf_op jit(solution)/shard_map/ppermute | solution.py:538
  46.5 9.7 %collective-permute-start.1 = (f32[160,128]{1,0:T(8,128)S(1)}, f32[160,128]{1,0:T(8,128)S(1)}, u32[]{:S(2)}, u32[]{:S(2)}) collective-permute-start(f32[160,128]{1,0:T(8,128)S(1)} %get-tuple-element.13.rest_0_), channel_id=1, source_target_pairs={{0,8},{4,12},{8,0},{12,4},{16,24},{20,28},{24,16},{28,20},{1,9},{5... | collective-permute-start | bytes 245768 | tf_op jit(solution)/shard_map/ppermute | solution.py:538
  50.7 5.7 %collective-permute-start = (f32[160,128]{1,0:T(8,128)S(1)}, f32[160,128]{1,0:T(8,128)S(1)}, u32[]{:S(2)}, u32[]{:S(2)}) collective-permute-start(f32[160,128]{1,0:T(8,128)S(1)} %get-tuple-element.13.rest_0_), channel_id=1, source_target_pairs={{0,4},{4,0},{8,12},{12,8},{16,20},{20,16},{24,28},{28,24},{1,5},{5... | collective-permute-start | bytes 245768 | tf_op jit(solution)/shard_map/ppermute | solution.py:538
  54.6 3.3 %collective-permute-start.23 = (f32[160,128]{1,0:T(8,128)S(1)}, f32[160,128]{1,0:T(8,128)S(1)}, u32[]{:S(2)}, u32[]{:S(2)}) collective-permute-start(f32[160,128]{1,0:T(8,128)S(1)} %collective-permute-done.7.rest_8_), channel_id=1, source_target_pairs={{0,1},{1,0},{2,3},{3,2},{4,5},{5,4},{6,7},{7,6},{8,9},{9,8},{10,11... | collective-permute-start | bytes 245768 | tf_op jit(solution)/shard_map/ppermute | solution.py:543
  55.6 2.3 %collective-permute-start.22 = (f32[160,128]{1,0:T(8,128)S(1)}, f32[160,128]{1,0:T(8,128)S(1)}, u32[]{:S(2)}, u32[]{:S(2)}) collective-permute-start(f32[160,128]{1,0:T(8,128)S(1)} %collective-permute-done.6.rest_7_), channel_id=1, source_target_pairs={{0,1},{1,0},{2,3},{3,2},{4,5},{5,4},{6,7},{7,6},{8,9},{9,8},{10,11... | collective-permute-start | bytes 245768 | tf_op jit(solution)/shard_map/ppermute | solution.py:543
  55.6 5.2 %collective-permute-start.14 = (f32[160,128]{1,0:T(8,128)S(1)}, f32[160,128]{1,0:T(8,128)S(1)}, u32[]{:S(2)}, u32[]{:S(2)}) collective-permute-start(f32[160,128]{1,0:T(8,128)S(1)} %collective-permute-done.6.rest_7_), channel_id=1, source_target_pairs={{0,2},{1,3},{2,0},{3,1},{4,6},{5,7},{6,4},{7,5},{8,10},{9,11},{10,... | collective-permute-start | bytes 245768 | tf_op jit(solution)/shard_map/ppermute | solution.py:543
  56.2 4.7 %collective-permute-start.21 = (f32[160,128]{1,0:T(8,128)S(1)}, f32[160,128]{1,0:T(8,128)S(1)}, u32[]{:S(2)}, u32[]{:S(2)}) collective-permute-start(f32[160,128]{1,0:T(8,128)S(1)} %collective-permute-done.5.rest_6_), channel_id=1, source_target_pairs={{0,1},{1,0},{2,3},{3,2},{4,5},{5,4},{6,7},{7,6},{8,9},{9,8},{10,11... | collective-permute-start | bytes 245768 | tf_op jit(solution)/shard_map/ppermute | solution.py:543
  56.4 6.2 %collective-permute-start.13 = (f32[160,128]{1,0:T(8,128)S(1)}, f32[160,128]{1,0:T(8,128)S(1)}, u32[]{:S(2)}, u32[]{:S(2)}) collective-permute-start(f32[160,128]{1,0:T(8,128)S(1)} %collective-permute-done.5.rest_6_), channel_id=1, source_target_pairs={{0,2},{1,3},{2,0},{3,1},{4,6},{5,7},{6,4},{7,5},{8,10},{9,11},{10,... | collective-permute-start | bytes 245768 | tf_op jit(solution)/shard_map/ppermute | solution.py:543
  57.9 4.7 %collective-permute-start.20 = (f32[160,128]{1,0:T(8,128)S(1)}, f32[160,128]{1,0:T(8,128)S(1)}, u32[]{:S(2)}, u32[]{:S(2)}) collective-permute-start(f32[160,128]{1,0:T(8,128)S(1)} %collective-permute-done.4.rest_5_), channel_id=1, source_target_pairs={{0,1},{1,0},{2,3},{3,2},{4,5},{5,4},{6,7},{7,6},{8,9},{9,8},{10,11... | collective-permute-start | bytes 245768 | tf_op jit(solution)/shard_map/ppermute | solution.py:543
  57.9 6.1 %collective-permute-start.12 = (f32[160,128]{1,0:T(8,128)S(1)}, f32[160,128]{1,0:T(8,128)S(1)}, u32[]{:S(2)}, u32[]{:S(2)}) collective-permute-start(f32[160,128]{1,0:T(8,128)S(1)} %collective-permute-done.4.rest_5_), channel_id=1, source_target_pairs={{0,2},{1,3},{2,0},{3,1},{4,6},{5,7},{6,4},{7,5},{8,10},{9,11},{10,... | collective-permute-start | bytes 245768 | tf_op jit(solution)/shard_map/ppermute | solution.py:543
  60.9 3.1 %collective-permute-start.19 = (f32[160,128]{1,0:T(8,128)S(1)}, f32[160,128]{1,0:T(8,128)S(1)}, u32[]{:S(2)}, u32[]{:S(2)}) collective-permute-start(f32[160,128]{1,0:T(8,128)S(1)} %collective-permute-done.3.rest_4_), channel_id=1, source_target_pairs={{0,1},{1,0},{2,3},{3,2},{4,5},{5,4},{6,7},{7,6},{8,9},{9,8},{10,11... | collective-permute-start | bytes 245768 | tf_op jit(solution)/shard_map/ppermute | solution.py:543
  60.9 4.9 %collective-permute-start.11 = (f32[160,128]{1,0:T(8,128)S(1)}, f32[160,128]{1,0:T(8,128)S(1)}, u32[]{:S(2)}, u32[]{:S(2)}) collective-permute-start(f32[160,128]{1,0:T(8,128)S(1)} %collective-permute-done.3.rest_4_), channel_id=1, source_target_pairs={{0,2},{1,3},{2,0},{3,1},{4,6},{5,7},{6,4},{7,5},{8,10},{9,11},{10,... | collective-permute-start | bytes 245768 | tf_op jit(solution)/shard_map/ppermute | solution.py:543
  62.6 3.1 %collective-permute-start.18 = (f32[160,128]{1,0:T(8,128)S(1)}, f32[160,128]{1,0:T(8,128)S(1)}, u32[]{:S(2)}, u32[]{:S(2)}) collective-permute-start(f32[160,128]{1,0:T(8,128)S(1)} %collective-permute-done.2.rest_3_), channel_id=1, source_target_pairs={{0,1},{1,0},{2,3},{3,2},{4,5},{5,4},{6,7},{7,6},{8,9},{9,8},{10,11... | collective-permute-start | bytes 245768 | tf_op jit(solution)/shard_map/ppermute | solution.py:543
  62.6 5.2 %collective-permute-start.10 = (f32[160,128]{1,0:T(8,128)S(1)}, f32[160,128]{1,0:T(8,128)S(1)}, u32[]{:S(2)}, u32[]{:S(2)}) collective-permute-start(f32[160,128]{1,0:T(8,128)S(1)} %collective-permute-done.2.rest_3_), channel_id=1, source_target_pairs={{0,2},{1,3},{2,0},{3,1},{4,6},{5,7},{6,4},{7,5},{8,10},{9,11},{10,... | collective-permute-start | bytes 245768 | tf_op jit(solution)/shard_map/ppermute | solution.py:543
  64.0 3.9 %collective-permute-start.17 = (f32[160,128]{1,0:T(8,128)S(1)}, f32[160,128]{1,0:T(8,128)S(1)}, u32[]{:S(2)}, u32[]{:S(2)}) collective-permute-start(f32[160,128]{1,0:T(8,128)S(1)} %collective-permute-done.1.rest_2_), channel_id=1, source_target_pairs={{0,1},{1,0},{2,3},{3,2},{4,5},{5,4},{6,7},{7,6},{8,9},{9,8},{10,11... | collective-permute-start | bytes 245768 | tf_op jit(solution)/shard_map/ppermute | solution.py:543
  64.0 5.6 %collective-permute-start.9 = (f32[160,128]{1,0:T(8,128)S(1)}, f32[160,128]{1,0:T(8,128)S(1)}, u32[]{:S(2)}, u32[]{:S(2)}) collective-permute-start(f32[160,128]{1,0:T(8,128)S(1)} %collective-permute-done.1.rest_2_), channel_id=1, source_target_pairs={{0,2},{1,3},{2,0},{3,1},{4,6},{5,7},{6,4},{7,5},{8,10},{9,11},{10,... | collective-permute-start | bytes 245768 | tf_op jit(solution)/shard_map/ppermute | solution.py:543
  65.8 3.9 %collective-permute-start.16 = (f32[160,128]{1,0:T(8,128)S(1)}, f32[160,128]{1,0:T(8,128)S(1)}, u32[]{:S(2)}, u32[]{:S(2)}) collective-permute-start(f32[160,128]{1,0:T(8,128)S(1)} %collective-permute-done.rest_1_), channel_id=1, source_target_pairs={{0,1},{1,0},{2,3},{3,2},{4,5},{5,4},{6,7},{7,6},{8,9},{9,8},{10,11... | collective-permute-start | bytes 245768 | tf_op jit(solution)/shard_map/ppermute | solution.py:543
  65.8 5.3 %collective-permute-start.8 = (f32[160,128]{1,0:T(8,128)S(1)}, f32[160,128]{1,0:T(8,128)S(1)}, u32[]{:S(2)}, u32[]{:S(2)}) collective-permute-start(f32[160,128]{1,0:T(8,128)S(1)} %collective-permute-done.rest_1_), channel_id=1, source_target_pairs={{0,2},{1,3},{2,0},{3,1},{4,6},{5,7},{6,4},{7,5},{8,10},{9,11},{10,... | collective-permute-start | bytes 245768 | tf_op jit(solution)/shard_map/ppermute | solution.py:543
  67.9 3.1 %collective-permute-start.30 = (f32[160,128]{1,0:T(8,128)S(1)}, f32[160,128]{1,0:T(8,128)S(1)}, u32[]{:S(2)}, u32[]{:S(2)}) collective-permute-start(f32[160,128]{1,0:T(8,128)S(1)} %collective-permute-done.14.rest_15_), channel_id=1, source_target_pairs={{0,1},{1,0},{2,3},{3,2},{4,5},{5,4},{6,7},{7,6},{8,9},{9,8},{10,11... | collective-permute-start | bytes 245768 | tf_op jit(solution)/shard_map/ppermute | solution.py:543
  67.9 3.7 %collective-permute-start.29 = (f32[160,128]{1,0:T(8,128)S(1)}, f32[160,128]{1,0:T(8,128)S(1)}, u32[]{:S(2)}, u32[]{:S(2)}) collective-permute-start(f32[160,128]{1,0:T(8,128)S(1)} %collective-permute-done.13.rest_14_), channel_id=1, source_target_pairs={{0,1},{1,0},{2,3},{3,2},{4,5},{5,4},{6,7},{7,6},{8,9},{9,8},{10,11... | collective-permute-start | bytes 245768 | tf_op jit(solution)/shard_map/ppermute | solution.py:543
  69.6 2.2 %collective-permute-start.28 = (f32[160,128]{1,0:T(8,128)S(1)}, f32[160,128]{1,0:T(8,128)S(1)}, u32[]{:S(2)}, u32[]{:S(2)}) collective-permute-start(f32[160,128]{1,0:T(8,128)S(1)} %collective-permute-done.12.rest_13_), channel_id=1, source_target_pairs={{0,1},{1,0},{2,3},{3,2},{4,5},{5,4},{6,7},{7,6},{8,9},{9,8},{10,11... | collective-permute-start | bytes 245768 | tf_op jit(solution)/shard_map/ppermute | solution.py:543
  69.7 2.2 %collective-permute-start.27 = (f32[160,128]{1,0:T(8,128)S(1)}, f32[160,128]{1,0:T(8,128)S(1)}, u32[]{:S(2)}, u32[]{:S(2)}) collective-permute-start(f32[160,128]{1,0:T(8,128)S(1)} %collective-permute-done.11.rest_12_), channel_id=1, source_target_pairs={{0,1},{1,0},{2,3},{3,2},{4,5},{5,4},{6,7},{7,6},{8,9},{9,8},{10,11... | collective-permute-start | bytes 245768 | tf_op jit(solution)/shard_map/ppermute | solution.py:543
  71.0 1.3 %collective-permute-start.26 = (f32[160,128]{1,0:T(8,128)S(1)}, f32[160,128]{1,0:T(8,128)S(1)}, u32[]{:S(2)}, u32[]{:S(2)}) collective-permute-start(f32[160,128]{1,0:T(8,128)S(1)} %collective-permute-done.10.rest_11_), channel_id=1, source_target_pairs={{0,1},{1,0},{2,3},{3,2},{4,5},{5,4},{6,7},{7,6},{8,9},{9,8},{10,11... | collective-permute-start | bytes 245768 | tf_op jit(solution)/shard_map/ppermute | solution.py:543
  71.0 1.4 %collective-permute-start.25 = (f32[160,128]{1,0:T(8,128)S(1)}, f32[160,128]{1,0:T(8,128)S(1)}, u32[]{:S(2)}, u32[]{:S(2)}) collective-permute-start(f32[160,128]{1,0:T(8,128)S(1)} %collective-permute-done.9.rest_10_), channel_id=1, source_target_pairs={{0,1},{1,0},{2,3},{3,2},{4,5},{5,4},{6,7},{7,6},{8,9},{9,8},{10,11... | collective-permute-start | bytes 245768 | tf_op jit(solution)/shard_map/ppermute | solution.py:543
  71.6 1.3 %collective-permute-start.24 = (f32[160,128]{1,0:T(8,128)S(1)}, f32[160,128]{1,0:T(8,128)S(1)}, u32[]{:S(2)}, u32[]{:S(2)}) collective-permute-start(f32[160,128]{1,0:T(8,128)S(1)} %collective-permute-done.8.rest_9_), channel_id=1, source_target_pairs={{0,1},{1,0},{2,3},{3,2},{4,5},{5,4},{6,7},{7,6},{8,9},{9,8},{10,11... | collective-permute-start | bytes 245768 | tf_op jit(solution)/shard_map/ppermute | solution.py:543
where the time goes:
time: 91 us; the launch traced here: 90.6 us
  Pallas kernels  30.7 us (34%)
  starting transfers between devices  27.6 us (30%)
  blocking collectives  14 us (15%)
  waiting for transfers between devices  13.5 us (15%)
  local copies, waits for them, and re-layouts  3.98 us (4%)
    pallas_call x1, Pallas kernels, smooth(): pl.pallas_call(functools.partial(smooth_kernel, sources, per_owner), out_...  17.8 us
    ppermute x7, starting transfers between devices, spread_payload(): lax.ppermute(payload, 'vol', [(i, i ^ k) for i in range(vol_count)])  15.7 us
    all_to_all x1, blocking collectives, per_device(): lax.all_to_all(request, 'vol', split_axis=0, concat_axis=0, tiled=True)  14 us
    ppermute x24, waiting for transfers between devices, spread_payload(): arrays.append(lax.ppermute(array, 'dsg', pairs))  10.1 us
    ppermute x24, starting transfers between devices, spread_payload(): arrays.append(lax.ppermute(array, 'dsg', pairs))  8.47 us
    pallas_call x1, Pallas kernels, near_densities(): pl.pallas_call(near_kernel, out_shape=jax.ShapeDtypeStruct((1, count), F3...  4.89 us
    pallas_call x1, Pallas kernels, far_answers(): pl.pallas_call(far_kernel, out_shape=jax.ShapeDtypeStruct((owners, 1, cap...  4.03 us
    unnamed x35, local copies, waits for them, and re-layouts  3.87 us
  transfers between devices with their start and end apart: 32, of which 13 were waited for; matrix products, arithmetic and copies ran while one was open for 0% of the time, Pallas kernels for 7%

commit v1 on v0

--- a/solution.py
+++ b/solution.py
@@ -22,6 +22,7 @@
 VMEM = pl.BlockSpec(memory_space=pltpu.VMEM)
 SMEM = pl.BlockSpec(memory_space=pltpu.SMEM)
 ANY = pl.BlockSpec(memory_space=pl.ANY)
+WHOLE = pl.BlockSpec()
 
 
 def params(megabytes):
@@ -63,7 +64,7 @@
         basis_pair=np.float32(np.kron(np.eye(2), basis)),
         edge_rows=np.float32(edge_rows),
         scale_rows=np.float32(scale_rows),
-        series=np.float32(series),
+        series=np.float32(np.concatenate([series, series], 1)),
         coupling=np.float32(np.concatenate([coupling(0), coupling(1)], 1)),
     )
 
@@ -121,7 +122,7 @@
             jax.ShapeDtypeStruct((owners, 8, capacity), F32),
             jax.ShapeDtypeStruct((1, count), jnp.int32),
         ),
-        in_specs=[VMEM] * 3,
+        in_specs=[WHOLE] * 3,
         out_specs=(VMEM, VMEM),
         compiler_params=params(16),
         name="pack_requests",
@@ -209,7 +210,7 @@
     return pl.pallas_call(
         near_kernel,
         out_shape=jax.ShapeDtypeStruct((1, count), F32),
-        in_specs=[SMEM, VMEM, VMEM],
+        in_specs=[SMEM, VMEM, WHOLE],
         out_specs=VMEM,
         scratch_shapes=[pltpu.VMEM((count, LANES), F32)],
         compiler_params=params(24),
@@ -218,7 +219,7 @@
     )(near_cell, fields, near_geom)
 
 
-def far_kernel(request_ref, fields_ref, out_ref, query_ref, cell_v, cell_s, rows_ref, dens_ref, sem):
+def far_kernel(request_ref, fields_ref, near_ref, out_ref, query_ref, cell_v, cell_s, rows_ref, dens_ref, sem):
     owners, _, capacity = request_ref.shape
     count = owners * capacity
     for o in range(owners):
@@ -233,13 +234,13 @@
         out_ref[o] = dens_ref[:, o * capacity : (o + 1) * capacity]
 
 
-def far_answers(requests, fields):
+def far_answers(requests, fields, near_dens):
     owners, _, capacity = requests.shape
     count = owners * capacity
     return pl.pallas_call(
         far_kernel,
         out_shape=jax.ShapeDtypeStruct((owners, 1, capacity), F32),
-        in_specs=[VMEM, VMEM],
+        in_specs=[VMEM, VMEM, ANY],
         out_specs=VMEM,
         scratch_shapes=[
             pltpu.VMEM((8, count), F32),
@@ -251,7 +252,7 @@
         ],
         compiler_params=params(24),
         name="far_answers",
-    )(requests, fields)
+    )(requests, fields, near_dens)
 
 
 def spline_columns(param):
@@ -307,7 +308,7 @@
             jax.ShapeDtypeStruct((GROUP * CTRL, CTRL), F32),
             jax.ShapeDtypeStruct((8, LANES), F32),
         ),
-        in_specs=[VMEM] * 4,
+        in_specs=[VMEM] + [WHOLE] * 3,
         out_specs=(VMEM, VMEM),
         compiler_params=params(24),
         cost_estimate=pl.CostEstimate(flops=80_000_000, bytes_accessed=1_000_000, transcendentals=0),
@@ -344,7 +345,8 @@
     both = jnp.concatenate(
         [jnp.concatenate([edge, blank], 1), jnp.concatenate([blank, edge], 1)], 0
     )
-    row = iota((8, LANES), 0)
+    out_ref[GRID_ROWS + 6 * GROUP : GRID_ROWS + 7 * GROUP, :] = slot_ref[0:GROUP, :]
+    out_ref[GRID_ROWS + 7 * GROUP : GRID_ROWS + 8 * GROUP, :] = jnp.broadcast_to(names, (GROUP, LANES))
     for pair in range(GROUP // 2):
         a, b = 2 * pair, 2 * pair + 1
         both_grids = jnp.concatenate(
@@ -362,8 +364,9 @@
                 ],
                 1,
             )
-            block = jnp.where(row == 6, slot_ref[slot : slot + 1, :], jnp.where(row == 7, names, block))
-            out_ref[GRID_ROWS + slot * 8 : GRID_ROWS + slot * 8 + 8, :] = block
+            for r in range(6):
+                at = GRID_ROWS + GROUP * r + slot
+                out_ref[at : at + 1, :] = block[r : r + 1]
 
 
 def make_payload(reply, place, far_geom, far_patch, slots, near_grid, const):
@@ -375,7 +378,7 @@
             jax.ShapeDtypeStruct((1, count), F32),
             jax.ShapeDtypeStruct((PAYLOAD_ROWS, LANES), F32),
         ),
-        in_specs=[VMEM] * 10,
+        in_specs=[VMEM] * 2 + [WHOLE] * 2 + [VMEM] * 2 + [WHOLE] * 4,
         out_specs=(VMEM, VMEM),
         scratch_shapes=[pltpu.VMEM((1, owners * capacity), F32)],
         compiler_params=params(24),
@@ -386,169 +389,263 @@
     )
 
 
-def smooth_kernel(
-    sources, per_owner, where_ref, adj_ref, coupling_ref, basis_ref, series_ref, edge_ref, scale_ref, *rest
-):
-    n_in = len(sources)
-    payload = rest[:n_in]
-    out_ref, buf, name_v, name_s, own, halo_rows, sem, name_sem = rest[n_in:]
-    devices = buf.shape[0] // PAYLOAD_ROWS
-    copies = []
-    for a, (source, ref) in enumerate(zip(sources, payload)):
-        rows = ref.shape[0]
-        copies.append(
-            pltpu.make_async_copy(
-                ref, buf.at[pl.ds(pl.multiple_of(where_ref[1 + a] * PAYLOAD_ROWS, 8), rows)], sem.at[a]
-            )
-        )
-        copies[-1].start()
-    own[...] = jnp.zeros(own.shape, F32)
-    for copy in copies:
-        copy.wait()
-    name_v[...] = buf[pl.ds(PAYLOAD_ROWS - 1, devices, stride=PAYLOAD_ROWS), :].astype(jnp.int32)
+def two(x):
+    return jnp.concatenate(halves(x), 1)
+
+
+def fold(x):
+    half = x.shape[1] // 2
+    return x[:, :half] + x[:, half:]
+
+
+def absorb(first_own, y_at, per_owner, items, sums, groups, name_v, name_s, edges, name_sem):
+    patches = groups.shape[2]
+    total = sum(parts for _, parts, _, _ in items)
+    at = 0
+    for ref, parts, _, _ in items:
+        for p in range(parts):
+            last = (p + 1) * PAYLOAD_ROWS - 1
+            name_v[at : at + 1, :] = ref[last : last + 1, :].astype(jnp.int32)
+            at += 1
     names = pltpu.make_async_copy(name_v, name_s, name_sem)
     names.start()
 
+    for group in sorted({2 * dy + dx for _, _, dy, dx in items}):
+        at = 0
+        for ref, parts, dy, dx in items:
+            if 2 * dy + dx == group:
+                for p in range(parts):
+                    for r in range(7):
+                        row = p * PAYLOAD_ROWS + GRID_ROWS + GROUP * r
+                        edges[r, at : at + GROUP, :] = ref[row : row + GROUP, :]
+                    at += GROUP
+        lane = iota((at, LANES), 1)
+        place = jnp.where(lane == edges[6, :at, :].astype(jnp.int32), 1.0, 0.0).T[:patches].astype(BF16)
+        for k in range(3):
+            rows = jnp.concatenate([edges[2 * k, :at, :], edges[2 * k + 1, :at, :]], 1)
+            groups[(group // 2 ^ y_at) * 2 + group % 2, k] = fold(nn(place, two(rows)))
+
+    names.wait()
+    low_half = iota((CTRL, LANES), 1) < CTRL
+    at = 0
+    for ref, parts, dy, _ in items:
+
+        def add_payload(p, carry, ref=ref, at=at, dy=dy):
+            for s in range(GROUP):
+                patch = name_s[at + p, s] - first_own
+
+                @pl.when((patch >= 0) & (patch < per_owner))
+                def _():
+                    row = pl.multiple_of(p * PAYLOAD_ROWS + (s // 2) * CTRL, 8)
+                    block = ref[pl.ds(row, CTRL), :]
+                    block = jnp.where(patch % 2 == s % 2, block, pltpu.roll(block, CTRL, 1))
+                    block = jnp.where(low_half == (patch % 2 == 0), block, 0.0)
+                    own = pl.multiple_of(patch // 2 * CTRL, CTRL)
+                    sums[dy ^ y_at, pl.ds(own, CTRL), :] = sums[dy ^ y_at, pl.ds(own, CTRL), :] + block
+
+            return carry
+
+        lax.fori_loop(0, parts, add_payload, 0)
+        at += parts
+
+
+def early_kernel(per_owner, items, where_ref, *rest):
+    refs = rest[: len(items)]
+    sums, groups, name_v, name_s, edges, name_sem = rest[len(items) :]
+    sums[...] = jnp.zeros(sums.shape, F32)
+    groups[...] = jnp.zeros(groups.shape, F32)
+    items = [(ref, *item) for ref, item in zip(refs, items)]
+    absorb(where_ref[0] * per_owner, where_ref[1], per_owner, items, sums, groups, name_v, name_s, edges, name_sem)
+
+
+def absorb_scratch(items):
+    total = sum(item[0] for item in items)
+    return [
+        pltpu.VMEM((total, LANES), jnp.int32),
+        pltpu.SMEM((total, LANES), jnp.int32),
+        pltpu.VMEM((7, total * GROUP, LANES), F32),
+        pltpu.SemaphoreType.DMA,
+    ]
+
+
+def sum_shapes(per_owner, patches):
+    return (
+        jax.ShapeDtypeStruct((2, per_owner // 2 * CTRL, LANES), F32),
+        jax.ShapeDtypeStruct((4, 3, patches, 4 * CTRL), F32),
+    )
+
+
+def early_sums(payloads, items, where, per_owner, patches):
+    return pl.pallas_call(
+        functools.partial(early_kernel, per_owner, items),
+        out_shape=sum_shapes(per_owner, patches),
+        in_specs=[SMEM] + [VMEM] * len(payloads),
+        out_specs=(VMEM, VMEM),
+        scratch_shapes=absorb_scratch(items),
+        compiler_params=params(16),
+        cost_estimate=pl.CostEstimate(flops=20_000_000, bytes_accessed=3_000_000, transcendentals=0),
+        name="early_sums",
+    )(where, *payloads)
+
+
+def smooth_kernel(
+    items, per_owner, has_early, where_ref, adj_ref, coupling_ref, basis_ref, pair_ref, series_ref, edge_ref,
+    scale_ref, *rest
+):
+    refs, rest = rest[: len(items)], rest[len(items) :]
+    if has_early:
+        early_sum, early_group, *rest = rest
+    out_ref, sums, groups, name_v, name_s, edges, name_sem, halo_all, halo_rows = rest
+    if has_early:
+        sums[...] = early_sum[...]
+        groups[...] = early_group[...]
+    else:
+        sums[...] = jnp.zeros(sums.shape, F32)
+        groups[...] = jnp.zeros(groups.shape, F32)
     patches = adj_ref.shape[0]
-    lane = iota((devices, LANES), 1)
-
-    def edge_rows(r):
-        return [
-            buf[pl.ds(GRID_ROWS + 8 * s + r, devices, stride=PAYLOAD_ROWS), :] for s in range(GROUP)
+    first_own = pl.multiple_of(where_ref[0] * per_owner, 8)
+    items = [(ref, *item) for ref, item in zip(refs, items)]
+    absorb(first_own, where_ref[1], per_owner, items, sums, groups, name_v, name_s, edges, name_sem)
+    base = [(groups[0, k] + groups[1, k]) + (groups[2, k] + groups[3, k]) for k in range(3)]
+
+    column = iota((patches, patches), 1)
+    wide = 4 * CTRL
+
+    def facing(adjacency):
+        hits = [
+            jnp.where(adjacency[:, s : s + 1] == column[: adjacency.shape[0]], 1.0, 0.0).astype(BF16)
+            for s in range(4)
         ]
-
-    places = [jnp.where(lane == n.astype(jnp.int32), 1.0, 0.0) for n in edge_rows(6)]
-    place = jnp.concatenate(places, 0).astype(BF16)
-    sums = []
-    for r in range(6):
-        parts = [p.astype(BF16) for p in split3(jnp.concatenate(edge_rows(r), 0))]
-        sums.append(tn(place, parts[0]) + (tn(place, parts[1]) + tn(place, parts[2])))
-    base = [jnp.concatenate([sums[2 * k], sums[2 * k + 1]], 1)[:patches] for k in range(3)]
-
-    adjacency = adj_ref[...]
-    column = iota((patches, patches), 1)
-    facing = [
-        jnp.where(adjacency[:, s : s + 1] == column, 1.0, 0.0).astype(BF16) for s in range(4)
-    ]
-    low_lane = iota((patches, LANES), 1) < CTRL
-
-    def halo(edges):
-        parts = [p.astype(BF16) for p in split3(edges)]
-
-        def look(side, at):
-            pieces = [nn(facing[side], p[:, at : at + LANES]) for p in parts]
-            return pieces[0] + (pieces[1] + pieces[2])
-
-        first = jnp.where(low_lane, look(0, LANES), look(2, LANES))
-        second = jnp.where(low_lane, look(1, 0), look(3, 0))
-        return jnp.concatenate([first, second], 1)
-
-    wide = 4 * CTRL
-    halo0 = halo(base[0])
-    effect0 = nn(halo0, coupling_ref[...], precision=EXACT)
+        return jnp.concatenate([hits[0], hits[2]], 0), jnp.concatenate([hits[1], hits[3]], 0)
+
+    def halo(facing, edges):
+        count = facing[0].shape[0] // 2
+        low_lane = iota((count, LANES), 1) < CTRL
+        first = fold(nn(facing[0], two(edges[:, LANES:])))
+        second = fold(nn(facing[1], two(edges[:, :LANES])))
+        return jnp.concatenate(
+            [jnp.where(low_lane, x[:count], x[count:]) for x in (first, second)], 1
+        )
+
+    def product(x, y):
+        x_high, x_low = halves(x)
+        y_high, y_low = halves(y)
+        return nn(x_high, y_high) + (nn(x_low, y_high) + nn(x_high, y_low))
+
+    every = facing(adj_ref[...])
+    halo0 = halo(every, base[0])
+    effect0 = product(halo0, coupling_ref[...])
     edges1 = base[0] + base[1] + effect0[:, :wide]
-    halo1 = halo(edges1)
-    effect1 = nn(halo1, coupling_ref[:, :wide], precision=EXACT)
+    halo1 = halo(every, edges1)
+    effect1 = product(halo1, coupling_ref[:, :wide])
     edges2 = base[0] + base[1] + base[2] + effect0[:, wide:] + effect1
-    halo2 = halo(edges2)
-
-    first_own = where_ref[0] * per_owner
-    mine = jnp.where(
-        iota((per_owner, patches), 1) == iota((per_owner, patches), 0) + first_own, 1.0, 0.0
-    ).astype(BF16)
+    halo2 = halo(facing(adj_ref[pl.ds(first_own, per_owner), :]), edges2)
+    halo_all[0] = halo1
+    halo_all[1] = halo0
     scale = scale_ref[...]
-    for k, h in enumerate((halo2, halo1, halo0)):
-        picked = [nn(mine, p.astype(BF16)) for p in split3(h)]
-        picked = picked[0] + (picked[1] + picked[2])
+    for k in range(3):
+        mine = halo2 if k == 0 else halo_all[k - 1, pl.ds(first_own, per_owner), :]
         factor = SMOOTHING * jnp.concatenate([scale[2 * k : 2 * k + 1]] * 2, 1)
         for side in range(2):
             halo_rows[pl.ds(2 * k + side, per_owner, stride=8), :] = (
-                picked[:, side * LANES : (side + 1) * LANES] * factor
+                mine[:, side * LANES : (side + 1) * LANES] * factor
             )
     zero = jnp.zeros((per_owner, LANES), F32)
     for r in (6, 7):
         halo_rows[pl.ds(r, per_owner, stride=8), :] = zero
 
-    names.wait()
-
-    def add_slot(device, carry):
-        for s in range(GROUP):
-            patch = name_s[device, s] - first_own
-
-            @pl.when((patch >= 0) & (patch < per_owner))
-            def _():
-                at = pl.multiple_of(device * PAYLOAD_ROWS + (s // 2) * CTRL, 8)
-                block = buf[pl.ds(at, CTRL), :]
-                if s % 2:
-                    block = pltpu.roll(block, CTRL, 1)
-                own_at = pl.multiple_of(patch * CTRL, CTRL)
-                own[pl.ds(own_at, CTRL), :] = own[pl.ds(own_at, CTRL), :] + block
-
-        return carry
-
-    lax.fori_loop(0, devices, add_slot, 0)
-
-    basis = basis_ref[...]
-    series = series_ref[...]
+    pairs = per_owner // 2
     edge = edge_ref[...]
-
-    def finish(patch, carry):
-        at = pl.multiple_of(patch * CTRL, CTRL)
-        rows = halo_rows[pl.ds(pl.multiple_of(patch * 8, 8), 8), :]
-        left = jnp.concatenate([edge, rows[:, CTRL:]], 0)
-        right = jnp.concatenate([rows[:, :CTRL], edge], 0)
-        spectral = own[pl.ds(at, CTRL), :][:, :CTRL] * series + tn(left, right, precision=EXACT)
-        out_ref[patch] = nn(nn(basis, spectral, precision=EXACT), basis, precision=EXACT)
-        return carry
-
-    lax.fori_loop(0, per_owner, finish, 0, unroll=4)
-
-
-def smooth(payloads, sources, where, adjacency, owners, devices, const):
-    per_owner = adjacency.shape[0] // owners
+    blank = jnp.zeros((8, CTRL), F32)
+    both = jnp.concatenate(
+        [jnp.concatenate([edge, blank], 1), jnp.concatenate([blank, edge], 1)], 0
+    )
+    low8 = iota((8, LANES), 1) < CTRL
+    along_rows, along_cols = [], []
+    for pair in range(pairs):
+        a = halo_rows[16 * pair : 16 * pair + 8, :]
+        b = halo_rows[16 * pair + 8 : 16 * pair + 16, :]
+        along_rows.append(jnp.where(low8, a, pltpu.roll(b, CTRL, 1)))
+        along_cols.append(jnp.concatenate([a[:, CTRL:], b[:, CTRL:]], 0))
+    from_rows = tn_product(edge, jnp.concatenate(along_rows, 1))
+    basis_both = pair_ref[...]
+    turned = []
+    for pair in range(pairs):
+        rows = slice(pair * CTRL, (pair + 1) * CTRL)
+        spectral = (sums[0, rows, :] + sums[1, rows, :]) * series_ref[...]
+        spectral = spectral + from_rows[:, pair * LANES : (pair + 1) * LANES]
+        turned.append(spectral + tn_product(along_cols[pair], both))
+    turned = product(jnp.concatenate(turned, 0), basis_both)
+    flat = jnp.concatenate([turned[pair * CTRL : (pair + 1) * CTRL] for pair in range(pairs)], 1)
+    done = product(basis_ref[...], flat)
+    for pair in range(pairs):
+        out_ref[2 * pair] = done[:, pair * LANES : pair * LANES + CTRL]
+        out_ref[2 * pair + 1] = done[:, pair * LANES + CTRL : (pair + 1) * LANES]
+
+
+def tn_product(x, y):
+    x_high, x_low = halves(x)
+    y_high, y_low = halves(y)
+    return tn(x_high, y_high) + (tn(x_low, y_high) + tn(x_high, y_low))
+
+
+def smooth(payloads, items, early, where, adjacency, per_owner, const):
+    patches = adjacency.shape[0]
     return pl.pallas_call(
-        functools.partial(smooth_kernel, sources, per_owner),
+        functools.partial(smooth_kernel, items, per_owner, bool(early)),
         out_shape=jax.ShapeDtypeStruct((per_owner, CTRL, CTRL), F32),
-        in_specs=[SMEM] + [VMEM] * 6 + [ANY] * len(payloads),
+        in_specs=[SMEM] + [WHOLE] * 7 + [VMEM] * (len(payloads) + len(early)),
         out_specs=VMEM,
         scratch_shapes=[
-            pltpu.VMEM((devices * PAYLOAD_ROWS, LANES), F32),
-            pltpu.VMEM((devices, LANES), jnp.int32),
-            pltpu.SMEM((devices, LANES), jnp.int32),
-            pltpu.VMEM((per_owner * CTRL, LANES), F32),
+            *[pltpu.VMEM(shape.shape, F32) for shape in sum_shapes(per_owner, patches)],
+            *absorb_scratch(items),
+            pltpu.VMEM((2, patches, 4 * CTRL), F32),
             pltpu.VMEM((per_owner * 8, LANES), F32),
-            pltpu.SemaphoreType.DMA((len(payloads),)),
-            pltpu.SemaphoreType.DMA,
         ],
-        compiler_params=params(48),
+        compiler_params=params(32),
         name="smooth",
     )(
-        where, adjacency, const["coupling"], const["basis"], const["series"], const["edge_rows"],
-        const["scale_rows"], *payloads,
-    )
-
-
-def spread_payload(payload, vol_count, dsg_count):
-    if vol_count > 8 or dsg_count != 4:
+        where, adjacency, const["coupling"], const["basis"], const["basis_pair"], const["series"],
+        const["edge_rows"], const["scale_rows"], *payloads, *early,
+    )
+
+
+def gather_and_smooth(payload, adjacency, vol_count, dsg_count, const):
+    patches = adjacency.shape[0]
+    per_owner = patches // dsg_count
+    y_at = lax.axis_index("vol") % 2 if (vol_count, dsg_count) == (8, 4) else 0
+    where = jnp.stack([lax.axis_index("dsg"), y_at]).astype(jnp.int32)
+    if vol_count != 8 or dsg_count != 4:
         whole = lax.all_gather(payload, ("vol", "dsg"), axis=0, tiled=True)
-        return [None], [whole]
-    sources, arrays = [(0, 0)], [payload]
-    for k in range(1, vol_count):
-        sources.append((k, 0))
-        arrays.append(lax.ppermute(payload, "vol", [(i, i ^ k) for i in range(vol_count)]))
-    for offset in (2, 1):
-        pairs = [(i, i ^ offset) for i in range(dsg_count)]
-        for (a, b), array in list(zip(sources, arrays)):
-            sources.append((a, b ^ offset))
-            arrays.append(lax.ppermute(array, "dsg", pairs))
-    return sources, arrays
+        items = ((vol_count * dsg_count, 0, 0),)
+        return smooth([whole], items, (), where, adjacency, per_owner, const)
+
+    def over(axis, array, bit):
+        count = vol_count if axis == "vol" else dsg_count
+        return lax.ppermute(array, axis, [(i, i ^ bit) for i in range(count)])
+
+    copies = jnp.broadcast_to(payload[None], (vol_count // 2,) + payload.shape)
+    along_z = lax.all_to_all(
+        copies, "vol", split_axis=0, concat_axis=0, tiled=True,
+        axis_index_groups=[list(range(y, vol_count, 2)) for y in range(2)],
+    )
+    here = along_z.reshape(-1, LANES)
+    half = here.shape[0] // 2
+    beside_y = over("vol", here, 1)
+    beside_x = over("dsg", here, 2)
+    corner = [over("dsg", beside_y[:half], 2), over("vol", beside_x[half:], 1)]
+    first = [here, over("dsg", here, 1), beside_x, over("dsg", beside_x, 1)]
+    first += [beside_y, over("dsg", beside_y, 1)]
+    items = ((4, 0, 0), (4, 0, 0), (4, 0, 1), (4, 0, 1), (4, 1, 0), (4, 1, 0))
+    early = early_sums(first, items, where, per_owner, patches)
+    last = corner + [over("dsg", c, 1) for c in corner]
+    return smooth(last, ((2, 1, 1),) * 4, early, where, adjacency, per_owner, const)
 
 
 def per_device(
     fields, far_geom, far_block, far_cell, far_patch, near_geom, near_cell, near_patch, adjacency
 ):
     vol_count, dsg_count = lax.axis_size("vol"), lax.axis_size("dsg")
-    vol_at, dsg_at = lax.axis_index("vol"), lax.axis_index("dsg")
     far_count = far_cell.shape[0]
     capacity = 5 * far_count // (2 * vol_count)
     const = {name: jnp.asarray(value) for name, value in constants().items()}
@@ -558,21 +655,13 @@
     )
     asked = lax.all_to_all(request, "vol", split_axis=0, concat_axis=0, tiled=True)
     near_dens = near_densities(near_cell, fields, near_geom)
-    answer = far_answers(asked, fields)
+    answer = far_answers(asked, fields, near_dens)
     reply = lax.all_to_all(answer, "vol", split_axis=0, concat_axis=0, tiled=True)
     near_patch, far_patch = near_patch.reshape(1, -1), far_patch.reshape(1, -1)
     near_grid, slots = near_grids(near_dens, near_geom, near_patch, far_patch)
     far_dens, payload = make_payload(reply, place, far_geom, far_patch, slots, near_grid, const)
 
-    sources, arrays = spread_payload(payload, vol_count, dsg_count)
-    where = [dsg_at]
-    for source in sources:
-        if source is None:
-            where.append(jnp.int32(0))
-        else:
-            where.append((vol_at ^ source[0]) * dsg_count + (dsg_at ^ source[1]))
-    where = jnp.stack([w.astype(jnp.int32) for w in where])
-    design = smooth(arrays, sources, where, adjacency, dsg_count, vol_count * dsg_count, const)
+    design = gather_and_smooth(payload, adjacency, vol_count, dsg_count, const)
     return far_dens.reshape(-1), design
 
 

time: 91 us -> 74.9 us (0.82)
  starting transfers between devices: 27.6 us -> 16.7 us
  Pallas kernels: 30.7 us -> 22.7 us
  waiting for transfers between devices: 13.5 us -> 17.4 us
  blocking collectives: 14 us -> 10.9 us
  local copies, waits for them, and re-layouts: 3.98 us -> 5.51 us
    ppermute x31 -> x9, starting transfers between devices: 24.2 us -> 3.43 us  [over(): return lax.ppermute(array, axis, [(i, i ^ bit) for i in range(count)])]
    pallas_call x1 -> x2, Pallas kernels: 17.8 us -> 9.15 us  [the longest x1 5.34 us: smooth(): pl.pallas_call(functools.partial(smooth_kernel, items, per_owner, bool(ea...]
    all_to_all x0 -> x1, starting transfers between devices: none -> 7.28 us  [per_device(): lax.all_to_all(request, 'vol', split_axis=0, concat_axis=0, tiled=True)]
    all_to_all x1, waiting for transfers between devices: 0.15 us -> 5.1 us  [per_device(): lax.all_to_all(answer, 'vol', split_axis=0, concat_axis=0, tiled=True)]
    all_to_all x1, blocking collectives: 14 us -> 10.9 us  [gather_and_smooth(): lax.all_to_all(copies, 'vol', split_axis=0, concat_axis=0, tiled=True, ax...]
    all_to_all x1, starting transfers between devices: 3.35 us -> 6.01 us  [per_device(): lax.all_to_all(answer, 'vol', split_axis=0, concat_axis=0, tiled=True)]
    unnamed x35 -> x37, local copies, waits for them, and re-layouts: 3.87 us -> 5.37 us
    ppermute x31 -> x9, waiting for transfers between devices: 13.4 us -> 12.3 us  [over(): return lax.ppermute(array, axis, [(i, i ^ bit) for i in range(count)])]
  transfers between devices with their start and end apart: 32 -> 11, of which waited for: 13 -> 5; matrix products, arithmetic and copies ran while one was open for 0% -> 0% of each run, Pallas kernels for 7% -> 14%
where the time goes in v1:
time: 74.9 us; the launch traced here: 74.2 us
  Pallas kernels  22.7 us (30%)
  waiting for transfers between devices  17.4 us (23%)
  starting transfers between devices  16.7 us (22%)
  blocking collectives  10.9 us (15%)
  local copies, waits for them, and re-layouts  5.51 us (7%)
  between operations  0.86 us (1%)
    ppermute x9, waiting for transfers between devices, over(): return lax.ppermute(array, axis, [(i, i ^ bit) for i in range(count)])  12.3 us
    all_to_all x1, blocking collectives, gather_and_smooth(): lax.all_to_all(copies, 'vol', split_axis=0, concat_axis=0, tiled=True, ax...  10.9 us
    all_to_all x1, starting transfers between devices, per_device(): lax.all_to_all(request, 'vol', split_axis=0, concat_axis=0, tiled=True)  7.28 us
    all_to_all x1, starting transfers between devices, per_device(): lax.all_to_all(answer, 'vol', split_axis=0, concat_axis=0, tiled=True)  6.01 us
    unnamed x37, local copies, waits for them, and re-layouts  5.37 us
    pallas_call x1, Pallas kernels, smooth(): pl.pallas_call(functools.partial(smooth_kernel, items, per_owner, bool(ea...  5.34 us
    all_to_all x1, waiting for transfers between devices, per_device(): lax.all_to_all(answer, 'vol', split_axis=0, concat_axis=0, tiled=True)  5.1 us
    pallas_call x1, Pallas kernels, near_densities(): pl.pallas_call(near_kernel, out_shape=jax.ShapeDtypeStruct((1, count), F3...  4.89 us
  transfers between devices with their start and end apart: 11, of which 5 were waited for; matrix products, arithmetic and copies ran while one was open for 0% of the time, Pallas kernels for 14%

profile of v1, /device:TPU:0, one launch (start us, length us, event | category | flops | bytes accessed | tf_op | source)
XLA Modules:
  0.0 74.2 jit_solution(5601577139421560655)
XLA Ops:
  0.6 0.0 copy-start.7
  0.6 0.7 copy-done.7
  1.4 0.0 copy-start.14
  1.4 0.7 copy-done.14
  2.0 0.0 copy-start.15
  2.0 0.7 copy-done.15
  2.7 1.4 %pack_requests.1 = (f32[8,8,160]{2,1,0:T(8,128)}, s32[1,512]{1,0:T(1,128)S(1)}) custom-call(f32[8,512]{1,0:T(8,128)S(1)} %copy-done.7, s32[1,512]{1,0:T(1,128)S(1)} %bitcast.14, s32[1,512]{1,0:T(1,128)S(1)} %bitcast.15), custom_call_target="tpu_custom_call" | custom-call | tf_op jit(solution)/shard_map/pack_requests/pallas_call | solution.py:119
  4.1 7.3 %all-to-all-start = ((f32[8,8,160]{2,1,0:T(8,128)}), f32[8,8,160]{2,1,0:T(8,128)S(1)}, u32[]{:S(2)}, u32[]{:S(2)}) async-start(f32[8,8,160]{2,1,0:T(8,128)} %get-tuple-element.10), calls=%async_computation | async-start | bytes 131072 | tf_op jit(solution)/shard_map/all_to_all | solution.py:656
  11.4 0.0 copy-start
  11.4 1.6 %copy-done = f32[4096,128]{1,0:T(8,128)S(1)} copy-done((f32[4096,128]{1,0:T(8,128)S(1)}, f32[4096,128]{1,0:T(8,128)}, u32[]{:S(2)}) %copy-start) | copy-done | bytes 2097176
  13.0 0.8 %copy-done.5 = f32[8,2048]{1,0:T(8,128)S(1)} copy-done((f32[8,2048]{1,0:T(8,128)S(1)}, f32[8,2048]{1,0:T(8,128)}, u32[]{:S(2)}) %copy-start.5) | copy-done | bytes 65560
  13.8 0.7 copy-done.12
  14.5 0.0 copy-start.1
  14.5 0.0 copy-start.3
  14.6 0.0 copy-start.4
  14.6 0.0 copy-start.8
  14.6 0.0 copy-start.10
  14.6 0.0 copy-start.11
  14.6 4.9 %near_densities.1.near_ref.dens_ref = f32[1,2048]{1,0:T(1,128)S(1)} custom-call(s32[2048]{0:T(1024)S(1)} %copy-done.12, f32[4096,128]{1,0:T(8,128)S(1)} %copy-done, f32[8,2048]{1,0:T(8,128)S(1)} %copy-done.5), custom_call_target="tpu_custom_call" | custom-call | flops 40000000 | bytes 4000000 | tf_op jit(solution)/shard_map/near_densities/pallas_call | solution.py:210
  19.5 0.0 copy-start.17
  19.5 0.0 all-to-all-done.request_ref
  19.5 0.0 copy-done.1
  19.5 4.0 %far_answers.1 = f32[8,1,160]{2,1,0:T(1,128)} custom-call(f32[8,8,160]{2,1,0:T(8,128)S(1)} %all-to-all-done.request_ref, f32[4096,128]{1,0:T(8,128)S(1)} %copy-done.1, f32[1,2048]{1,0:T(1,128)S(1)} %near_densities.1.near_ref.dens_ref), custom_call_target="tpu_custom_call" | custom-call | tf_op jit(solution)/shard_map/far_answers/pallas_call | solution.py:240
  23.6 6.0 %all-to-all-start.1 = ((f32[8,1,160]{2,1,0:T(1,128)}), f32[8,1,160]{2,1,0:T(1,128)S(1)}, u32[]{:S(2)}, u32[]{:S(2)}) async-start(f32[8,1,160]{2,1,0:T(1,128)} %far_answers.1), calls=%async_computation.1 | async-start | bytes 16384 | tf_op jit(solution)/shard_map/all_to_all | solution.py:659
  29.6 0.0 copy-done.6
  29.6 0.0 copy-done.13
  29.6 0.0 copy-done.16
  29.6 1.4 %near_grids.1 = (f32[256,64]{1,0:T(8,128)S(1)}, f32[8,128]{1,0:T(8,128)S(1)}) custom-call(f32[1,2048]{1,0:T(1,128)S(1)} %near_densities.1.near_ref.dens_ref, f32[8,2048]{1,0:T(8,128)S(1)} %copy-done.6, s32[1,2048]{1,0:T(1,128)S(1)} %bitcast.16, s32[1,512]{1,0:T(1,128)S(1)} %bitcast.12), custom_call_target="tpu_custom_call" | custom-call | flops 80000000 | bytes 1000000 | tf_op jit(solution)/shard_map/near_grids/pallas_call | solution.py:305
  31.0 0.0 copy-start.2
  31.0 0.0 copy-start.9
  31.0 5.1 %all-to-all-done.1.reply_ref = f32[8,1,160]{2,1,0:T(1,128)S(1)} async-done(((f32[8,1,160]{2,1,0:T(1,128)}), f32[8,1,160]{2,1,0:T(1,128)S(1)}, u32[]{:S(2)}, u32[]{:S(2)}) %all-to-all-start.1) | async-done | bytes 5152 | tf_op jit(solution)/shard_map/all_to_all | solution.py:659
  36.1 0.0 copy-done.3
  36.1 0.0 copy-done.4
  36.1 0.0 copy-done.8
  36.1 0.0 copy-done.10
  36.1 0.0 copy-done.11
  36.1 1.9 %make_payload.1 = (f32[1,512]{1,0:T(1,128)}, f32[160,128]{1,0:T(8,128)S(1)}) custom-call(f32[8,1,160]{2,1,0:T(1,128)S(1)} %all-to-all-done.1.reply_ref, s32[1,512]{1,0:T(1,128)S(1)} %get-tuple-element.11.place_ref, f32[8,512]{1,0:T(8,128)S(1)} %copy-done.8, s32[1,512]{1,0:T(1,128)S(1)} %bitcast.13, f32[8,128]{1,0:T(8,128)S(1)} %get-tuple-element.12.slot_ref, ...), custom_call_target="tpu_custom_call" | custom-call | tf_op jit(solution)/shard_map/make_payload/pallas_call | solution.py:375
  38.0 0.1 broadcast_in_dim.2
  38.1 10.9 %all_to_all.15 = f32[4,160,128]{2,1,0:T(8,128)S(1)} all-to-all(f32[4,160,128]{2,1,0:T(8,128)S(1)} %broadcast_in_dim.2), channel_id=1, replica_groups={{0,8,16,24},{4,12,20,28},{1,9,17,25},{5,13,21,29},{2,10,18,26},{6,14,22..., dimensions={0} | all-to-all | bytes 655360 | tf_op jit(solution)/shard_map/all_to_all | solution.py:628
  49.1 1.5 %collective-permute-start.2 = (f32[640,128]{1,0:T(8,128)S(1)}, f32[640,128]{1,0:T(8,128)S(1)}, u32[]{:S(2)}, u32[]{:S(2)}) collective-permute-start(f32[640,128]{1,0:T(8,128)S(1)} %bitcast.8), channel_id=1, source_target_pairs={{0,2},{1,3},{2,0},{3,1},{4,6},{5,7},{6,4},{7,5},{8,10},{9,11},{10,... | collective-permute-start | bytes 983048 | tf_op jit(solution)/shard_map/ppermute | solution.py:625
  50.5 0.5 collective-permute-start
  51.1 0.0 collective-permute-start.6
  51.1 5.0 %collective-permute-done.2.rest_2_ = f32[640,128]{1,0:T(8,128)S(1)} collective-permute-done((f32[640,128]{1,0:T(8,128)S(1)}, f32[640,128]{1,0:T(8,128)S(1)}, u32[]{:S(2)}, u32[]{:S(2)}) %collective-permute-start.2) | collective-permute-done | bytes 327712 | tf_op jit(solution)/shard_map/ppermute | solution.py:625
  56.1 0.0 collective-permute-start.7
  56.1 1.5 %collective-permute-done.rest_4_ = f32[640,128]{1,0:T(8,128)S(1)} collective-permute-done((f32[640,128]{1,0:T(8,128)S(1)}, f32[640,128]{1,0:T(8,128)S(1)}, u32[]{:S(2)}, u32[]{:S(2)}) %collective-permute-start) | collective-permute-done | bytes 327712 | tf_op jit(solution)/shard_map/ppermute | solution.py:625
  57.6 0.0 collective-permute-start.8
  57.6 0.6 collective-permute-start.1
  58.3 0.6 collective-permute-start.3
  58.9 5.5 %collective-permute-done.1.rest_0_ = f32[320,128]{1,0:T(8,128)S(1)} collective-permute-done((f32[320,128]{1,0:T(8,128)S(1)}, f32[320,128]{1,0:T(8,128)S(1)}, u32[]{:S(2)}, u32[]{:S(2)}) %collective-permute-start.1) | collective-permute-done | bytes 163872 | tf_op jit(solution)/shard_map/ppermute | solution.py:625
  64.3 0.0 collective-permute-start.4
  64.3 0.3 collective-permute-done.3.rest_1_
  64.7 0.2 collective-permute-start.5
  64.8 0.0 copy-done.17
  64.8 0.1 copy.17.adj_ref
  64.9 0.1 pad_add_fusion.where_ref
  65.0 0.0 collective-permute-done.6.rest_1_
  65.0 0.0 collective-permute-done.7.rest_3_
  65.0 0.0 collective-permute-done.8.rest_5_
  65.0 3.8 %early_sums.1 = (f32[2,768,128]{2,1,0:T(8,128)S(1)}, f32[4,3,96,256]{3,2,1,0:T(8,128)S(1)}) custom-call(s32[2]{0:T(128)S(1)} %pad_add_fusion.where_ref, f32[640,128]{1,0:T(8,128)S(1)} %bitcast.11, f32[640,128]{1,0:T(8,128)S(1)} %collective-permute-done.6.rest_1_, f32[640,128]{1,0:T(8,128)S(1)} %collective-permute-done.2.rest_2_, ...), custom_call_target="tpu_custom_call" | custom-call | flops 20000000 | bytes 3000000 | tf_op jit(solution)/shard_map/early_sums/pallas_call | solution.py:479
  68.8 0.0 collective-permute-done.4.rest_2_
  68.9 0.0 collective-permute-done.5.rest_3_
  68.9 0.0 copy-done.2
  68.9 0.0 copy-done.9
  68.9 5.3 %smooth.1 = f32[24,64,64]{2,1,0:T(8,128)} custom-call(s32[2]{0:T(128)S(1)} %pad_add_fusion.where_ref, s32[96,4]{1,0:T(8,128)S(1)} %copy.17.adj_ref, f32[256,512]{1,0:T(8,128)S(1)} %copy-done.2, f32[64,64]{1,0:T(8,128)S(1)} %copy-done.4, f32[128,128]{1,0:T(8,128)S(1)} %copy-done.3, f32[64,128]{1,0:T(8,128)S(1)} %copy-done.9, f32[8,64]{1,0:T(8,128)S(1)} %copy-done.10, ...), custom_call_target="tpu_custom_call" | custom-call | tf_op jit(solution)/shard_map/smooth/pallas_call | solution.py:594
  (7 shorter events, 0.0 us)
Async XLA Ops:
  0.6 0.7 copy-start.7
  1.4 0.7 copy-start.14
  2.0 0.7 copy-start.15
  4.1 15.4 %all-to-all-start = ((f32[8,8,160]{2,1,0:T(8,128)}), f32[8,8,160]{2,1,0:T(8,128)S(1)}, u32[]{:S(2)}, u32[]{:S(2)}) async-start(f32[8,8,160]{2,1,0:T(8,128)} %get-tuple-element.10), calls=%async_computation | async-start | bytes 131072 | tf_op jit(solution)/shard_map/all_to_all | solution.py:656
  11.4 1.6 %copy-start = (f32[4096,128]{1,0:T(8,128)S(1)}, f32[4096,128]{1,0:T(8,128)}, u32[]{:S(2)}) copy-start(f32[4096,128]{1,0:T(8,128)} %fields_ref.3) | copy-start | bytes 6291460
  13.0 0.8 %copy-start.5 = (f32[8,2048]{1,0:T(8,128)S(1)}, f32[8,2048]{1,0:T(8,128)}, u32[]{:S(2)}) copy-start(f32[8,2048]{1,0:T(8,128)} %geom_ref.6) | copy-start | bytes 196612
  13.8 0.7 copy-start.12
  14.5 5.0 %copy-start.1 = (f32[4096,128]{1,0:T(8,128)S(1)}, f32[4096,128]{1,0:T(8,128)}, u32[]{:S(2)}) copy-start(f32[4096,128]{1,0:T(8,128)} %fields_ref.3) | copy-start | bytes 6291460
  14.5 15.0 %copy-start.6 = (f32[8,2048]{1,0:T(8,128)S(1)}, f32[8,2048]{1,0:T(8,128)}, u32[]{:S(2)}) copy-start(f32[8,2048]{1,0:T(8,128)} %geom_ref.6) | copy-start | bytes 196612
  14.5 15.0 %copy-start.13 = (s32[512]{0:T(512)S(1)}, s32[512]{0:T(512)}, u32[]{:S(2)}) copy-start(s32[512]{0:T(512)} %param.19) | copy-start | bytes 6148
  14.5 15.1 %copy-start.16 = (s32[2048]{0:T(1024)S(1)}, s32[2048]{0:T(1024)}, u32[]{:S(2)}) copy-start(s32[2048]{0:T(1024)} %param.22) | copy-start | bytes 24580
  14.5 21.5 %copy-start.3 = (f32[128,128]{1,0:T(8,128)S(1)}, f32[128,128]{1,0:T(8,128)}, u32[]{:S(2)}) copy-start(f32[128,128]{1,0:T(8,128)} %constant.35.clone.pair_ref) | copy-start | bytes 196612
  14.6 21.5 %copy-start.4 = (f32[64,64]{1,0:T(8,128)S(1)}, f32[64,64]{1,0:T(8,128)}, u32[]{:S(2)}) copy-start(f32[64,64]{1,0:T(8,128)} %constant.34.clone.basis_ref) | copy-start | bytes 49156
  14.6 21.5 %copy-start.8 = (f32[8,512]{1,0:T(8,128)S(1)}, f32[8,512]{1,0:T(8,128)}, u32[]{:S(2)}) copy-start(f32[8,512]{1,0:T(8,128)} %geom_ref.7) | copy-start | bytes 49156
  14.6 21.5 %copy-start.10 = (f32[8,64]{1,0:T(8,128)S(1)}, f32[8,64]{1,0:T(8,128)}, u32[]{:S(2)}) copy-start(f32[8,64]{1,0:T(8,128)} %constant.36.clone.edge_ref) | copy-start | bytes 6148
  14.6 21.5 %copy-start.11 = (f32[8,64]{1,0:T(8,128)S(1)}, f32[8,64]{1,0:T(8,128)}, u32[]{:S(2)}) copy-start(f32[8,64]{1,0:T(8,128)} %constant.37.clone.scale_ref) | copy-start | bytes 6148
  19.5 45.3 %copy-start.17 = (s32[96,4]{0,1:T(4,128)S(1)}, s32[96,4]{0,1:T(4,128)}, u32[]{:S(2)}) copy-start(s32[96,4]{0,1:T(4,128)} %param.23) | copy-start | bytes 4612
  23.6 12.5 %all-to-all-start.1 = ((f32[8,1,160]{2,1,0:T(1,128)}), f32[8,1,160]{2,1,0:T(1,128)S(1)}, u32[]{:S(2)}, u32[]{:S(2)}) async-start(f32[8,1,160]{2,1,0:T(1,128)} %far_answers.1), calls=%async_computation.1 | async-start | bytes 16384 | tf_op jit(solution)/shard_map/all_to_all | solution.py:659
  31.0 37.9 %copy-start.2 = (f32[256,512]{1,0:T(8,128)S(1)}, f32[256,512]{1,0:T(8,128)}, u32[]{:S(2)}) copy-start(f32[256,512]{1,0:T(8,128)} %constant.39.clone.coupling_ref) | copy-start | bytes 1572868
  31.0 37.9 %copy-start.9 = (f32[64,128]{1,0:T(8,128)S(1)}, f32[64,128]{1,0:T(8,128)}, u32[]{:S(2)}) copy-start(f32[64,128]{1,0:T(8,128)} %constant.38.clone.series_ref) | copy-start | bytes 98308
  49.1 7.1 %collective-permute-start.2 = (f32[640,128]{1,0:T(8,128)S(1)}, f32[640,128]{1,0:T(8,128)S(1)}, u32[]{:S(2)}, u32[]{:S(2)}) collective-permute-start(f32[640,128]{1,0:T(8,128)S(1)} %bitcast.8), channel_id=1, source_target_pairs={{0,2},{1,3},{2,0},{3,1},{4,6},{5,7},{6,4},{7,5},{8,10},{9,11},{10,... | collective-permute-start | bytes 983048 | tf_op jit(solution)/shard_map/ppermute | solution.py:625
  50.5 7.1 %collective-permute-start = (f32[640,128]{1,0:T(8,128)S(1)}, f32[640,128]{1,0:T(8,128)S(1)}, u32[]{:S(2)}, u32[]{:S(2)}) collective-permute-start(f32[640,128]{1,0:T(8,128)S(1)} %bitcast.9), channel_id=1, source_target_pairs={{0,4},{4,0},{8,12},{12,8},{16,20},{20,16},{24,28},{28,24},{1,5},{5... | collective-permute-start | bytes 983048 | tf_op jit(solution)/shard_map/ppermute | solution.py:625
  51.1 13.9 %collective-permute-start.6 = (f32[640,128]{1,0:T(8,128)S(1)}, f32[640,128]{1,0:T(8,128)S(1)}, u32[]{:S(2)}, u32[]{:S(2)}) collective-permute-start(f32[640,128]{1,0:T(8,128)S(1)} %bitcast.10), channel_id=1, source_target_pairs={{0,1},{1,0},{2,3},{3,2},{4,5},{5,4},{6,7},{7,6},{8,9},{9,8},{10,11... | collective-permute-start | bytes 983048 | tf_op jit(solution)/shard_map/ppermute | solution.py:625
  56.1 8.9 %collective-permute-start.7 = (f32[640,128]{1,0:T(8,128)S(1)}, f32[640,128]{1,0:T(8,128)S(1)}, u32[]{:S(2)}, u32[]{:S(2)}) collective-permute-start(f32[640,128]{1,0:T(8,128)S(1)} %collective-permute-done.2.rest_2_), channel_id=1, source_target_pairs={{0,1},{1,0},{2,3},{3,2},{4,5},{5,4},{6,7},{7,6},{8,9},{9,8},{10,11... | collective-permute-start | bytes 983048 | tf_op jit(solution)/shard_map/ppermute | solution.py:625
  57.6 7.4 %collective-permute-start.8 = (f32[640,128]{1,0:T(8,128)S(1)}, f32[640,128]{1,0:T(8,128)S(1)}, u32[]{:S(2)}, u32[]{:S(2)}) collective-permute-start(f32[640,128]{1,0:T(8,128)S(1)} %collective-permute-done.rest_4_), channel_id=1, source_target_pairs={{0,1},{1,0},{2,3},{3,2},{4,5},{5,4},{6,7},{7,6},{8,9},{9,8},{10,11... | collective-permute-start | bytes 983048 | tf_op jit(solution)/shard_map/ppermute | solution.py:625
  57.6 6.7 %collective-permute-start.1 = (f32[320,128]{1,0:T(8,128)S(1)}, f32[320,128]{1,0:T(8,128)S(1)}, u32[]{:S(2)}, u32[]{:S(2)}) collective-permute-start(f32[320,128]{1,0:T(8,128)S(1)} %slice.8), channel_id=1, source_target_pairs={{0,2},{1,3},{2,0},{3,1},{4,6},{5,7},{6,4},{7,5},{8,10},{9,11},{10,... | collective-permute-start | bytes 491528 | tf_op jit(solution)/shard_map/ppermute | solution.py:625
  58.3 6.4 %collective-permute-start.3 = (f32[320,128]{1,0:T(8,128)S(1)}, f32[320,128]{1,0:T(8,128)S(1)}, u32[]{:S(2)}, u32[]{:S(2)}) collective-permute-start(f32[320,128]{1,0:T(8,128)S(1)} %slice.9), channel_id=1, source_target_pairs={{0,4},{4,0},{8,12},{12,8},{16,20},{20,16},{24,28},{28,24},{1,5},{5... | collective-permute-start | bytes 491528 | tf_op jit(solution)/shard_map/ppermute | solution.py:625
  64.3 4.5 %collective-permute-start.4 = (f32[320,128]{1,0:T(8,128)S(1)}, f32[320,128]{1,0:T(8,128)S(1)}, u32[]{:S(2)}, u32[]{:S(2)}) collective-permute-start(f32[320,128]{1,0:T(8,128)S(1)} %collective-permute-done.1.rest_0_), channel_id=1, source_target_pairs={{0,1},{1,0},{2,3},{3,2},{4,5},{5,4},{6,7},{7,6},{8,9},{9,8},{10,11... | collective-permute-start | bytes 491528 | tf_op jit(solution)/shard_map/ppermute | solution.py:625
  64.7 4.2 %collective-permute-start.5 = (f32[320,128]{1,0:T(8,128)S(1)}, f32[320,128]{1,0:T(8,128)S(1)}, u32[]{:S(2)}, u32[]{:S(2)}) collective-permute-start(f32[320,128]{1,0:T(8,128)S(1)} %collective-permute-done.3.rest_1_), channel_id=1, source_target_pairs={{0,1},{1,0},{2,3},{3,2},{4,5},{5,4},{6,7},{7,6},{8,9},{9,8},{10,11... | collective-permute-start | bytes 491528 | tf_op jit(solution)/shard_map/ppermute | solution.py:625

commit v2 on v1

--- a/solution.py
+++ b/solution.py
@@ -15,7 +15,7 @@
 SMOOTHING = 16.0
 NO_PATCH = 1.0e6
 GRID_ROWS = GROUP // 2 * CTRL
-PAYLOAD_ROWS = GRID_ROWS + GROUP * 8
+PAYLOAD_ROWS = GRID_ROWS + 2 * GROUP
 F32 = jnp.float32
 BF16 = jnp.bfloat16
 EXACT = lax.Precision.HIGHEST
@@ -23,6 +23,7 @@
 SMEM = pl.BlockSpec(memory_space=pltpu.SMEM)
 ANY = pl.BlockSpec(memory_space=pl.ANY)
 WHOLE = pl.BlockSpec()
+HBM = pl.BlockSpec(memory_space=pltpu.HBM)
 
 
 def params(megabytes):
@@ -63,7 +64,7 @@
         basis=np.float32(basis),
         basis_pair=np.float32(np.kron(np.eye(2), basis)),
         edge_rows=np.float32(edge_rows),
-        scale_rows=np.float32(scale_rows),
+        scale_rows=np.float32(np.concatenate([scale_rows, scale_rows], 1)),
         series=np.float32(np.concatenate([series, series], 1)),
         coupling=np.float32(np.concatenate([coupling(0), coupling(1)], 1)),
     )
@@ -92,7 +93,42 @@
     return lax.broadcasted_iota(jnp.int32, shape, axis)
 
 
-def pack_kernel(capacity, geom_ref, block_ref, cell_ref, request_ref, place_ref):
+def halves(x):
+    high = x.astype(BF16)
+    return high, (x - high.astype(F32)).astype(BF16)
+
+
+def two(x):
+    return jnp.concatenate(halves(x), 1)
+
+
+def fold(x):
+    half = x.shape[1] // 2
+    return x[:, :half] + x[:, half:]
+
+
+def product(x, y):
+    x_high, x_low = halves(x)
+    y_high, y_low = halves(y)
+    return nn(x_high, y_high) + (nn(x_low, y_high) + nn(x_high, y_low))
+
+
+def nt_product(x, y):
+    x_high, x_low = halves(x)
+    y_high, y_low = halves(y)
+    return nt(x_high, y_high) + (nt(x_low, y_high) + nt(x_high, y_low))
+
+
+def fetch(pairs, sem):
+    copies = [pltpu.make_async_copy(a, b, sem.at[i]) for i, (a, b) in enumerate(pairs)]
+    for copy in copies:
+        copy.start()
+    for copy in copies:
+        copy.wait()
+
+
+def pack_kernel(capacity, geom_in, block_in, cell_in, request_ref, place_ref, geom_ref, block_ref, cell_ref, sem):
+    fetch([(geom_in, geom_ref), (block_in, block_ref), (cell_in, cell_ref)], sem)
     owners = request_ref.shape[0]
     count = geom_ref.shape[1]
     block = block_ref[...]
@@ -122,15 +158,21 @@
             jax.ShapeDtypeStruct((owners, 8, capacity), F32),
             jax.ShapeDtypeStruct((1, count), jnp.int32),
         ),
-        in_specs=[WHOLE] * 3,
+        in_specs=[HBM] * 3,
         out_specs=(VMEM, VMEM),
-        compiler_params=params(16),
+        scratch_shapes=[
+            pltpu.VMEM((8, count), F32),
+            pltpu.VMEM((1, count), jnp.int32),
+            pltpu.VMEM((1, count), jnp.int32),
+            pltpu.SemaphoreType.DMA((3,)),
+        ],
+        compiler_params=params(60),
         name="pack_requests",
     )(far_geom, far_block, far_cell)
 
 
 def gather_rows(cells, fields_ref, rows_ref, count):
-    unroll = 16
+    unroll = 32
 
     def step(i, carry):
         for u in range(unroll):
@@ -196,11 +238,13 @@
         out_ref[:, pl.ds(at, LANES)] = tile_density(columns, geom_ref[:, pl.ds(at, LANES)])
         return carry
 
-    lax.fori_loop(0, count // LANES, step, 0)
-
-
-def near_kernel(cell_ref, fields_ref, geom_ref, out_ref, rows_ref):
-    count = geom_ref.shape[1]
+    tiles = count // LANES
+    lax.fori_loop(0, tiles, step, 0, unroll=4 if tiles % 4 == 0 else 2)
+
+
+def near_kernel(cell_in, fields_in, geom_in, out_ref, cell_ref, fields_ref, geom_ref, rows_ref, sem):
+    count = geom_in.shape[1]
+    fetch([(fields_in, fields_ref), (cell_in, cell_ref), (geom_in, geom_ref)], sem)
     gather_rows(lambda p: cell_ref[p], fields_ref, rows_ref, count)
     densities(rows_ref, geom_ref, out_ref, count)
 
@@ -210,17 +254,29 @@
     return pl.pallas_call(
         near_kernel,
         out_shape=jax.ShapeDtypeStruct((1, count), F32),
-        in_specs=[SMEM, VMEM, WHOLE],
+        in_specs=[HBM] * 3,
         out_specs=VMEM,
-        scratch_shapes=[pltpu.VMEM((count, LANES), F32)],
-        compiler_params=params(24),
+        scratch_shapes=[
+            pltpu.SMEM((count,), jnp.int32),
+            pltpu.VMEM(fields.shape, F32),
+            pltpu.VMEM((8, count), F32),
+            pltpu.VMEM((count, LANES), F32),
+            pltpu.SemaphoreType.DMA((3,)),
+        ],
+        compiler_params=params(60),
         cost_estimate=pl.CostEstimate(flops=40_000_000, bytes_accessed=4_000_000, transcendentals=0),
         name="near_densities",
     )(near_cell, fields, near_geom)
 
 
-def far_kernel(request_ref, fields_ref, near_ref, out_ref, query_ref, cell_v, cell_s, rows_ref, dens_ref, sem):
-    owners, _, capacity = request_ref.shape
+def far_kernel(
+    request_in, fields_in, near_ref, out_ref, request_ref, fields_ref, query_ref, cell_v, cell_s, rows_ref, dens_ref,
+    sems, sem,
+):
+    owners, _, capacity = request_in.shape
+    fields_copy = pltpu.make_async_copy(fields_in, fields_ref, sems.at[1])
+    fields_copy.start()
+    fetch([(request_in, request_ref)], sems)
     count = owners * capacity
     for o in range(owners):
         query_ref[:, o * capacity : (o + 1) * capacity] = request_ref[o]
@@ -228,6 +284,7 @@
     copy = pltpu.make_async_copy(cell_v, cell_s, sem)
     copy.start()
     copy.wait()
+    fields_copy.wait()
     gather_rows(lambda p: cell_s[0, p], fields_ref, rows_ref, count)
     densities(rows_ref, query_ref, dens_ref, count)
     for o in range(owners):
@@ -240,14 +297,17 @@
     return pl.pallas_call(
         far_kernel,
         out_shape=jax.ShapeDtypeStruct((owners, 1, capacity), F32),
-        in_specs=[VMEM, VMEM, ANY],
+        in_specs=[ANY, ANY, ANY],
         out_specs=VMEM,
         scratch_shapes=[
+            pltpu.VMEM(requests.shape, F32),
+            pltpu.VMEM(fields.shape, F32),
             pltpu.VMEM((8, count), F32),
             pltpu.VMEM((1, count), jnp.int32),
             pltpu.SMEM((1, count), jnp.int32),
             pltpu.VMEM((count, LANES), F32),
             pltpu.VMEM((1, count), F32),
+            pltpu.SemaphoreType.DMA((2,)),
             pltpu.SemaphoreType.DMA,
         ],
         compiler_params=params(24),
@@ -274,11 +334,6 @@
     return out
 
 
-def halves(x):
-    high = x.astype(BF16)
-    return high, (x - high.astype(F32)).astype(BF16)
-
-
 def slot_grids(density, s, t, patch, slots):
     left_high, left_low = halves(spline_columns(s))
     right_high, right_low = halves(spline_columns(t) * density)
@@ -318,7 +373,7 @@
 
 def payload_kernel(
     reply_ref, place_ref, geom_ref, far_ref, slot_ref, near_ref,
-    basis_ref, pair_ref, edge_ref, scale_ref,
+    basis_ref, pair_ref,
     dens_ref, out_ref, flat_ref,
 ):
     owners, _, capacity = reply_ref.shape
@@ -339,34 +394,17 @@
     names = jnp.zeros((1, LANES), F32)
     for s in range(GROUP):
         names = jnp.where(lane == s, slot_ref[s : s + 1, :], names)
-    edge = edge_ref[...]
-    scale = scale_ref[...]
-    blank = jnp.zeros((8, CTRL), F32)
-    both = jnp.concatenate(
-        [jnp.concatenate([edge, blank], 1), jnp.concatenate([blank, edge], 1)], 0
-    )
-    out_ref[GRID_ROWS + 6 * GROUP : GRID_ROWS + 7 * GROUP, :] = slot_ref[0:GROUP, :]
-    out_ref[GRID_ROWS + 7 * GROUP : GRID_ROWS + 8 * GROUP, :] = jnp.broadcast_to(names, (GROUP, LANES))
+    out_ref[GRID_ROWS : GRID_ROWS + GROUP, :] = slot_ref[0:GROUP, :]
+    out_ref[GRID_ROWS + GROUP : PAYLOAD_ROWS, :] = jnp.broadcast_to(names, (GROUP, LANES))
+    blocks = [
+        jnp.concatenate([grids[a * CTRL : (a + 1) * CTRL], grids[(a + 1) * CTRL : (a + 2) * CTRL]], 1)
+        for a in range(0, GROUP, 2)
+    ]
+    turned = product(jnp.concatenate(blocks, 0), pair_ref[...])
+    turned = jnp.concatenate([turned[:CTRL], turned[CTRL:]], 1)
+    spectral = product(basis_ref[...], turned)
     for pair in range(GROUP // 2):
-        a, b = 2 * pair, 2 * pair + 1
-        both_grids = jnp.concatenate(
-            [grids[a * CTRL : (a + 1) * CTRL], grids[b * CTRL : (b + 1) * CTRL]], 1
-        )
-        spectral = nn(nn(basis_ref[...], both_grids, precision=EXACT), pair_ref[...], precision=EXACT)
-        out_ref[pair * CTRL : (pair + 1) * CTRL, :] = spectral
-        along_rows = nn(edge, spectral, precision=EXACT)
-        along_cols = nt(both, spectral, precision=EXACT)
-        for side, slot in enumerate((a, b)):
-            block = jnp.concatenate(
-                [
-                    along_rows[:, side * CTRL : (side + 1) * CTRL] * scale,
-                    along_cols[8 * side : 8 * side + 8] * scale,
-                ],
-                1,
-            )
-            for r in range(6):
-                at = GRID_ROWS + GROUP * r + slot
-                out_ref[at : at + 1, :] = block[r : r + 1]
+        out_ref[pair * CTRL : (pair + 1) * CTRL, :] = spectral[:, pair * LANES : (pair + 1) * LANES]
 
 
 def make_payload(reply, place, far_geom, far_patch, slots, near_grid, const):
@@ -378,29 +416,25 @@
             jax.ShapeDtypeStruct((1, count), F32),
             jax.ShapeDtypeStruct((PAYLOAD_ROWS, LANES), F32),
         ),
-        in_specs=[VMEM] * 2 + [WHOLE] * 2 + [VMEM] * 2 + [WHOLE] * 4,
+        in_specs=[VMEM] * 2 + [WHOLE] * 2 + [VMEM] * 2 + [WHOLE] * 2,
         out_specs=(VMEM, VMEM),
         scratch_shapes=[pltpu.VMEM((1, owners * capacity), F32)],
         compiler_params=params(24),
         name="make_payload",
     )(
         reply, place, far_geom, far_patch, slots, near_grid,
-        const["basis"], const["basis_pair"], const["edge_rows"], const["scale_rows"],
+        const["basis"], const["basis_pair"],
     )
 
 
-def two(x):
-    return jnp.concatenate(halves(x), 1)
-
-
-def fold(x):
-    half = x.shape[1] // 2
-    return x[:, :half] + x[:, half:]
-
-
-def absorb(first_own, y_at, per_owner, items, sums, groups, name_v, name_s, edges, name_sem):
+def pair_rows(edge):
+    blank = jnp.zeros((8, CTRL), F32)
+    return jnp.concatenate([jnp.concatenate([edge, blank], 1), jnp.concatenate([blank, edge], 1)], 0)
+
+
+def absorb(first_own, y_at, per_owner, items, sums, groups, edge, scale, name_v, name_s, edges, where_to, name_sem):
     patches = groups.shape[2]
-    total = sum(parts for _, parts, _, _ in items)
+    low8 = iota((8, LANES), 1) < CTRL
     at = 0
     for ref, parts, _, _ in items:
         for p in range(parts):
@@ -410,102 +444,91 @@
     names = pltpu.make_async_copy(name_v, name_s, name_sem)
     names.start()
 
-    for group in sorted({2 * dy + dx for _, _, dy, dx in items}):
+    sums[...] = jnp.zeros(sums.shape, F32)
+    edge_high, edge_low = halves(edge)
+    edge_both = jnp.concatenate([edge_high, edge_low], 0)
+    both_high, both_low = halves(pair_rows(edge))
+    both_both = jnp.concatenate([both_high, both_low], 0)
+    for group in sorted({(dy, dx) for _, _, dy, dx in items}):
         at = 0
-        for ref, parts, dy, dx in items:
-            if 2 * dy + dx == group:
-                for p in range(parts):
-                    for r in range(7):
-                        row = p * PAYLOAD_ROWS + GRID_ROWS + GROUP * r
-                        edges[r, at : at + GROUP, :] = ref[row : row + GROUP, :]
-                    at += GROUP
+        chunks = [
+            (ref, p) for ref, parts, dy, dx in items if (dy, dx) == group for p in range(0, parts, 2)
+        ]
+        for ref, start in chunks:
+            blocks = []
+            for p in (start, start + 1):
+                row = p * PAYLOAD_ROWS
+                blocks += [halves(ref[row + q * CTRL : row + (q + 1) * CTRL, :]) for q in range(GROUP // 2)]
+                row += GRID_ROWS
+                where_to[at + GROUP * (p - start) : at + GROUP * (p - start + 1), :] = ref[row : row + GROUP, :]
+            high, low = [jnp.concatenate(x, 1) for x in zip(*blocks)]
+            along_rows = nn(edge_both, high)
+            along_rows = (along_rows[:8] + along_rows[8:]) + nn(edge_high, low)
+            high, low = [jnp.concatenate(x, 0) for x in zip(*blocks)]
+            along_cols = nt(both_both, high)
+            along_cols = (along_cols[:16] + along_cols[16:]) + nt(both_high, low)
+            for s in range(2 * GROUP):
+                q = s // 2
+                first = along_rows[:, q * LANES : (q + 1) * LANES]
+                second = along_cols[8 * (s % 2) : 8 * (s % 2) + 8, q // 2 * LANES : (q // 2 + 1) * LANES]
+                if s % 2:
+                    first = pltpu.roll(first, CTRL, 1)
+                if q % 2 == 0:
+                    second = pltpu.roll(second, CTRL, 1)
+                edges[8 * at : 8 * at + 8, :] = jnp.where(low8, first, second) * scale
+                at += 1
         lane = iota((at, LANES), 1)
-        place = jnp.where(lane == edges[6, :at, :].astype(jnp.int32), 1.0, 0.0).T[:patches].astype(BF16)
+        place = jnp.where(lane == where_to[:at, :].astype(jnp.int32), 1.0, 0.0).T[:patches].astype(BF16)
         for k in range(3):
-            rows = jnp.concatenate([edges[2 * k, :at, :], edges[2 * k + 1, :at, :]], 1)
-            groups[(group // 2 ^ y_at) * 2 + group % 2, k] = fold(nn(place, two(rows)))
+            rows = [edges[pl.ds(2 * k + side, at, stride=8), :] for side in range(2)]
+            groups[(group[0] ^ y_at) * 2 + group[1], k] = fold(nn(place, two(jnp.concatenate(rows, 1))))
 
     names.wait()
-    low_half = iota((CTRL, LANES), 1) < CTRL
-    at = 0
-    for ref, parts, dy, _ in items:
-
-        def add_payload(p, carry, ref=ref, at=at, dy=dy):
-            for s in range(GROUP):
-                patch = name_s[at + p, s] - first_own
-
-                @pl.when((patch >= 0) & (patch < per_owner))
-                def _():
-                    row = pl.multiple_of(p * PAYLOAD_ROWS + (s // 2) * CTRL, 8)
-                    block = ref[pl.ds(row, CTRL), :]
-                    block = jnp.where(patch % 2 == s % 2, block, pltpu.roll(block, CTRL, 1))
-                    block = jnp.where(low_half == (patch % 2 == 0), block, 0.0)
-                    own = pl.multiple_of(patch // 2 * CTRL, CTRL)
-                    sums[dy ^ y_at, pl.ds(own, CTRL), :] = sums[dy ^ y_at, pl.ds(own, CTRL), :] + block
-
-            return carry
-
-        lax.fori_loop(0, parts, add_payload, 0)
-        at += parts
-
-
-def early_kernel(per_owner, items, where_ref, *rest):
-    refs = rest[: len(items)]
-    sums, groups, name_v, name_s, edges, name_sem = rest[len(items) :]
-    sums[...] = jnp.zeros(sums.shape, F32)
-    groups[...] = jnp.zeros(groups.shape, F32)
-    items = [(ref, *item) for ref, item in zip(refs, items)]
-    absorb(where_ref[0] * per_owner, where_ref[1], per_owner, items, sums, groups, name_v, name_s, edges, name_sem)
-
-
-def absorb_scratch(items):
-    total = sum(item[0] for item in items)
-    return [
-        pltpu.VMEM((total, LANES), jnp.int32),
-        pltpu.SMEM((total, LANES), jnp.int32),
-        pltpu.VMEM((7, total * GROUP, LANES), F32),
-        pltpu.SemaphoreType.DMA,
-    ]
-
-
-def sum_shapes(per_owner, patches):
-    return (
-        jax.ShapeDtypeStruct((2, per_owner // 2 * CTRL, LANES), F32),
-        jax.ShapeDtypeStruct((4, 3, patches, 4 * CTRL), F32),
-    )
-
-
-def early_sums(payloads, items, where, per_owner, patches):
-    return pl.pallas_call(
-        functools.partial(early_kernel, per_owner, items),
-        out_shape=sum_shapes(per_owner, patches),
-        in_specs=[SMEM] + [VMEM] * len(payloads),
-        out_specs=(VMEM, VMEM),
-        scratch_shapes=absorb_scratch(items),
-        compiler_params=params(16),
-        cost_estimate=pl.CostEstimate(flops=20_000_000, bytes_accessed=3_000_000, transcendentals=0),
-        name="early_sums",
-    )(where, *payloads)
+
+    def add_items(wanted):
+        at = 0
+        for ref, parts, dy, _ in items:
+
+            def add_payload(p, carry, ref=ref, at=at):
+                for s in range(GROUP):
+                    patch = name_s[at + p, s] - first_own
+
+                    @pl.when((patch >= 0) & (patch < per_owner))
+                    def _():
+                        row = pl.multiple_of(p * PAYLOAD_ROWS + (s // 2) * CTRL, 8)
+                        own = pl.multiple_of(patch * CTRL, CTRL)
+                        sums[s % 2, pl.ds(own, CTRL), :] = sums[s % 2, pl.ds(own, CTRL), :] + ref[pl.ds(row, CTRL), :]
+
+                return carry
+
+            if dy == wanted:
+                lax.fori_loop(0, parts, add_payload, 0)
+            at += parts
+
+    @pl.when(y_at == 0)
+    def _():
+        add_items(0)
+        add_items(1)
+
+    @pl.when(y_at != 0)
+    def _():
+        add_items(1)
+        add_items(0)
 
 
 def smooth_kernel(
-    items, per_owner, has_early, where_ref, adj_ref, coupling_ref, basis_ref, pair_ref, series_ref, edge_ref,
-    scale_ref, *rest
+    items, per_owner, where_ref, adj_ref, coupling_ref, basis_ref, pair_ref, series_ref, edge_ref, scale_ref, *rest
 ):
     refs, rest = rest[: len(items)], rest[len(items) :]
-    if has_early:
-        early_sum, early_group, *rest = rest
-    out_ref, sums, groups, name_v, name_s, edges, name_sem, halo_all, halo_rows = rest
-    if has_early:
-        sums[...] = early_sum[...]
-        groups[...] = early_group[...]
-    else:
-        sums[...] = jnp.zeros(sums.shape, F32)
-        groups[...] = jnp.zeros(groups.shape, F32)
+    out_ref, sums, groups, halo_all, halo_rows, *scratch = rest
     patches = adj_ref.shape[0]
     first_own = pl.multiple_of(where_ref[0] * per_owner, 8)
     items = [(ref, *item) for ref, item in zip(refs, items)]
-    absorb(first_own, where_ref[1], per_owner, items, sums, groups, name_v, name_s, edges, name_sem)
+    edge = edge_ref[...]
+    scale = scale_ref[...]
+    if len(items) == 1:
+        groups[...] = jnp.zeros(groups.shape, F32)
+    absorb(first_own, where_ref[1], per_owner, items, sums, groups, edge, scale, *scratch)
     base = [(groups[0, k] + groups[1, k]) + (groups[2, k] + groups[3, k]) for k in range(3)]
 
     column = iota((patches, patches), 1)
@@ -526,11 +549,6 @@
         return jnp.concatenate(
             [jnp.where(low_lane, x[:count], x[count:]) for x in (first, second)], 1
         )
-
-    def product(x, y):
-        x_high, x_low = halves(x)
-        y_high, y_low = halves(y)
-        return nn(x_high, y_high) + (nn(x_low, y_high) + nn(x_high, y_low))
 
     every = facing(adj_ref[...])
     halo0 = halo(every, base[0])
@@ -542,10 +560,9 @@
     halo2 = halo(facing(adj_ref[pl.ds(first_own, per_owner), :]), edges2)
     halo_all[0] = halo1
     halo_all[1] = halo0
-    scale = scale_ref[...]
     for k in range(3):
         mine = halo2 if k == 0 else halo_all[k - 1, pl.ds(first_own, per_owner), :]
-        factor = SMOOTHING * jnp.concatenate([scale[2 * k : 2 * k + 1]] * 2, 1)
+        factor = SMOOTHING * scale[2 * k : 2 * k + 1]
         for side in range(2):
             halo_rows[pl.ds(2 * k + side, per_owner, stride=8), :] = (
                 mine[:, side * LANES : (side + 1) * LANES] * factor
@@ -555,11 +572,7 @@
         halo_rows[pl.ds(r, per_owner, stride=8), :] = zero
 
     pairs = per_owner // 2
-    edge = edge_ref[...]
-    blank = jnp.zeros((8, CTRL), F32)
-    both = jnp.concatenate(
-        [jnp.concatenate([edge, blank], 1), jnp.concatenate([blank, edge], 1)], 0
-    )
+    both = pair_rows(edge)
     low8 = iota((8, LANES), 1) < CTRL
     along_rows, along_cols = [], []
     for pair in range(pairs):
@@ -568,11 +581,14 @@
         along_rows.append(jnp.where(low8, a, pltpu.roll(b, CTRL, 1)))
         along_cols.append(jnp.concatenate([a[:, CTRL:], b[:, CTRL:]], 0))
     from_rows = tn_product(edge, jnp.concatenate(along_rows, 1))
+    low_half = iota((CTRL, LANES), 1) < CTRL
     basis_both = pair_ref[...]
     turned = []
     for pair in range(pairs):
-        rows = slice(pair * CTRL, (pair + 1) * CTRL)
-        spectral = (sums[0, rows, :] + sums[1, rows, :]) * series_ref[...]
+        a, b = [slice(patch * CTRL, (patch + 1) * CTRL) for patch in (2 * pair, 2 * pair + 1)]
+        left = sums[0, a, :] + pltpu.roll(sums[1, a, :], CTRL, 1)
+        right = pltpu.roll(sums[0, b, :], CTRL, 1) + sums[1, b, :]
+        spectral = jnp.where(low_half, left, right) * series_ref[...]
         spectral = spectral + from_rows[:, pair * LANES : (pair + 1) * LANES]
         turned.append(spectral + tn_product(along_cols[pair], both))
     turned = product(jnp.concatenate(turned, 0), basis_both)
@@ -589,24 +605,30 @@
     return tn(x_high, y_high) + (tn(x_low, y_high) + tn(x_high, y_low))
 
 
-def smooth(payloads, items, early, where, adjacency, per_owner, const):
+def smooth(payloads, items, where, adjacency, per_owner, const):
     patches = adjacency.shape[0]
+    total = sum(item[0] for item in items)
     return pl.pallas_call(
-        functools.partial(smooth_kernel, items, per_owner, bool(early)),
+        functools.partial(smooth_kernel, items, per_owner),
         out_shape=jax.ShapeDtypeStruct((per_owner, CTRL, CTRL), F32),
-        in_specs=[SMEM] + [WHOLE] * 7 + [VMEM] * (len(payloads) + len(early)),
+        in_specs=[SMEM] + [WHOLE] * 7 + [VMEM] * len(payloads),
         out_specs=VMEM,
         scratch_shapes=[
-            *[pltpu.VMEM(shape.shape, F32) for shape in sum_shapes(per_owner, patches)],
-            *absorb_scratch(items),
+            pltpu.VMEM((2, per_owner * CTRL, LANES), F32),
+            pltpu.VMEM((4, 3, patches, 4 * CTRL), F32),
             pltpu.VMEM((2, patches, 4 * CTRL), F32),
             pltpu.VMEM((per_owner * 8, LANES), F32),
+            pltpu.VMEM((total, LANES), jnp.int32),
+            pltpu.SMEM((total, LANES), jnp.int32),
+            pltpu.VMEM((total * GROUP * 8, LANES), F32),
+            pltpu.VMEM((total * GROUP, LANES), F32),
+            pltpu.SemaphoreType.DMA,
         ],
         compiler_params=params(32),
         name="smooth",
     )(
         where, adjacency, const["coupling"], const["basis"], const["basis_pair"], const["series"],
-        const["edge_rows"], const["scale_rows"], *payloads, *early,
+        const["edge_rows"], const["scale_rows"], *payloads,
     )
 
 
@@ -618,7 +640,7 @@
     if vol_count != 8 or dsg_count != 4:
         whole = lax.all_gather(payload, ("vol", "dsg"), axis=0, tiled=True)
         items = ((vol_count * dsg_count, 0, 0),)
-        return smooth([whole], items, (), where, adjacency, per_owner, const)
+        return smooth([whole], items, where, adjacency, per_owner, const)
 
     def over(axis, array, bit):
         count = vol_count if axis == "vol" else dsg_count
@@ -634,12 +656,11 @@
     beside_y = over("vol", here, 1)
     beside_x = over("dsg", here, 2)
     corner = [over("dsg", beside_y[:half], 2), over("vol", beside_x[half:], 1)]
-    first = [here, over("dsg", here, 1), beside_x, over("dsg", beside_x, 1)]
-    first += [beside_y, over("dsg", beside_y, 1)]
-    items = ((4, 0, 0), (4, 0, 0), (4, 0, 1), (4, 0, 1), (4, 1, 0), (4, 1, 0))
-    early = early_sums(first, items, where, per_owner, patches)
-    last = corner + [over("dsg", c, 1) for c in corner]
-    return smooth(last, ((2, 1, 1),) * 4, early, where, adjacency, per_owner, const)
+    arrays = [here, beside_x, beside_y]
+    arrays = [x for array in arrays for x in (array, over("dsg", array, 1))]
+    arrays += corner + [over("dsg", c, 1) for c in corner]
+    items = ((4, 0, 0), (4, 0, 0), (4, 0, 1), (4, 0, 1), (4, 1, 0), (4, 1, 0)) + ((2, 1, 1),) * 4
+    return smooth(arrays, items, where, adjacency, per_owner, const)
 
 
 def per_device(

time: 74.9 us -> 68.1 us (0.909)
  local copies, waits for them, and re-layouts: 5.51 us -> 0.92 us
  waiting for transfers between devices: 17.4 us -> 16.5 us
  blocking collectives: 10.9 us -> 10.1 us
    unnamed x37 -> x31, local copies, waits for them, and re-layouts: 5.37 us -> 0.88 us
    ppermute x9, waiting for transfers between devices: 12.3 us -> 9.52 us  [over(): return lax.ppermute(array, axis, [(i, i ^ bit) for i in range(count)])]
    ppermute x9, starting transfers between devices: 3.43 us -> 5.81 us  [over(): return lax.ppermute(array, axis, [(i, i ^ bit) for i in range(count)])]
    all_to_all x1, waiting for transfers between devices: 0.01 us -> 1.81 us  [per_device(): lax.all_to_all(request, 'vol', split_axis=0, concat_axis=0, tiled=True)]
    all_to_all x1, starting transfers between devices: 6.01 us -> 4.26 us  [per_device(): lax.all_to_all(answer, 'vol', split_axis=0, concat_axis=0, tiled=True)]
    pallas_call x1, Pallas kernels: 1.41 us -> 2.3 us  [pack_requests(): pl.pallas_call(functools.partial(pack_kernel, capacity), out_shape=(jax.S...]
    all_to_all x1, blocking collectives: 10.9 us -> 10.1 us  [gather_and_smooth(): lax.all_to_all(copies, 'vol', split_axis=0, concat_axis=0, tiled=True, ax...]
    pallas_call x2 -> x1, Pallas kernels: 9.15 us -> 8.32 us  [smooth(): pl.pallas_call(functools.partial(smooth_kernel, items, per_owner), out_sh...]
  transfers between devices with their start and end apart: 11 -> 11, of which waited for: 5 -> 6; matrix products, arithmetic and copies ran while one was open for 0% -> 0% of each run, Pallas kernels for 14% -> 9%
where the time goes in v2:
time: 68.1 us; the launch traced here: 67.7 us
  Pallas kernels  22 us (32%)
  starting transfers between devices  17.4 us (26%)
  waiting for transfers between devices  16.5 us (24%)
  blocking collectives  10.1 us (15%)
  local copies, waits for them, and re-layouts  0.92 us (1%)
  between operations  0.83 us (1%)
    all_to_all x1, blocking collectives, gather_and_smooth(): lax.all_to_all(copies, 'vol', split_axis=0, concat_axis=0, tiled=True, ax...  10.1 us
    ppermute x9, waiting for transfers between devices, over(): return lax.ppermute(array, axis, [(i, i ^ bit) for i in range(count)])  9.52 us
    pallas_call x1, Pallas kernels, smooth(): pl.pallas_call(functools.partial(smooth_kernel, items, per_owner), out_sh...  8.32 us
    all_to_all x1, starting transfers between devices, per_device(): lax.all_to_all(request, 'vol', split_axis=0, concat_axis=0, tiled=True)  7.29 us
    ppermute x9, starting transfers between devices, over(): return lax.ppermute(array, axis, [(i, i ^ bit) for i in range(count)])  5.81 us
    all_to_all x1, waiting for transfers between devices, per_device(): lax.all_to_all(answer, 'vol', split_axis=0, concat_axis=0, tiled=True)  5.12 us
    pallas_call x1, Pallas kernels, near_densities(): pl.pallas_call(near_kernel, out_shape=jax.ShapeDtypeStruct((1, count), F3...  4.98 us
    all_to_all x1, starting transfers between devices, per_device(): lax.all_to_all(answer, 'vol', split_axis=0, concat_axis=0, tiled=True)  4.26 us
  transfers between devices with their start and end apart: 11, of which 6 were waited for; matrix products, arithmetic and copies ran while one was open for 0% of the time, Pallas kernels for 9%

profile of v2, /device:TPU:0, one launch (start us, length us, event | category | flops | bytes accessed | tf_op | source)
XLA Modules:
  0.0 67.7 jit_solution(16372269978355227264)
XLA Ops:
  0.6 0.0 copy-start
  0.6 2.3 %pack_requests.1 = (f32[8,8,160]{2,1,0:T(8,128)}, s32[1,512]{1,0:T(1,128)}) custom-call(f32[8,512]{1,0:T(8,128)} %geom_ref.3, s32[1,512]{1,0:T(1,128)} %bitcast.15, s32[1,512]{1,0:T(1,128)} %bitcast.16), custom_call_target="tpu_custom_call" | custom-call | tf_op jit(solution)/shard_map/pack_requests/pallas_call | solution.py:155
  3.0 7.3 %all-to-all-start = ((f32[8,8,160]{2,1,0:T(8,128)}), f32[8,8,160]{2,1,0:T(8,128)S(1)}, u32[]{:S(2)}, u32[]{:S(2)}) async-start(f32[8,8,160]{2,1,0:T(8,128)} %get-tuple-element.8), calls=%async_computation | async-start | bytes 131072 | tf_op jit(solution)/shard_map/all_to_all | solution.py:677
  10.2 0.0 copy-start.4
  10.3 0.0 copy-start.11
  10.3 0.0 copy-start.13
  10.3 0.0 copy-start.2
  10.3 0.0 copy-start.3
  10.3 0.0 copy-start.5
  10.3 0.0 copy-start.12
  10.3 5.0 %near_densities.1.near_ref.dens_ref = f32[1,2048]{1,0:T(1,128)} custom-call(s32[2048]{0:T(1024)} %cell_in.1, f32[4096,128]{1,0:T(8,128)} %fields_in.3, f32[8,2048]{1,0:T(8,128)} %geom_ref.2), custom_call_target="tpu_custom_call" | custom-call | flops 40000000 | bytes 4000000 | tf_op jit(solution)/shard_map/near_densities/pallas_call | solution.py:254
  15.3 0.0 copy-start.1
  15.3 0.0 copy-start.6
  15.3 1.8 %all-to-all-done.request_in = f32[8,8,160]{2,1,0:T(8,128)S(1)} async-done(((f32[8,8,160]{2,1,0:T(8,128)}), f32[8,8,160]{2,1,0:T(8,128)S(1)}, u32[]{:S(2)}, u32[]{:S(2)}) %all-to-all-start) | async-done | bytes 40992 | tf_op jit(solution)/shard_map/all_to_all | solution.py:677
  17.2 0.0 copy-done
  17.2 0.0 copy-start.7
  17.2 0.7 %copy-done.7 = f32[1,2048]{1,0:T(1,128)S(1)} copy-done((f32[1,2048]{1,0:T(1,128)S(1)}, f32[1,2048]{1,0:T(1,128)}, u32[]{:S(2)}) %copy-start.7) | copy-done | bytes 8216
  17.9 0.0 copy-start.8
  17.9 0.0 copy-start.14
  17.9 0.0 copy-start.9
  17.9 0.0 copy-start.10
  17.9 3.5 %far_answers.1 = f32[8,1,160]{2,1,0:T(1,128)} custom-call(f32[8,8,160]{2,1,0:T(8,128)S(1)} %all-to-all-done.request_in, f32[4096,128]{1,0:T(8,128)S(1)} %copy-done, f32[1,2048]{1,0:T(1,128)S(1)} %copy-done.7), custom_call_target="tpu_custom_call" | custom-call | tf_op jit(solution)/shard_map/far_answers/pallas_call | solution.py:297
  21.4 4.3 %all-to-all-start.1 = ((f32[8,1,160]{2,1,0:T(1,128)}), f32[8,1,160]{2,1,0:T(1,128)S(1)}, u32[]{:S(2)}, u32[]{:S(2)}) async-start(f32[8,1,160]{2,1,0:T(1,128)} %far_answers.1), calls=%async_computation.1 | async-start | bytes 16384 | tf_op jit(solution)/shard_map/all_to_all | solution.py:680
  25.7 0.0 copy-done.4
  25.7 0.0 copy-done.11
  25.7 0.0 copy-done.13
  25.7 0.0 copy-done.8
  25.7 1.4 %near_grids.1 = (f32[256,64]{1,0:T(8,128)S(1)}, f32[8,128]{1,0:T(8,128)S(1)}) custom-call(f32[1,2048]{1,0:T(1,128)S(1)} %copy-done.8, f32[8,2048]{1,0:T(8,128)S(1)} %copy-done.4, s32[1,2048]{1,0:T(1,128)S(1)} %bitcast.14, s32[1,512]{1,0:T(1,128)S(1)} %bitcast.12), custom_call_target="tpu_custom_call" | custom-call | flops 80000000 | bytes 1000000 | tf_op jit(solution)/shard_map/near_grids/pallas_call | solution.py:360
  27.1 5.1 %all-to-all-done.1.reply_ref = f32[8,1,160]{2,1,0:T(1,128)S(1)} async-done(((f32[8,1,160]{2,1,0:T(1,128)}), f32[8,1,160]{2,1,0:T(1,128)S(1)}, u32[]{:S(2)}, u32[]{:S(2)}) %all-to-all-start.1) | async-done | bytes 5152 | tf_op jit(solution)/shard_map/all_to_all | solution.py:680
  32.2 0.0 copy-done.2
  32.2 0.0 copy-done.3
  32.2 0.0 copy-done.5
  32.2 0.0 copy-done.12
  32.2 1.6 %make_payload.1 = (f32[1,512]{1,0:T(1,128)}, f32[136,128]{1,0:T(8,128)S(1)}) custom-call(f32[8,1,160]{2,1,0:T(1,128)S(1)} %all-to-all-done.1.reply_ref, s32[1,512]{1,0:T(1,128)S(1)} %copy-done.12, f32[8,512]{1,0:T(8,128)S(1)} %copy-done.5, s32[1,512]{1,0:T(1,128)S(1)} %bitcast.13, f32[8,128]{1,0:T(8,128)S(1)} %get-tuple-element.10.slot_ref, ...), custom_call_target="tpu_custom_call" | custom-call | tf_op jit(solution)/shard_map/make_payload/pallas_call | solution.py:413
  33.8 10.1 %all_to_all.15 = f32[4,136,128]{2,1,0:T(8,128)S(1)} all-to-all(f32[4,136,128]{2,1,0:T(8,128)S(1)} %broadcast_in_dim.2), channel_id=1, replica_groups={{0,8,16,24},{4,12,20,28},{1,9,17,25},{5,13,21,29},{2,10,18,26},{6,14,22..., dimensions={0} | all-to-all | bytes 557056 | tf_op jit(solution)/shard_map/all_to_all | solution.py:650
  43.8 0.5 collective-permute-start.3
  44.4 1.5 %collective-permute-start.1 = (f32[544,128]{1,0:T(8,128)S(1)}, f32[544,128]{1,0:T(8,128)S(1)}, u32[]{:S(2)}, u32[]{:S(2)}) collective-permute-start(f32[544,128]{1,0:T(8,128)S(1)} %bitcast.9), channel_id=1, source_target_pairs={{0,2},{1,3},{2,0},{3,1},{4,6},{5,7},{6,4},{7,5},{8,10},{9,11},{10,... | collective-permute-start | bytes 835592 | tf_op jit(solution)/shard_map/ppermute | solution.py:647
  45.9 0.0 collective-permute-start
  45.9 4.8 %collective-permute-done.3.rest_4_ = f32[544,128]{1,0:T(8,128)S(1)} collective-permute-done((f32[544,128]{1,0:T(8,128)S(1)}, f32[544,128]{1,0:T(8,128)S(1)}, u32[]{:S(2)}, u32[]{:S(2)}) %collective-permute-start.3) | collective-permute-done | bytes 278560 | tf_op jit(solution)/shard_map/ppermute | solution.py:647
  50.7 2.2 %collective-permute-start.5 = (f32[272,128]{1,0:T(8,128)S(1)}, f32[272,128]{1,0:T(8,128)S(1)}, u32[]{:S(2)}, u32[]{:S(2)}) collective-permute-start(f32[272,128]{1,0:T(8,128)S(1)} %slice.8), channel_id=1, source_target_pairs={{0,2},{1,3},{2,0},{3,1},{4,6},{5,7},{6,4},{7,5},{8,10},{9,11},{10,... | collective-permute-start | bytes 417800 | tf_op jit(solution)/shard_map/ppermute | solution.py:647
  52.9 0.0 collective-permute-done.1.rest_2_
  52.9 1.1 %collective-permute-start.6 = (f32[272,128]{1,0:T(8,128)S(1)}, f32[272,128]{1,0:T(8,128)S(1)}, u32[]{:S(2)}, u32[]{:S(2)}) collective-permute-start(f32[272,128]{1,0:T(8,128)S(1)} %slice.9), channel_id=1, source_target_pairs={{0,4},{4,0},{8,12},{12,8},{16,20},{20,16},{24,28},{28,24},{1,5},{5... | collective-permute-start | bytes 417800 | tf_op jit(solution)/shard_map/ppermute | solution.py:647
  54.0 0.0 collective-permute-start.4
  54.0 0.5 collective-permute-start.2
  54.5 1.4 %collective-permute-done.5.rest_6_ = f32[272,128]{1,0:T(8,128)S(1)} collective-permute-done((f32[272,128]{1,0:T(8,128)S(1)}, f32[272,128]{1,0:T(8,128)S(1)}, u32[]{:S(2)}, u32[]{:S(2)}) %collective-permute-start.5) | collective-permute-done | bytes 139296 | tf_op jit(solution)/shard_map/ppermute | solution.py:647
  55.9 0.0 collective-permute-start.7
  55.9 2.1 %collective-permute-done.6.rest_7_ = f32[272,128]{1,0:T(8,128)S(1)} collective-permute-done((f32[272,128]{1,0:T(8,128)S(1)}, f32[272,128]{1,0:T(8,128)S(1)}, u32[]{:S(2)}, u32[]{:S(2)}) %collective-permute-start.6) | collective-permute-done | bytes 139296 | tf_op jit(solution)/shard_map/ppermute | solution.py:647
  58.0 0.0 collective-permute-start.8
  58.0 0.0 copy-done.14
  58.0 0.1 copy.17.adj_ref
  58.1 0.1 pad_add_fusion.where_ref
  58.2 0.0 collective-permute-done.rest_1_
  58.2 0.0 collective-permute-done.7.rest_8_
  58.2 1.2 %collective-permute-done.8.rest_9_ = f32[272,128]{1,0:T(8,128)S(1)} collective-permute-done((f32[272,128]{1,0:T(8,128)S(1)}, f32[272,128]{1,0:T(8,128)S(1)}, u32[]{:S(2)}, u32[]{:S(2)}) %collective-permute-start.8) | collective-permute-done | bytes 139296 | tf_op jit(solution)/shard_map/ppermute | solution.py:647
  59.4 0.0 collective-permute-done.4.rest_5_
  59.4 0.0 collective-permute-done.2.rest_3_
  59.4 0.0 copy-done.1
  59.4 0.0 copy-done.6
  59.4 0.0 copy-done.9
  59.4 0.0 copy-done.10
  59.4 8.3 %smooth.1 = f32[24,64,64]{2,1,0:T(8,128)} custom-call(s32[2]{0:T(128)S(1)} %pad_add_fusion.where_ref, s32[96,4]{1,0:T(8,128)S(1)} %copy.17.adj_ref, f32[256,512]{1,0:T(8,128)S(1)} %copy-done.1, f32[64,64]{1,0:T(8,128)S(1)} %copy-done.3, f32[128,128]{1,0:T(8,128)S(1)} %copy-done.2, f32[64,128]{1,0:T(8,128)S(1)} %copy-done.6, f32[8,64]{1,0:T(8,128)S(1)} %copy-done.10, ...), custom_call_target="tpu_custom_call" | custom-call | tf_op jit(solution)/shard_map/smooth/pallas_call | solution.py:611
  (3 shorter events, 0.0 us)
Async XLA Ops:
  0.6 16.5 %copy-start = (f32[4096,128]{1,0:T(8,128)S(1)}, f32[4096,128]{1,0:T(8,128)}, u32[]{:S(2)}) copy-start(f32[4096,128]{1,0:T(8,128)} %fields_in.3) | copy-start | bytes 6291460
  3.0 14.2 %all-to-all-start = ((f32[8,8,160]{2,1,0:T(8,128)}), f32[8,8,160]{2,1,0:T(8,128)S(1)}, u32[]{:S(2)}, u32[]{:S(2)}) async-start(f32[8,8,160]{2,1,0:T(8,128)} %get-tuple-element.8), calls=%async_computation | async-start | bytes 131072 | tf_op jit(solution)/shard_map/all_to_all | solution.py:677
  10.2 15.4 %copy-start.4 = (f32[8,2048]{1,0:T(8,128)S(1)}, f32[8,2048]{1,0:T(8,128)}, u32[]{:S(2)}) copy-start(f32[8,2048]{1,0:T(8,128)} %geom_ref.2) | copy-start | bytes 196612
  10.3 15.4 %copy-start.11 = (s32[512]{0:T(512)S(1)}, s32[512]{0:T(512)}, u32[]{:S(2)}) copy-start(s32[512]{0:T(512)} %param.19) | copy-start | bytes 6148
  10.3 15.4 %copy-start.13 = (s32[2048]{0:T(1024)S(1)}, s32[2048]{0:T(1024)}, u32[]{:S(2)}) copy-start(s32[2048]{0:T(1024)} %param.22) | copy-start | bytes 24580
  10.3 21.9 %copy-start.2 = (f32[128,128]{1,0:T(8,128)S(1)}, f32[128,128]{1,0:T(8,128)}, u32[]{:S(2)}) copy-start(f32[128,128]{1,0:T(8,128)} %constant.35.clone.pair_ref) | copy-start | bytes 196612
  10.3 21.9 %copy-start.3 = (f32[64,64]{1,0:T(8,128)S(1)}, f32[64,64]{1,0:T(8,128)}, u32[]{:S(2)}) copy-start(f32[64,64]{1,0:T(8,128)} %constant.34.clone.basis_ref) | copy-start | bytes 49156
  10.3 21.9 %copy-start.5 = (f32[8,512]{1,0:T(8,128)S(1)}, f32[8,512]{1,0:T(8,128)}, u32[]{:S(2)}) copy-start(f32[8,512]{1,0:T(8,128)} %geom_ref.3) | copy-start | bytes 49156
  10.3 21.9 %copy-start.12 = (s32[1,512]{1,0:T(1,128)S(1)}, s32[1,512]{1,0:T(1,128)}, u32[]{:S(2)}) copy-start(s32[1,512]{1,0:T(1,128)} %get-tuple-element.9.place_ref) | copy-start | bytes 6148
  15.3 44.1 %copy-start.1 = (f32[256,512]{1,0:T(8,128)S(1)}, f32[256,512]{1,0:T(8,128)}, u32[]{:S(2)}) copy-start(f32[256,512]{1,0:T(8,128)} %constant.39.clone.coupling_ref) | copy-start | bytes 1572868
  15.3 44.1 %copy-start.6 = (f32[64,128]{1,0:T(8,128)S(1)}, f32[64,128]{1,0:T(8,128)}, u32[]{:S(2)}) copy-start(f32[64,128]{1,0:T(8,128)} %constant.38.clone.series_ref) | copy-start | bytes 98308
  17.2 0.7 %copy-start.7 = (f32[1,2048]{1,0:T(1,128)S(1)}, f32[1,2048]{1,0:T(1,128)}, u32[]{:S(2)}) copy-start(f32[1,2048]{1,0:T(1,128)} %near_densities.1.near_ref.dens_ref) | copy-start | bytes 24580
  17.9 7.8 %copy-start.8 = (f32[1,2048]{1,0:T(1,128)S(1)}, f32[1,2048]{1,0:T(1,128)}, u32[]{:S(2)}) copy-start(f32[1,2048]{1,0:T(1,128)} %near_densities.1.near_ref.dens_ref) | copy-start | bytes 24580
  17.9 40.2 %copy-start.14 = (s32[96,4]{0,1:T(4,128)S(1)}, s32[96,4]{0,1:T(4,128)}, u32[]{:S(2)}) copy-start(s32[96,4]{0,1:T(4,128)} %param.23) | copy-start | bytes 4612
  17.9 41.6 %copy-start.9 = (f32[8,128]{1,0:T(8,128)S(1)}, f32[8,128]{1,0:T(8,128)}, u32[]{:S(2)}) copy-start(f32[8,128]{1,0:T(8,128)} %constant.37.clone.scale_ref) | copy-start | bytes 12292
  17.9 41.6 %copy-start.10 = (f32[8,64]{1,0:T(8,128)S(1)}, f32[8,64]{1,0:T(8,128)}, u32[]{:S(2)}) copy-start(f32[8,64]{1,0:T(8,128)} %constant.36.clone.edge_ref) | copy-start | bytes 6148
  21.4 10.8 %all-to-all-start.1 = ((f32[8,1,160]{2,1,0:T(1,128)}), f32[8,1,160]{2,1,0:T(1,128)S(1)}, u32[]{:S(2)}, u32[]{:S(2)}) async-start(f32[8,1,160]{2,1,0:T(1,128)} %far_answers.1), calls=%async_computation.1 | async-start | bytes 16384 | tf_op jit(solution)/shard_map/all_to_all | solution.py:680
  43.8 6.9 %collective-permute-start.3 = (f32[544,128]{1,0:T(8,128)S(1)}, f32[544,128]{1,0:T(8,128)S(1)}, u32[]{:S(2)}, u32[]{:S(2)}) collective-permute-start(f32[544,128]{1,0:T(8,128)S(1)} %bitcast.8), channel_id=1, source_target_pairs={{0,4},{4,0},{8,12},{12,8},{16,20},{20,16},{24,28},{28,24},{1,5},{5... | collective-permute-start | bytes 835592 | tf_op jit(solution)/shard_map/ppermute | solution.py:647
  44.4 8.5 %collective-permute-start.1 = (f32[544,128]{1,0:T(8,128)S(1)}, f32[544,128]{1,0:T(8,128)S(1)}, u32[]{:S(2)}, u32[]{:S(2)}) collective-permute-start(f32[544,128]{1,0:T(8,128)S(1)} %bitcast.9), channel_id=1, source_target_pairs={{0,2},{1,3},{2,0},{3,1},{4,6},{5,7},{6,4},{7,5},{8,10},{9,11},{10,... | collective-permute-start | bytes 835592 | tf_op jit(solution)/shard_map/ppermute | solution.py:647
  45.9 12.3 %collective-permute-start = (f32[544,128]{1,0:T(8,128)S(1)}, f32[544,128]{1,0:T(8,128)S(1)}, u32[]{:S(2)}, u32[]{:S(2)}) collective-permute-start(f32[544,128]{1,0:T(8,128)S(1)} %bitcast.10), channel_id=1, source_target_pairs={{0,1},{1,0},{2,3},{3,2},{4,5},{5,4},{6,7},{7,6},{8,9},{9,8},{10,11... | collective-permute-start | bytes 835592 | tf_op jit(solution)/shard_map/ppermute | solution.py:647
  50.7 5.2 %collective-permute-start.5 = (f32[272,128]{1,0:T(8,128)S(1)}, f32[272,128]{1,0:T(8,128)S(1)}, u32[]{:S(2)}, u32[]{:S(2)}) collective-permute-start(f32[272,128]{1,0:T(8,128)S(1)} %slice.8), channel_id=1, source_target_pairs={{0,2},{1,3},{2,0},{3,1},{4,6},{5,7},{6,4},{7,5},{8,10},{9,11},{10,... | collective-permute-start | bytes 417800 | tf_op jit(solution)/shard_map/ppermute | solution.py:647
  52.9 5.1 %collective-permute-start.6 = (f32[272,128]{1,0:T(8,128)S(1)}, f32[272,128]{1,0:T(8,128)S(1)}, u32[]{:S(2)}, u32[]{:S(2)}) collective-permute-start(f32[272,128]{1,0:T(8,128)S(1)} %slice.9), channel_id=1, source_target_pairs={{0,4},{4,0},{8,12},{12,8},{16,20},{20,16},{24,28},{28,24},{1,5},{5... | collective-permute-start | bytes 417800 | tf_op jit(solution)/shard_map/ppermute | solution.py:647
  54.0 5.4 %collective-permute-start.4 = (f32[544,128]{1,0:T(8,128)S(1)}, f32[544,128]{1,0:T(8,128)S(1)}, u32[]{:S(2)}, u32[]{:S(2)}) collective-permute-start(f32[544,128]{1,0:T(8,128)S(1)} %collective-permute-done.3.rest_4_), channel_id=1, source_target_pairs={{0,1},{1,0},{2,3},{3,2},{4,5},{5,4},{6,7},{7,6},{8,9},{9,8},{10,11... | collective-permute-start | bytes 835592 | tf_op jit(solution)/shard_map/ppermute | solution.py:647
  54.0 5.4 %collective-permute-start.2 = (f32[544,128]{1,0:T(8,128)S(1)}, f32[544,128]{1,0:T(8,128)S(1)}, u32[]{:S(2)}, u32[]{:S(2)}) collective-permute-start(f32[544,128]{1,0:T(8,128)S(1)} %collective-permute-done.1.rest_2_), channel_id=1, source_target_pairs={{0,1},{1,0},{2,3},{3,2},{4,5},{5,4},{6,7},{7,6},{8,9},{9,8},{10,11... | collective-permute-start | bytes 835592 | tf_op jit(solution)/shard_map/ppermute | solution.py:647
  55.9 2.3 %collective-permute-start.7 = (f32[272,128]{1,0:T(8,128)S(1)}, f32[272,128]{1,0:T(8,128)S(1)}, u32[]{:S(2)}, u32[]{:S(2)}) collective-permute-start(f32[272,128]{1,0:T(8,128)S(1)} %collective-permute-done.5.rest_6_), channel_id=1, source_target_pairs={{0,1},{1,0},{2,3},{3,2},{4,5},{5,4},{6,7},{7,6},{8,9},{9,8},{10,11... | collective-permute-start | bytes 417800 | tf_op jit(solution)/shard_map/ppermute | solution.py:647
  58.0 1.4 %collective-permute-start.8 = (f32[272,128]{1,0:T(8,128)S(1)}, f32[272,128]{1,0:T(8,128)S(1)}, u32[]{:S(2)}, u32[]{:S(2)}) collective-permute-start(f32[272,128]{1,0:T(8,128)S(1)} %collective-permute-done.6.rest_7_), channel_id=1, source_target_pairs={{0,1},{1,0},{2,3},{3,2},{4,5},{5,4},{6,7},{7,6},{8,9},{9,8},{10,11... | collective-permute-start | bytes 417800 | tf_op jit(solution)/shard_map/ppermute | solution.py:647

commit v3 on v2

--- a/solution.py
+++ b/solution.py
@@ -242,40 +242,41 @@
     lax.fori_loop(0, tiles, step, 0, unroll=4 if tiles % 4 == 0 else 2)
 
 
-def near_kernel(cell_in, fields_in, geom_in, out_ref, cell_ref, fields_ref, geom_ref, rows_ref, sem):
-    count = geom_in.shape[1]
-    fetch([(fields_in, fields_ref), (cell_in, cell_ref), (geom_in, geom_ref)], sem)
+def near_kernel(first, cell_in, fields_in, geom_in, out_ref, cell_ref, fields_ref, geom_ref, rows_ref, sem):
+    count = out_ref.shape[1]
+    part = pl.ds(first, count)
+    fetch([(cell_in.at[part], cell_ref), (geom_in.at[:, part], geom_ref), (fields_in, fields_ref)], sem)
     gather_rows(lambda p: cell_ref[p], fields_ref, rows_ref, count)
     densities(rows_ref, geom_ref, out_ref, count)
 
 
-def near_densities(near_cell, fields, near_geom):
-    count = near_geom.shape[1]
+def near_scratch(fields, count):
+    return [
+        pltpu.SMEM((count,), jnp.int32),
+        pltpu.VMEM(fields.shape, F32),
+        pltpu.VMEM((8, count), F32),
+        pltpu.VMEM((count, LANES), F32),
+        pltpu.SemaphoreType.DMA((3,)),
+    ]
+
+
+def near_densities(near_cell, fields, near_geom, count):
     return pl.pallas_call(
-        near_kernel,
+        functools.partial(near_kernel, 0),
         out_shape=jax.ShapeDtypeStruct((1, count), F32),
         in_specs=[HBM] * 3,
         out_specs=VMEM,
-        scratch_shapes=[
-            pltpu.SMEM((count,), jnp.int32),
-            pltpu.VMEM(fields.shape, F32),
-            pltpu.VMEM((8, count), F32),
-            pltpu.VMEM((count, LANES), F32),
-            pltpu.SemaphoreType.DMA((3,)),
-        ],
+        scratch_shapes=near_scratch(fields, count),
         compiler_params=params(60),
-        cost_estimate=pl.CostEstimate(flops=40_000_000, bytes_accessed=4_000_000, transcendentals=0),
+        cost_estimate=pl.CostEstimate(flops=20_000_000, bytes_accessed=4_000_000, transcendentals=0),
         name="near_densities",
     )(near_cell, fields, near_geom)
 
 
 def far_kernel(
-    request_in, fields_in, near_ref, out_ref, request_ref, fields_ref, query_ref, cell_v, cell_s, rows_ref, dens_ref,
-    sems, sem,
+    request_in, fields_ref, out_ref, request_ref, query_ref, cell_v, cell_s, rows_ref, dens_ref, sems, sem
 ):
     owners, _, capacity = request_in.shape
-    fields_copy = pltpu.make_async_copy(fields_in, fields_ref, sems.at[1])
-    fields_copy.start()
     fetch([(request_in, request_ref)], sems)
     count = owners * capacity
     for o in range(owners):
@@ -284,35 +285,33 @@
     copy = pltpu.make_async_copy(cell_v, cell_s, sem)
     copy.start()
     copy.wait()
-    fields_copy.wait()
     gather_rows(lambda p: cell_s[0, p], fields_ref, rows_ref, count)
     densities(rows_ref, query_ref, dens_ref, count)
     for o in range(owners):
         out_ref[o] = dens_ref[:, o * capacity : (o + 1) * capacity]
 
 
-def far_answers(requests, fields, near_dens):
+def far_answers(requests, fields):
     owners, _, capacity = requests.shape
     count = owners * capacity
     return pl.pallas_call(
         far_kernel,
         out_shape=jax.ShapeDtypeStruct((owners, 1, capacity), F32),
-        in_specs=[ANY, ANY, ANY],
+        in_specs=[ANY, VMEM],
         out_specs=VMEM,
         scratch_shapes=[
             pltpu.VMEM(requests.shape, F32),
-            pltpu.VMEM(fields.shape, F32),
             pltpu.VMEM((8, count), F32),
             pltpu.VMEM((1, count), jnp.int32),
             pltpu.SMEM((1, count), jnp.int32),
             pltpu.VMEM((count, LANES), F32),
             pltpu.VMEM((1, count), F32),
-            pltpu.SemaphoreType.DMA((2,)),
+            pltpu.SemaphoreType.DMA((1,)),
             pltpu.SemaphoreType.DMA,
         ],
         compiler_params=params(24),
         name="far_answers",
-    )(requests, fields, near_dens)
+    )(requests, fields)
 
 
 def spline_columns(param):
@@ -343,7 +342,24 @@
     return nt(high, right_high) + (nt(high, right_low) + nt(low, right_high))
 
 
-def near_grid_kernel(dens_ref, geom_ref, near_ref, far_ref, grid_ref, slot_ref):
+def near_grid_kernel(
+    dens_in, cell_in, fields_in, geom_in, near_in, far_in, grid_ref, slot_ref,
+    dens_ref, spline_ref, near_ref, far_ref, rest_ref, cell_ref, fields_ref, geom_ref, rows_ref, more, sem,
+):
+    count, done = near_in.shape[1], dens_in.shape[1]
+    others = [
+        (dens_in, dens_ref.at[:, pl.ds(0, done)]),
+        (geom_in, spline_ref),
+        (near_in, near_ref),
+        (far_in, far_ref),
+    ]
+    others = [pltpu.make_async_copy(a, b, more.at[i]) for i, (a, b) in enumerate(others)]
+    for copy in others:
+        copy.start()
+    near_kernel(done, cell_in, fields_in, geom_in, rest_ref, cell_ref, fields_ref, geom_ref, rows_ref, sem)
+    for copy in others:
+        copy.wait()
+    dens_ref[:, done:count] = rest_ref[...]
     near, far = near_ref[...].astype(F32), far_ref[...].astype(F32)
     slots = []
     last = jnp.full((1, 1), -1.0, F32)
@@ -353,22 +369,33 @@
         last = jnp.minimum(a, b)
         slots.append(last)
     slot_ref[...] = jnp.concatenate([jnp.broadcast_to(s, (1, LANES)) for s in slots + slots], 0)
-    grid_ref[...] = slot_grids(dens_ref[...], geom_ref[6:7, :], geom_ref[7:8, :], near, slots)
-
-
-def near_grids(dens, near_geom, near_patch, far_patch):
+    grid_ref[...] = slot_grids(dens_ref[...], spline_ref[6:7, :], spline_ref[7:8, :], near, slots)
+
+
+def near_grids(dens, near_cell, fields, near_geom, near_patch, far_patch):
+    count, done = near_geom.shape[1], dens.shape[1]
     return pl.pallas_call(
         near_grid_kernel,
         out_shape=(
             jax.ShapeDtypeStruct((GROUP * CTRL, CTRL), F32),
             jax.ShapeDtypeStruct((8, LANES), F32),
         ),
-        in_specs=[VMEM] + [WHOLE] * 3,
+        in_specs=[ANY] * 6,
         out_specs=(VMEM, VMEM),
+        scratch_shapes=[
+            pltpu.VMEM((1, count), F32),
+            pltpu.VMEM((8, count), F32),
+            pltpu.VMEM((1, count), jnp.int32),
+            pltpu.VMEM(far_patch.shape, jnp.int32),
+            pltpu.VMEM((1, count - done), F32),
+            *near_scratch(fields, count - done)[:-1],
+            pltpu.SemaphoreType.DMA((4,)),
+            pltpu.SemaphoreType.DMA((3,)),
+        ],
         compiler_params=params(24),
-        cost_estimate=pl.CostEstimate(flops=80_000_000, bytes_accessed=1_000_000, transcendentals=0),
+        cost_estimate=pl.CostEstimate(flops=100_000_000, bytes_accessed=4_000_000, transcendentals=0),
         name="near_grids",
-    )(dens, near_geom, near_patch, far_patch)
+    )(dens, near_cell, fields, near_geom, near_patch, far_patch)
 
 
 def payload_kernel(
@@ -433,13 +460,14 @@
 
 
 def absorb(first_own, y_at, per_owner, items, sums, groups, edge, scale, name_v, name_s, edges, where_to, name_sem):
-    patches = groups.shape[2]
+    patches = groups.shape[1]
     low8 = iota((8, LANES), 1) < CTRL
     at = 0
     for ref, parts, _, _ in items:
         for p in range(parts):
             last = (p + 1) * PAYLOAD_ROWS - 1
-            name_v[at : at + 1, :] = ref[last : last + 1, :].astype(jnp.int32)
+            patch = ref[last : last + 1, :].astype(jnp.int32) - first_own
+            name_v[at : at + 1, :] = jnp.where((patch >= 0) & (patch < per_owner), patch, -1)
             at += 1
     names = pltpu.make_async_copy(name_v, name_s, name_sem)
     names.start()
@@ -449,11 +477,9 @@
     edge_both = jnp.concatenate([edge_high, edge_low], 0)
     both_high, both_low = halves(pair_rows(edge))
     both_both = jnp.concatenate([both_high, both_low], 0)
-    for group in sorted({(dy, dx) for _, _, dy, dx in items}):
+    for dy in sorted({dy for _, _, dy, _ in items}):
         at = 0
-        chunks = [
-            (ref, p) for ref, parts, dy, dx in items if (dy, dx) == group for p in range(0, parts, 2)
-        ]
+        chunks = [(ref, p) for ref, parts, own, _ in items if own == dy for p in range(0, parts, 2)]
         for ref, start in chunks:
             blocks = []
             for p in (start, start + 1):
@@ -479,9 +505,8 @@
                 at += 1
         lane = iota((at, LANES), 1)
         place = jnp.where(lane == where_to[:at, :].astype(jnp.int32), 1.0, 0.0).T[:patches].astype(BF16)
-        for k in range(3):
-            rows = [edges[pl.ds(2 * k + side, at, stride=8), :] for side in range(2)]
-            groups[(group[0] ^ y_at) * 2 + group[1], k] = fold(nn(place, two(jnp.concatenate(rows, 1))))
+        rows = jnp.concatenate([edges[pl.ds(r, at, stride=8), :] for r in range(6)], 1)
+        groups[dy ^ y_at] = fold(nn(place, two(rows)))
 
     names.wait()
 
@@ -491,9 +516,9 @@
 
             def add_payload(p, carry, ref=ref, at=at):
                 for s in range(GROUP):
-                    patch = name_s[at + p, s] - first_own
-
-                    @pl.when((patch >= 0) & (patch < per_owner))
+                    patch = name_s[at + p, s]
+
+                    @pl.when(patch >= 0)
                     def _():
                         row = pl.multiple_of(p * PAYLOAD_ROWS + (s // 2) * CTRL, 8)
                         own = pl.multiple_of(patch * CTRL, CTRL)
@@ -529,7 +554,8 @@
     if len(items) == 1:
         groups[...] = jnp.zeros(groups.shape, F32)
     absorb(first_own, where_ref[1], per_owner, items, sums, groups, edge, scale, *scratch)
-    base = [(groups[0, k] + groups[1, k]) + (groups[2, k] + groups[3, k]) for k in range(3)]
+    base = groups[0] + groups[1]
+    base = [base[:, 4 * CTRL * k : 4 * CTRL * (k + 1)] for k in range(3)]
 
     column = iota((patches, patches), 1)
     wide = 4 * CTRL
@@ -579,10 +605,14 @@
         a = halo_rows[16 * pair : 16 * pair + 8, :]
         b = halo_rows[16 * pair + 8 : 16 * pair + 16, :]
         along_rows.append(jnp.where(low8, a, pltpu.roll(b, CTRL, 1)))
-        along_cols.append(jnp.concatenate([a[:, CTRL:], b[:, CTRL:]], 0))
+        low, high = (pltpu.roll(x, CTRL, 1) for x in (a, b)) if pair % 2 == 0 else (a, b)
+        along_cols.append(jnp.concatenate([low, high], 0))
     from_rows = tn_product(edge, jnp.concatenate(along_rows, 1))
     low_half = iota((CTRL, LANES), 1) < CTRL
     basis_both = pair_ref[...]
+    low16 = iota((16, LANES), 1) < CTRL
+    along_cols = [jnp.where(low16, x, y) for x, y in zip(along_cols[::2], along_cols[1::2])]
+    from_cols = tn_product(jnp.concatenate(along_cols, 1), both)
     turned = []
     for pair in range(pairs):
         a, b = [slice(patch * CTRL, (patch + 1) * CTRL) for patch in (2 * pair, 2 * pair + 1)]
@@ -590,7 +620,7 @@
         right = pltpu.roll(sums[0, b, :], CTRL, 1) + sums[1, b, :]
         spectral = jnp.where(low_half, left, right) * series_ref[...]
         spectral = spectral + from_rows[:, pair * LANES : (pair + 1) * LANES]
-        turned.append(spectral + tn_product(along_cols[pair], both))
+        turned.append(spectral + from_cols[pair * CTRL : (pair + 1) * CTRL, :])
     turned = product(jnp.concatenate(turned, 0), basis_both)
     flat = jnp.concatenate([turned[pair * CTRL : (pair + 1) * CTRL] for pair in range(pairs)], 1)
     done = product(basis_ref[...], flat)
@@ -615,7 +645,7 @@
         out_specs=VMEM,
         scratch_shapes=[
             pltpu.VMEM((2, per_owner * CTRL, LANES), F32),
-            pltpu.VMEM((4, 3, patches, 4 * CTRL), F32),
+            pltpu.VMEM((2, patches, 12 * CTRL), F32),
             pltpu.VMEM((2, patches, 4 * CTRL), F32),
             pltpu.VMEM((per_owner * 8, LANES), F32),
             pltpu.VMEM((total, LANES), jnp.int32),
@@ -675,11 +705,12 @@
         far_geom, far_block.reshape(1, -1), far_cell.reshape(1, -1), vol_count, capacity
     )
     asked = lax.all_to_all(request, "vol", split_axis=0, concat_axis=0, tiled=True)
-    near_dens = near_densities(near_cell, fields, near_geom)
-    answer = far_answers(asked, fields, near_dens)
+    near_dens = near_densities(near_cell, fields, near_geom, near_cell.shape[0] // 2)
+    asked, near_dens = lax.optimization_barrier((asked, near_dens))
+    answer = far_answers(asked, fields)
     reply = lax.all_to_all(answer, "vol", split_axis=0, concat_axis=0, tiled=True)
     near_patch, far_patch = near_patch.reshape(1, -1), far_patch.reshape(1, -1)
-    near_grid, slots = near_grids(near_dens, near_geom, near_patch, far_patch)
+    near_grid, slots = near_grids(near_dens, near_cell, fields, near_geom, near_patch, far_patch)
     far_dens, payload = make_payload(reply, place, far_geom, far_patch, slots, near_grid, const)
 
     design = gather_and_smooth(payload, adjacency, vol_count, dsg_count, const)

time: 68.1 us -> 65.7 us (0.965)
  starting transfers between devices: 17.4 us -> 16.4 us
  waiting for transfers between devices: 16.5 us -> 15.8 us
    all_to_all x1, waiting for transfers between devices: 5.12 us -> 2.91 us  [per_device(): lax.all_to_all(answer, 'vol', split_axis=0, concat_axis=0, tiled=True)]
    pallas_call x1, Pallas kernels: 1.35 us -> 3.48 us  [near_grids(): pl.pallas_call(near_grid_kernel, out_shape=(jax.ShapeDtypeStruct((GROUP *...]
    all_to_all x1, waiting for transfers between devices: 1.81 us -> 3.2 us  [per_device(): lax.all_to_all(request, 'vol', split_axis=0, concat_axis=0, tiled=True)]
    pallas_call x1, Pallas kernels: 4.98 us -> 3.6 us  [near_densities(): pl.pallas_call(functools.partial(near_kernel, 0), out_shape=jax.ShapeDtyp...]
    all_to_all x1, starting transfers between devices: 4.26 us -> 3.48 us  [per_device(): lax.all_to_all(answer, 'vol', split_axis=0, concat_axis=0, tiled=True)]
    pallas_call x1, Pallas kernels: 8.32 us -> 7.58 us  [smooth(): pl.pallas_call(functools.partial(smooth_kernel, items, per_owner), out_sh...]
    unnamed x31, local copies, waits for them, and re-layouts: 0.88 us -> 0.2 us
  transfers between devices with their start and end apart: 11 -> 11, of which waited for: 6 -> 7; matrix products, arithmetic and copies ran while one was open for 0% -> 0% of each run, Pallas kernels for 9% -> 11%
where the time goes in v3:
time: 65.7 us; the launch traced here: 65.4 us
  Pallas kernels  21.9 us (33%)
  starting transfers between devices  16.4 us (25%)
  waiting for transfers between devices  15.8 us (24%)
  blocking collectives  10.1 us (15%)
  between operations  0.89 us (1%)
    all_to_all x1, blocking collectives, gather_and_smooth(): lax.all_to_all(copies, 'vol', split_axis=0, concat_axis=0, tiled=True, ax...  10.1 us
    ppermute x9, waiting for transfers between devices, over(): return lax.ppermute(array, axis, [(i, i ^ bit) for i in range(count)])  9.72 us
    pallas_call x1, Pallas kernels, smooth(): pl.pallas_call(functools.partial(smooth_kernel, items, per_owner), out_sh...  7.58 us
    all_to_all x1, starting transfers between devices, per_device(): lax.all_to_all(request, 'vol', split_axis=0, concat_axis=0, tiled=True)  7.29 us
    ppermute x9, starting transfers between devices, over(): return lax.ppermute(array, axis, [(i, i ^ bit) for i in range(count)])  5.65 us
    pallas_call x1, Pallas kernels, near_densities(): pl.pallas_call(functools.partial(near_kernel, 0), out_shape=jax.ShapeDtyp...  3.6 us
    pallas_call x1, Pallas kernels, near_grids(): pl.pallas_call(near_grid_kernel, out_shape=(jax.ShapeDtypeStruct((GROUP *...  3.48 us
    all_to_all x1, starting transfers between devices, per_device(): lax.all_to_all(answer, 'vol', split_axis=0, concat_axis=0, tiled=True)  3.48 us
  transfers between devices with their start and end apart: 11, of which 7 were waited for; matrix products, arithmetic and copies ran while one was open for 0% of the time, Pallas kernels for 11%

profile of v3, /device:TPU:0, one launch (start us, length us, event | category | flops | bytes accessed | tf_op | source)
XLA Modules:
  0.0 65.4 jit_solution(9805442262326561179)
XLA Ops:
  0.6 0.0 copy-start
  0.6 2.3 %pack_requests.1 = (f32[8,8,160]{2,1,0:T(8,128)}, s32[1,512]{1,0:T(1,128)}) custom-call(f32[8,512]{1,0:T(8,128)} %geom_ref.1, s32[1,512]{1,0:T(1,128)} %bitcast.15, s32[1,512]{1,0:T(1,128)} %bitcast.16), custom_call_target="tpu_custom_call" | custom-call | tf_op jit(solution)/shard_map/pack_requests/pallas_call | solution.py:155
  3.0 7.3 %all-to-all-start = ((f32[8,8,160]{2,1,0:T(8,128)}), f32[8,8,160]{2,1,0:T(8,128)S(1)}, u32[]{:S(2)}, u32[]{:S(2)}) async-start(f32[8,8,160]{2,1,0:T(8,128)} %get-tuple-element.10), calls=%async_computation | async-start | bytes 131072 | tf_op jit(solution)/shard_map/all_to_all | solution.py:707
  10.2 0.0 copy-start.3
  10.3 0.0 copy-start.7
  10.3 0.0 copy-start.9
  10.3 0.0 copy-start.10
  10.3 3.6 %near_densities.1.dens_in = f32[1,1024]{1,0:T(1,128)} custom-call(s32[2048]{0:T(1024)} %cell_in.3, f32[4096,128]{1,0:T(8,128)} %fields_in.3, f32[8,2048]{1,0:T(8,128)} %geom_in.5), custom_call_target="tpu_custom_call" | custom-call | flops 20000000 | bytes 4000000 | tf_op jit(solution)/shard_map/near_densities/pallas_call | solution.py:264
  13.9 0.0 copy-start.8
  13.9 0.0 copy-start.2
  13.9 0.0 copy-start.4
  13.9 0.0 copy-start.5
  13.9 0.0 copy-start.13
  14.0 3.2 %all-to-all-done.request_in = f32[8,8,160]{2,1,0:T(8,128)S(1)} async-done(((f32[8,8,160]{2,1,0:T(8,128)}), f32[8,8,160]{2,1,0:T(8,128)S(1)}, u32[]{:S(2)}, u32[]{:S(2)}) %all-to-all-start) | async-done | bytes 40992 | tf_op jit(solution)/shard_map/all_to_all | solution.py:707
  17.2 0.0 copy-done
  17.2 3.4 %far_answers.1 = f32[8,1,160]{2,1,0:T(1,128)} custom-call(f32[8,8,160]{2,1,0:T(8,128)S(1)} %all-to-all-done.request_in, f32[4096,128]{1,0:T(8,128)S(1)} %copy-done), custom_call_target="tpu_custom_call" | custom-call | tf_op jit(solution)/shard_map/far_answers/pallas_call | solution.py:297
  20.5 0.0 copy-start.14
  20.5 0.0 copy-start.1
  20.5 0.0 copy-start.6
  20.6 0.0 copy-start.11
  20.6 0.0 copy-start.12
  20.6 3.5 %all-to-all-start.1 = ((f32[8,1,160]{2,1,0:T(1,128)}), f32[8,1,160]{2,1,0:T(1,128)S(1)}, u32[]{:S(2)}, u32[]{:S(2)}) async-start(f32[8,1,160]{2,1,0:T(1,128)} %far_answers.1), calls=%async_computation.1 | async-start | bytes 16384 | tf_op jit(solution)/shard_map/all_to_all | solution.py:711
  24.1 0.0 copy-done.3
  24.1 0.0 copy-done.7
  24.1 0.0 copy-done.9
  24.1 0.0 copy-done.10
  24.1 0.0 copy-done.8
  24.1 3.5 %near_grids.1 = (f32[256,64]{1,0:T(8,128)S(1)}, f32[8,128]{1,0:T(8,128)S(1)}) custom-call(f32[1,1024]{1,0:T(1,128)S(1)} %copy-done.8, s32[2048]{0:T(1024)S(1)} %copy-done.7, f32[4096,128]{1,0:T(8,128)S(1)} %copy-done, f32[8,2048]{1,0:T(8,128)S(1)} %copy-done.3, s32[1,2048]{1,0:T(1,128)S(1)} %bitcast.12, s32[1,512]{1,0:T(1,128)S(1)} %bitcast.13), custom_call_target="tpu_custom_call" | custom-call | flops 100000000 | bytes 4000000 | tf_op jit(solution)/shard_map/near_grids/pallas_call | solution.py:377
  27.6 2.9 %all-to-all-done.1.reply_ref = f32[8,1,160]{2,1,0:T(1,128)S(1)} async-done(((f32[8,1,160]{2,1,0:T(1,128)}), f32[8,1,160]{2,1,0:T(1,128)S(1)}, u32[]{:S(2)}, u32[]{:S(2)}) %all-to-all-start.1) | async-done | bytes 5152 | tf_op jit(solution)/shard_map/all_to_all | solution.py:711
  30.5 0.0 copy-done.2
  30.5 0.0 copy-done.4
  30.5 0.0 copy-done.5
  30.5 0.0 copy-done.13
  30.5 1.6 %make_payload.1 = (f32[1,512]{1,0:T(1,128)}, f32[136,128]{1,0:T(8,128)S(1)}) custom-call(f32[8,1,160]{2,1,0:T(1,128)S(1)} %all-to-all-done.1.reply_ref, s32[1,512]{1,0:T(1,128)S(1)} %copy-done.13, f32[8,512]{1,0:T(8,128)S(1)} %copy-done.5, s32[1,512]{1,0:T(1,128)S(1)} %bitcast.14, f32[8,128]{1,0:T(8,128)S(1)} %get-tuple-element.14.slot_ref, ...), custom_call_target="tpu_custom_call" | custom-call | tf_op jit(solution)/shard_map/make_payload/pallas_call | solution.py:440
  32.1 10.1 %all_to_all.15 = f32[4,136,128]{2,1,0:T(8,128)S(1)} all-to-all(f32[4,136,128]{2,1,0:T(8,128)S(1)} %broadcast_in_dim.2), channel_id=1, replica_groups={{0,8,16,24},{4,12,20,28},{1,9,17,25},{5,13,21,29},{2,10,18,26},{6,14,22..., dimensions={0} | all-to-all | bytes 557056 | tf_op jit(solution)/shard_map/all_to_all | solution.py:680
  42.2 1.0 %collective-permute-start.3 = (f32[544,128]{1,0:T(8,128)S(1)}, f32[544,128]{1,0:T(8,128)S(1)}, u32[]{:S(2)}, u32[]{:S(2)}) collective-permute-start(f32[544,128]{1,0:T(8,128)S(1)} %bitcast.8), channel_id=1, source_target_pairs={{0,4},{4,0},{8,12},{12,8},{16,20},{20,16},{24,28},{28,24},{1,5},{5... | collective-permute-start | bytes 835592 | tf_op jit(solution)/shard_map/ppermute | solution.py:677
  43.2 1.5 %collective-permute-start.1 = (f32[544,128]{1,0:T(8,128)S(1)}, f32[544,128]{1,0:T(8,128)S(1)}, u32[]{:S(2)}, u32[]{:S(2)}) collective-permute-start(f32[544,128]{1,0:T(8,128)S(1)} %bitcast.9), channel_id=1, source_target_pairs={{0,2},{1,3},{2,0},{3,1},{4,6},{5,7},{6,4},{7,5},{8,10},{9,11},{10,... | collective-permute-start | bytes 835592 | tf_op jit(solution)/shard_map/ppermute | solution.py:677
  44.7 0.0 collective-permute-start
  44.7 4.4 %collective-permute-done.3.rest_4_ = f32[544,128]{1,0:T(8,128)S(1)} collective-permute-done((f32[544,128]{1,0:T(8,128)S(1)}, f32[544,128]{1,0:T(8,128)S(1)}, u32[]{:S(2)}, u32[]{:S(2)}) %collective-permute-start.3) | collective-permute-done | bytes 278560 | tf_op jit(solution)/shard_map/ppermute | solution.py:677
  49.2 1.6 %collective-permute-start.5 = (f32[272,128]{1,0:T(8,128)S(1)}, f32[272,128]{1,0:T(8,128)S(1)}, u32[]{:S(2)}, u32[]{:S(2)}) collective-permute-start(f32[272,128]{1,0:T(8,128)S(1)} %slice.8), channel_id=1, source_target_pairs={{0,2},{1,3},{2,0},{3,1},{4,6},{5,7},{6,4},{7,5},{8,10},{9,11},{10,... | collective-permute-start | bytes 417800 | tf_op jit(solution)/shard_map/ppermute | solution.py:677
  50.7 0.6 collective-permute-done.1.rest_2_
  51.3 1.0 %collective-permute-start.6 = (f32[272,128]{1,0:T(8,128)S(1)}, f32[272,128]{1,0:T(8,128)S(1)}, u32[]{:S(2)}, u32[]{:S(2)}) collective-permute-start(f32[272,128]{1,0:T(8,128)S(1)} %slice.9), channel_id=1, source_target_pairs={{0,4},{4,0},{8,12},{12,8},{16,20},{20,16},{24,28},{28,24},{1,5},{5... | collective-permute-start | bytes 417800 | tf_op jit(solution)/shard_map/ppermute | solution.py:677
  52.3 0.0 collective-permute-start.4
  52.3 0.5 collective-permute-start.2
  52.8 1.4 %collective-permute-done.5.rest_6_ = f32[272,128]{1,0:T(8,128)S(1)} collective-permute-done((f32[272,128]{1,0:T(8,128)S(1)}, f32[272,128]{1,0:T(8,128)S(1)}, u32[]{:S(2)}, u32[]{:S(2)}) %collective-permute-start.5) | collective-permute-done | bytes 139296 | tf_op jit(solution)/shard_map/ppermute | solution.py:677
  54.3 0.0 collective-permute-start.7
  54.3 2.1 %collective-permute-done.6.rest_7_ = f32[272,128]{1,0:T(8,128)S(1)} collective-permute-done((f32[272,128]{1,0:T(8,128)S(1)}, f32[272,128]{1,0:T(8,128)S(1)}, u32[]{:S(2)}, u32[]{:S(2)}) %collective-permute-start.6) | collective-permute-done | bytes 139296 | tf_op jit(solution)/shard_map/ppermute | solution.py:677
  56.4 0.0 collective-permute-start.8
  56.4 0.0 copy-done.14
  56.4 0.1 copy.17.adj_ref
  56.5 0.1 pad_add_fusion.where_ref
  56.6 0.0 collective-permute-done.rest_1_
  56.6 0.0 collective-permute-done.7.rest_8_
  56.6 1.2 %collective-permute-done.8.rest_9_ = f32[272,128]{1,0:T(8,128)S(1)} collective-permute-done((f32[272,128]{1,0:T(8,128)S(1)}, f32[272,128]{1,0:T(8,128)S(1)}, u32[]{:S(2)}, u32[]{:S(2)}) %collective-permute-start.8) | collective-permute-done | bytes 139296 | tf_op jit(solution)/shard_map/ppermute | solution.py:677
  57.8 0.0 collective-permute-done.4.rest_5_
  57.8 0.0 collective-permute-done.2.rest_3_
  57.8 0.0 copy-done.1
  57.8 0.0 copy-done.6
  57.8 0.0 copy-done.11
  57.8 0.0 copy-done.12
  57.8 7.6 %smooth.1 = f32[24,64,64]{2,1,0:T(8,128)} custom-call(s32[2]{0:T(128)S(1)} %pad_add_fusion.where_ref, s32[96,4]{1,0:T(8,128)S(1)} %copy.17.adj_ref, f32[256,512]{1,0:T(8,128)S(1)} %copy-done.1, f32[64,64]{1,0:T(8,128)S(1)} %copy-done.4, f32[128,128]{1,0:T(8,128)S(1)} %copy-done.2, f32[64,128]{1,0:T(8,128)S(1)} %copy-done.6, f32[8,64]{1,0:T(8,128)S(1)} %copy-done.12, ...), custom_call_target="tpu_custom_call" | custom-call | tf_op jit(solution)/shard_map/smooth/pallas_call | solution.py:641
  (3 shorter events, 0.0 us)
Async XLA Ops:
  0.6 16.5 %copy-start = (f32[4096,128]{1,0:T(8,128)S(1)}, f32[4096,128]{1,0:T(8,128)}, u32[]{:S(2)}) copy-start(f32[4096,128]{1,0:T(8,128)} %fields_in.3) | copy-start | bytes 6291460
  3.0 14.2 %all-to-all-start = ((f32[8,8,160]{2,1,0:T(8,128)}), f32[8,8,160]{2,1,0:T(8,128)S(1)}, u32[]{:S(2)}, u32[]{:S(2)}) async-start(f32[8,8,160]{2,1,0:T(8,128)} %get-tuple-element.10), calls=%async_computation | async-start | bytes 131072 | tf_op jit(solution)/shard_map/all_to_all | solution.py:707
  10.2 13.8 %copy-start.3 = (f32[8,2048]{1,0:T(8,128)S(1)}, f32[8,2048]{1,0:T(8,128)}, u32[]{:S(2)}) copy-start(f32[8,2048]{1,0:T(8,128)} %geom_in.5) | copy-start | bytes 196612
  10.3 13.8 %copy-start.7 = (s32[2048]{0:T(1024)S(1)}, s32[2048]{0:T(1024)}, u32[]{:S(2)}) copy-start(s32[2048]{0:T(1024)} %cell_in.3) | copy-start | bytes 24580
  10.3 13.8 %copy-start.9 = (s32[2048]{0:T(1024)S(1)}, s32[2048]{0:T(1024)}, u32[]{:S(2)}) copy-start(s32[2048]{0:T(1024)} %param.22) | copy-start | bytes 24580
  10.3 13.8 %copy-start.10 = (s32[512]{0:T(512)S(1)}, s32[512]{0:T(512)}, u32[]{:S(2)}) copy-start(s32[512]{0:T(512)} %param.19) | copy-start | bytes 6148
  13.9 10.2 %copy-start.8 = (f32[1,1024]{1,0:T(1,128)S(1)}, f32[1,1024]{1,0:T(1,128)}, u32[]{:S(2)}) copy-start(f32[1,1024]{1,0:T(1,128)} %near_densities.1.dens_in) | copy-start | bytes 12292
  13.9 16.6 %copy-start.2 = (f32[128,128]{1,0:T(8,128)S(1)}, f32[128,128]{1,0:T(8,128)}, u32[]{:S(2)}) copy-start(f32[128,128]{1,0:T(8,128)} %constant.35.clone.pair_ref) | copy-start | bytes 196612
  13.9 16.6 %copy-start.4 = (f32[64,64]{1,0:T(8,128)S(1)}, f32[64,64]{1,0:T(8,128)}, u32[]{:S(2)}) copy-start(f32[64,64]{1,0:T(8,128)} %constant.34.clone.basis_ref) | copy-start | bytes 49156
  13.9 16.6 %copy-start.5 = (f32[8,512]{1,0:T(8,128)S(1)}, f32[8,512]{1,0:T(8,128)}, u32[]{:S(2)}) copy-start(f32[8,512]{1,0:T(8,128)} %geom_ref.1) | copy-start | bytes 49156
  13.9 16.6 %copy-start.13 = (s32[1,512]{1,0:T(1,128)S(1)}, s32[1,512]{1,0:T(1,128)}, u32[]{:S(2)}) copy-start(s32[1,512]{1,0:T(1,128)} %get-tuple-element.12.place_ref) | copy-start | bytes 6148
  20.5 35.9 %copy-start.14 = (s32[96,4]{0,1:T(4,128)S(1)}, s32[96,4]{0,1:T(4,128)}, u32[]{:S(2)}) copy-start(s32[96,4]{0,1:T(4,128)} %param.23) | copy-start | bytes 4612
  20.5 37.3 %copy-start.1 = (f32[256,512]{1,0:T(8,128)S(1)}, f32[256,512]{1,0:T(8,128)}, u32[]{:S(2)}) copy-start(f32[256,512]{1,0:T(8,128)} %constant.39.clone.coupling_ref) | copy-start | bytes 1572868
  20.5 37.3 %copy-start.6 = (f32[64,128]{1,0:T(8,128)S(1)}, f32[64,128]{1,0:T(8,128)}, u32[]{:S(2)}) copy-start(f32[64,128]{1,0:T(8,128)} %constant.38.clone.series_ref) | copy-start | bytes 98308
  20.6 37.2 %copy-start.11 = (f32[8,128]{1,0:T(8,128)S(1)}, f32[8,128]{1,0:T(8,128)}, u32[]{:S(2)}) copy-start(f32[8,128]{1,0:T(8,128)} %constant.37.clone.scale_ref) | copy-start | bytes 12292
  20.6 37.2 %copy-start.12 = (f32[8,64]{1,0:T(8,128)S(1)}, f32[8,64]{1,0:T(8,128)}, u32[]{:S(2)}) copy-start(f32[8,64]{1,0:T(8,128)} %constant.36.clone.edge_ref) | copy-start | bytes 6148
  20.6 9.9 %all-to-all-start.1 = ((f32[8,1,160]{2,1,0:T(1,128)}), f32[8,1,160]{2,1,0:T(1,128)S(1)}, u32[]{:S(2)}, u32[]{:S(2)}) async-start(f32[8,1,160]{2,1,0:T(1,128)} %far_answers.1), calls=%async_computation.1 | async-start | bytes 16384 | tf_op jit(solution)/shard_map/all_to_all | solution.py:711
  42.2 7.0 %collective-permute-start.3 = (f32[544,128]{1,0:T(8,128)S(1)}, f32[544,128]{1,0:T(8,128)S(1)}, u32[]{:S(2)}, u32[]{:S(2)}) collective-permute-start(f32[544,128]{1,0:T(8,128)S(1)} %bitcast.8), channel_id=1, source_target_pairs={{0,4},{4,0},{8,12},{12,8},{16,20},{20,16},{24,28},{28,24},{1,5},{5... | collective-permute-start | bytes 835592 | tf_op jit(solution)/shard_map/ppermute | solution.py:677
  43.2 8.0 %collective-permute-start.1 = (f32[544,128]{1,0:T(8,128)S(1)}, f32[544,128]{1,0:T(8,128)S(1)}, u32[]{:S(2)}, u32[]{:S(2)}) collective-permute-start(f32[544,128]{1,0:T(8,128)S(1)} %bitcast.9), channel_id=1, source_target_pairs={{0,2},{1,3},{2,0},{3,1},{4,6},{5,7},{6,4},{7,5},{8,10},{9,11},{10,... | collective-permute-start | bytes 835592 | tf_op jit(solution)/shard_map/ppermute | solution.py:677
  44.7 11.9 %collective-permute-start = (f32[544,128]{1,0:T(8,128)S(1)}, f32[544,128]{1,0:T(8,128)S(1)}, u32[]{:S(2)}, u32[]{:S(2)}) collective-permute-start(f32[544,128]{1,0:T(8,128)S(1)} %bitcast.10), channel_id=1, source_target_pairs={{0,1},{1,0},{2,3},{3,2},{4,5},{5,4},{6,7},{7,6},{8,9},{9,8},{10,11... | collective-permute-start | bytes 835592 | tf_op jit(solution)/shard_map/ppermute | solution.py:677
  49.2 5.1 %collective-permute-start.5 = (f32[272,128]{1,0:T(8,128)S(1)}, f32[272,128]{1,0:T(8,128)S(1)}, u32[]{:S(2)}, u32[]{:S(2)}) collective-permute-start(f32[272,128]{1,0:T(8,128)S(1)} %slice.8), channel_id=1, source_target_pairs={{0,2},{1,3},{2,0},{3,1},{4,6},{5,7},{6,4},{7,5},{8,10},{9,11},{10,... | collective-permute-start | bytes 417800 | tf_op jit(solution)/shard_map/ppermute | solution.py:677
  51.3 5.1 %collective-permute-start.6 = (f32[272,128]{1,0:T(8,128)S(1)}, f32[272,128]{1,0:T(8,128)S(1)}, u32[]{:S(2)}, u32[]{:S(2)}) collective-permute-start(f32[272,128]{1,0:T(8,128)S(1)} %slice.9), channel_id=1, source_target_pairs={{0,4},{4,0},{8,12},{12,8},{16,20},{20,16},{24,28},{28,24},{1,5},{5... | collective-permute-start | bytes 417800 | tf_op jit(solution)/shard_map/ppermute | solution.py:677
  52.3 5.4 %collective-permute-start.4 = (f32[544,128]{1,0:T(8,128)S(1)}, f32[544,128]{1,0:T(8,128)S(1)}, u32[]{:S(2)}, u32[]{:S(2)}) collective-permute-start(f32[544,128]{1,0:T(8,128)S(1)} %collective-permute-done.3.rest_4_), channel_id=1, source_target_pairs={{0,1},{1,0},{2,3},{3,2},{4,5},{5,4},{6,7},{7,6},{8,9},{9,8},{10,11... | collective-permute-start | bytes 835592 | tf_op jit(solution)/shard_map/ppermute | solution.py:677
  52.3 5.4 %collective-permute-start.2 = (f32[544,128]{1,0:T(8,128)S(1)}, f32[544,128]{1,0:T(8,128)S(1)}, u32[]{:S(2)}, u32[]{:S(2)}) collective-permute-start(f32[544,128]{1,0:T(8,128)S(1)} %collective-permute-done.1.rest_2_), channel_id=1, source_target_pairs={{0,1},{1,0},{2,3},{3,2},{4,5},{5,4},{6,7},{7,6},{8,9},{9,8},{10,11... | collective-permute-start | bytes 835592 | tf_op jit(solution)/shard_map/ppermute | solution.py:677
  54.3 2.3 %collective-permute-start.7 = (f32[272,128]{1,0:T(8,128)S(1)}, f32[272,128]{1,0:T(8,128)S(1)}, u32[]{:S(2)}, u32[]{:S(2)}) collective-permute-start(f32[272,128]{1,0:T(8,128)S(1)} %collective-permute-done.5.rest_6_), channel_id=1, source_target_pairs={{0,1},{1,0},{2,3},{3,2},{4,5},{5,4},{6,7},{7,6},{8,9},{9,8},{10,11... | collective-permute-start | bytes 417800 | tf_op jit(solution)/shard_map/ppermute | solution.py:677
  56.4 1.4 %collective-permute-start.8 = (f32[272,128]{1,0:T(8,128)S(1)}, f32[272,128]{1,0:T(8,128)S(1)}, u32[]{:S(2)}, u32[]{:S(2)}) collective-permute-start(f32[272,128]{1,0:T(8,128)S(1)} %collective-permute-done.6.rest_7_), channel_id=1, source_target_pairs={{0,1},{1,0},{2,3},{3,2},{4,5},{5,4},{6,7},{7,6},{8,9},{9,8},{10,11... | collective-permute-start | bytes 417800 | tf_op jit(solution)/shard_map/ppermute | solution.py:677

commit v4 on v3

--- a/solution.py
+++ b/solution.py
@@ -662,11 +662,34 @@
     )
 
 
+def join_kernel(where_ref, *refs):
+    *parts, out_ref, sem = refs
+    copies = []
+    for k, part in enumerate(parts):
+        at = pl.multiple_of((where_ref[2] // 2 ^ k) * PAYLOAD_ROWS, 8)
+        copies.append(pltpu.make_async_copy(part, out_ref.at[pl.ds(at, PAYLOAD_ROWS)], sem.at[k]))
+        copies[-1].start()
+    for copy in copies:
+        copy.wait()
+
+
+def join(parts, where):
+    return pl.pallas_call(
+        join_kernel,
+        out_shape=jax.ShapeDtypeStruct((len(parts) * PAYLOAD_ROWS, LANES), F32),
+        in_specs=[SMEM] + [VMEM] * len(parts),
+        out_specs=VMEM,
+        scratch_shapes=[pltpu.SemaphoreType.DMA((len(parts),))],
+        compiler_params=params(16),
+        name="join",
+    )(where, *parts)
+
+
 def gather_and_smooth(payload, adjacency, vol_count, dsg_count, const):
     patches = adjacency.shape[0]
     per_owner = patches // dsg_count
     y_at = lax.axis_index("vol") % 2 if (vol_count, dsg_count) == (8, 4) else 0
-    where = jnp.stack([lax.axis_index("dsg"), y_at]).astype(jnp.int32)
+    where = jnp.stack([lax.axis_index("dsg"), y_at, lax.axis_index("vol")]).astype(jnp.int32)
     if vol_count != 8 or dsg_count != 4:
         whole = lax.all_gather(payload, ("vol", "dsg"), axis=0, tiled=True)
         items = ((vol_count * dsg_count, 0, 0),)
@@ -676,12 +699,7 @@
         count = vol_count if axis == "vol" else dsg_count
         return lax.ppermute(array, axis, [(i, i ^ bit) for i in range(count)])
 
-    copies = jnp.broadcast_to(payload[None], (vol_count // 2,) + payload.shape)
-    along_z = lax.all_to_all(
-        copies, "vol", split_axis=0, concat_axis=0, tiled=True,
-        axis_index_groups=[list(range(y, vol_count, 2)) for y in range(2)],
-    )
-    here = along_z.reshape(-1, LANES)
+    here = join([payload] + [over("vol", payload, 2 * k) for k in (1, 2, 3)], where)
     half = here.shape[0] // 2
     beside_y = over("vol", here, 1)
     beside_x = over("dsg", here, 2)

time: 65.7 us -> 64.1 us (0.976)
  blocking collectives: 10.1 us -> 0 us
  starting transfers between devices: 16.4 us -> 21.1 us
  waiting for transfers between devices: 15.8 us -> 18.7 us
  Pallas kernels: 21.9 us -> 22.9 us
    all_to_all x1 -> x0, blocking collectives: 10.1 us -> none  [gather_and_smooth(): lax.all_to_all(copies, 'vol', split_axis=0, concat_axis=0, tiled=True, ax...]
    ppermute x9 -> x12, starting transfers between devices: 5.65 us -> 10.3 us  [over(): return lax.ppermute(array, axis, [(i, i ^ bit) for i in range(count)])]
    ppermute x9 -> x12, waiting for transfers between devices: 9.72 us -> 12.6 us  [over(): return lax.ppermute(array, axis, [(i, i ^ bit) for i in range(count)])]
    pallas_call x0 -> x1, Pallas kernels: none -> 0.98 us  [join(): pl.pallas_call(join_kernel, out_shape=jax.ShapeDtypeStruct((len(parts) *...]
  transfers between devices with their start and end apart: 11 -> 14, of which waited for: 7 -> 8; matrix products, arithmetic and copies ran while one was open for 0% -> 0% of each run, Pallas kernels for 11% -> 11%
where the time goes in v4:
time: 64.1 us; the launch traced here: 63.8 us
  Pallas kernels  22.9 us (36%)
  starting transfers between devices  21.1 us (33%)
  waiting for transfers between devices  18.7 us (29%)
  between operations  0.9 us (1%)
    ppermute x12, waiting for transfers between devices, over(): return lax.ppermute(array, axis, [(i, i ^ bit) for i in range(count)])  12.6 us
    ppermute x12, starting transfers between devices, over(): return lax.ppermute(array, axis, [(i, i ^ bit) for i in range(count)])  10.3 us
    pallas_call x1, Pallas kernels, smooth(): pl.pallas_call(functools.partial(smooth_kernel, items, per_owner), out_sh...  7.59 us
    all_to_all x1, starting transfers between devices, per_device(): lax.all_to_all(request, 'vol', split_axis=0, concat_axis=0, tiled=True)  7.29 us
    pallas_call x1, Pallas kernels, near_densities(): pl.pallas_call(functools.partial(near_kernel, 0), out_shape=jax.ShapeDtyp...  3.61 us
    pallas_call x1, Pallas kernels, near_grids(): pl.pallas_call(near_grid_kernel, out_shape=(jax.ShapeDtypeStruct((GROUP *...  3.48 us
    all_to_all x1, starting transfers between devices, per_device(): lax.all_to_all(answer, 'vol', split_axis=0, concat_axis=0, tiled=True)  3.48 us
    pallas_call x1, Pallas kernels, far_answers(): pl.pallas_call(far_kernel, out_shape=jax.ShapeDtypeStruct((owners, 1, cap...  3.35 us
  transfers between devices with their start and end apart: 14, of which 8 were waited for; matrix products, arithmetic and copies ran while one was open for 0% of the time, Pallas kernels for 11%

profile of v4, /device:TPU:0, one launch (start us, length us, event | category | flops | bytes accessed | tf_op | source)
XLA Modules:
  0.0 63.8 jit_solution(1046184575699298448)
XLA Ops:
  0.6 0.0 copy-start
  0.6 2.3 %pack_requests.1 = (f32[8,8,160]{2,1,0:T(8,128)}, s32[1,512]{1,0:T(1,128)}) custom-call(f32[8,512]{1,0:T(8,128)} %geom_ref.1, s32[1,512]{1,0:T(1,128)} %bitcast.11, s32[1,512]{1,0:T(1,128)} %bitcast.12), custom_call_target="tpu_custom_call" | custom-call | tf_op jit(solution)/shard_map/pack_requests/pallas_call | solution.py:155
  3.0 7.3 %all-to-all-start = ((f32[8,8,160]{2,1,0:T(8,128)}), f32[8,8,160]{2,1,0:T(8,128)S(1)}, u32[]{:S(2)}, u32[]{:S(2)}) async-start(f32[8,8,160]{2,1,0:T(8,128)} %get-tuple-element.10), calls=%async_computation | async-start | bytes 131072 | tf_op jit(solution)/shard_map/all_to_all | solution.py:725
  10.3 0.0 copy-start.7
  10.3 0.0 copy-start.9
  10.3 0.0 copy-start.10
  10.3 3.6 %near_densities.1.dens_in = f32[1,1024]{1,0:T(1,128)} custom-call(s32[2048]{0:T(1024)} %cell_in.3, f32[4096,128]{1,0:T(8,128)} %fields_in.3, f32[8,2048]{1,0:T(8,128)} %geom_in.5), custom_call_target="tpu_custom_call" | custom-call | flops 20000000 | bytes 4000000 | tf_op jit(solution)/shard_map/near_densities/pallas_call | solution.py:264
  13.9 0.0 copy-start.8
  13.9 0.0 copy-start.2
  13.9 0.0 copy-start.4
  13.9 0.0 copy-start.5
  14.0 0.0 copy-start.13
  14.0 3.2 %all-to-all-done.request_in = f32[8,8,160]{2,1,0:T(8,128)S(1)} async-done(((f32[8,8,160]{2,1,0:T(8,128)}), f32[8,8,160]{2,1,0:T(8,128)S(1)}, u32[]{:S(2)}, u32[]{:S(2)}) %all-to-all-start) | async-done | bytes 40992 | tf_op jit(solution)/shard_map/all_to_all | solution.py:725
  17.2 0.0 copy-done
  17.2 3.4 %far_answers.1 = f32[8,1,160]{2,1,0:T(1,128)} custom-call(f32[8,8,160]{2,1,0:T(8,128)S(1)} %all-to-all-done.request_in, f32[4096,128]{1,0:T(8,128)S(1)} %copy-done), custom_call_target="tpu_custom_call" | custom-call | tf_op jit(solution)/shard_map/far_answers/pallas_call | solution.py:297
  20.5 0.0 copy-start.14
  20.5 0.0 copy-start.1
  20.5 0.0 copy-start.6
  20.6 0.0 copy-start.11
  20.6 0.0 copy-start.12
  20.6 3.5 %all-to-all-start.1 = ((f32[8,1,160]{2,1,0:T(1,128)}), f32[8,1,160]{2,1,0:T(1,128)S(1)}, u32[]{:S(2)}, u32[]{:S(2)}) async-start(f32[8,1,160]{2,1,0:T(1,128)} %far_answers.1), calls=%async_computation.1 | async-start | bytes 16384 | tf_op jit(solution)/shard_map/all_to_all | solution.py:729
  24.1 0.0 copy-done.3
  24.1 0.0 copy-done.7
  24.1 0.0 copy-done.9
  24.1 0.0 copy-done.10
  24.1 0.0 copy-done.8
  24.1 3.5 %near_grids.1 = (f32[256,64]{1,0:T(8,128)S(1)}, f32[8,128]{1,0:T(8,128)S(1)}) custom-call(f32[1,1024]{1,0:T(1,128)S(1)} %copy-done.8, s32[2048]{0:T(1024)S(1)} %copy-done.7, f32[4096,128]{1,0:T(8,128)S(1)} %copy-done, f32[8,2048]{1,0:T(8,128)S(1)} %copy-done.3, s32[1,2048]{1,0:T(1,128)S(1)} %bitcast.8, s32[1,512]{1,0:T(1,128)S(1)} %bitcast.9), custom_call_target="tpu_custom_call" | custom-call | flops 100000000 | bytes 4000000 | tf_op jit(solution)/shard_map/near_grids/pallas_call | solution.py:377
  27.6 2.9 %all-to-all-done.1.reply_ref = f32[8,1,160]{2,1,0:T(1,128)S(1)} async-done(((f32[8,1,160]{2,1,0:T(1,128)}), f32[8,1,160]{2,1,0:T(1,128)S(1)}, u32[]{:S(2)}, u32[]{:S(2)}) %all-to-all-start.1) | async-done | bytes 5152 | tf_op jit(solution)/shard_map/all_to_all | solution.py:729
  30.5 0.0 copy-done.2
  30.5 0.0 copy-done.4
  30.5 0.0 copy-done.5
  30.5 1.6 %make_payload.1 = (f32[1,512]{1,0:T(1,128)}, f32[136,128]{1,0:T(8,128)S(1)}) custom-call(f32[8,1,160]{2,1,0:T(1,128)S(1)} %all-to-all-done.1.reply_ref, s32[1,512]{1,0:T(1,128)S(1)} %copy-done.13, f32[8,512]{1,0:T(8,128)S(1)} %copy-done.5, s32[1,512]{1,0:T(1,128)S(1)} %bitcast.10, f32[8,128]{1,0:T(8,128)S(1)} %get-tuple-element.14.slot_ref, ...), custom_call_target="tpu_custom_call" | custom-call | tf_op jit(solution)/shard_map/make_payload/pallas_call | solution.py:440
  32.1 0.9 %collective-permute-start.2 = (f32[136,128]{1,0:T(8,128)S(1)}, f32[136,128]{1,0:T(8,128)S(1)}, u32[]{:S(2)}, u32[]{:S(2)}) collective-permute-start(f32[136,128]{1,0:T(8,128)S(1)} %get-tuple-element.17.refs_0_), channel_id=1, source_target_pairs={{0,24},{4,28},{8,16},{12,20},{16,8},{20,12},{24,0},{28,4},{1,25},{... | collective-permute-start | bytes 208904 | tf_op jit(solution)/shard_map/ppermute | solution.py:700
  32.9 1.1 %collective-permute-start.1 = (f32[136,128]{1,0:T(8,128)S(1)}, f32[136,128]{1,0:T(8,128)S(1)}, u32[]{:S(2)}, u32[]{:S(2)}) collective-permute-start(f32[136,128]{1,0:T(8,128)S(1)} %get-tuple-element.17.refs_0_), channel_id=1, source_target_pairs={{0,16},{4,20},{8,24},{12,28},{16,0},{20,4},{24,8},{28,12},{1,17},{... | collective-permute-start | bytes 208904 | tf_op jit(solution)/shard_map/ppermute | solution.py:700
  34.1 2.4 %collective-permute-start = (f32[136,128]{1,0:T(8,128)S(1)}, f32[136,128]{1,0:T(8,128)S(1)}, u32[]{:S(2)}, u32[]{:S(2)}) collective-permute-start(f32[136,128]{1,0:T(8,128)S(1)} %get-tuple-element.17.refs_0_), channel_id=1, source_target_pairs={{0,8},{4,12},{8,0},{12,4},{16,24},{20,28},{24,16},{28,20},{1,9},{5... | collective-permute-start | bytes 208904 | tf_op jit(solution)/shard_map/ppermute | solution.py:700
  36.5 0.1 pad_add_fusion.where_ref
  36.6 1.8 %collective-permute-done.2.refs_3_ = f32[136,128]{1,0:T(8,128)S(1)} collective-permute-done((f32[136,128]{1,0:T(8,128)S(1)}, f32[136,128]{1,0:T(8,128)S(1)}, u32[]{:S(2)}, u32[]{:S(2)}) %collective-permute-start.2) | collective-permute-done | bytes 69664 | tf_op jit(solution)/shard_map/ppermute | solution.py:700
  38.3 1.3 %collective-permute-done.1.refs_2_ = f32[136,128]{1,0:T(8,128)S(1)} collective-permute-done((f32[136,128]{1,0:T(8,128)S(1)}, f32[136,128]{1,0:T(8,128)S(1)}, u32[]{:S(2)}, u32[]{:S(2)}) %collective-permute-start.1) | collective-permute-done | bytes 69664 | tf_op jit(solution)/shard_map/ppermute | solution.py:700
  39.6 0.0 collective-permute-done.refs_1_
  39.7 1.0 %join.1.rest_0_ = f32[544,128]{1,0:T(8,128)S(1)} custom-call(s32[3]{0:T(128)S(1)} %pad_add_fusion.where_ref, f32[136,128]{1,0:T(8,128)S(1)} %get-tuple-element.17.refs_0_, f32[136,128]{1,0:T(8,128)S(1)} %collective-permute-done.refs_1_, f32[136,128]{1,0:T(8,128)S(1)} %collective-permute-done.1.refs_2_, f32[136,128]{1,0:T(8,128)S(1)} %collective-permute-done.2.refs_3_), custom_call_target="tpu_custom_call" | custom-call | tf_op jit(solution)/shard_map/join/pallas_call | solution.py:677
  40.6 0.6 %collective-permute-start.6 = (f32[544,128]{1,0:T(8,128)S(1)}, f32[544,128]{1,0:T(8,128)S(1)}, u32[]{:S(2)}, u32[]{:S(2)}) collective-permute-start(f32[544,128]{1,0:T(8,128)S(1)} %join.1.rest_0_), channel_id=1, source_target_pairs={{0,4},{4,0},{8,12},{12,8},{16,20},{20,16},{24,28},{28,24},{1,5},{5... | collective-permute-start | bytes 835592 | tf_op jit(solution)/shard_map/ppermute | solution.py:700
  41.3 1.5 %collective-permute-start.4 = (f32[544,128]{1,0:T(8,128)S(1)}, f32[544,128]{1,0:T(8,128)S(1)}, u32[]{:S(2)}, u32[]{:S(2)}) collective-permute-start(f32[544,128]{1,0:T(8,128)S(1)} %join.1.rest_0_), channel_id=1, source_target_pairs={{0,2},{1,3},{2,0},{3,1},{4,6},{5,7},{6,4},{7,5},{8,10},{9,11},{10,... | collective-permute-start | bytes 835592 | tf_op jit(solution)/shard_map/ppermute | solution.py:700
  42.8 0.0 collective-permute-start.3
  42.8 4.8 %collective-permute-done.6.rest_4_ = f32[544,128]{1,0:T(8,128)S(1)} collective-permute-done((f32[544,128]{1,0:T(8,128)S(1)}, f32[544,128]{1,0:T(8,128)S(1)}, u32[]{:S(2)}, u32[]{:S(2)}) %collective-permute-start.6) | collective-permute-done | bytes 278560 | tf_op jit(solution)/shard_map/ppermute | solution.py:700
  47.6 2.1 %collective-permute-start.8 = (f32[272,128]{1,0:T(8,128)S(1)}, f32[272,128]{1,0:T(8,128)S(1)}, u32[]{:S(2)}, u32[]{:S(2)}) collective-permute-start(f32[272,128]{1,0:T(8,128)S(1)} %slice.8), channel_id=1, source_target_pairs={{0,2},{1,3},{2,0},{3,1},{4,6},{5,7},{6,4},{7,5},{8,10},{9,11},{10,... | collective-permute-start | bytes 417800 | tf_op jit(solution)/shard_map/ppermute | solution.py:700
  49.7 0.0 collective-permute-done.4.rest_2_
  49.7 1.1 %collective-permute-start.9 = (f32[272,128]{1,0:T(8,128)S(1)}, f32[272,128]{1,0:T(8,128)S(1)}, u32[]{:S(2)}, u32[]{:S(2)}) collective-permute-start(f32[272,128]{1,0:T(8,128)S(1)} %slice.9), channel_id=1, source_target_pairs={{0,4},{4,0},{8,12},{12,8},{16,20},{20,16},{24,28},{28,24},{1,5},{5... | collective-permute-start | bytes 417800 | tf_op jit(solution)/shard_map/ppermute | solution.py:700
  50.9 0.0 collective-permute-start.7
  50.9 0.5 collective-permute-start.5
  51.4 1.4 %collective-permute-done.8.rest_6_ = f32[272,128]{1,0:T(8,128)S(1)} collective-permute-done((f32[272,128]{1,0:T(8,128)S(1)}, f32[272,128]{1,0:T(8,128)S(1)}, u32[]{:S(2)}, u32[]{:S(2)}) %collective-permute-start.8) | collective-permute-done | bytes 139296 | tf_op jit(solution)/shard_map/ppermute | solution.py:700
  52.7 0.0 collective-permute-start.10
  52.7 2.1 %collective-permute-done.9.rest_7_ = f32[272,128]{1,0:T(8,128)S(1)} collective-permute-done((f32[272,128]{1,0:T(8,128)S(1)}, f32[272,128]{1,0:T(8,128)S(1)}, u32[]{:S(2)}, u32[]{:S(2)}) %collective-permute-start.9) | collective-permute-done | bytes 139296 | tf_op jit(solution)/shard_map/ppermute | solution.py:700
  54.8 0.0 collective-permute-start.11
  54.8 0.0 copy-done.14
  54.8 0.1 copy.17.adj_ref
  55.0 0.0 collective-permute-done.3.rest_1_
  55.0 0.0 collective-permute-done.10.rest_8_
  55.0 0.0 collective-permute-done.7.rest_5_
  55.0 1.2 %collective-permute-done.11.rest_9_ = f32[272,128]{1,0:T(8,128)S(1)} collective-permute-done((f32[272,128]{1,0:T(8,128)S(1)}, f32[272,128]{1,0:T(8,128)S(1)}, u32[]{:S(2)}, u32[]{:S(2)}) %collective-permute-start.11) | collective-permute-done | bytes 139296 | tf_op jit(solution)/shard_map/ppermute | solution.py:700
  56.2 0.0 collective-permute-done.5.rest_3_
  56.2 0.0 copy-done.6
  56.2 0.0 copy-done.11
  56.2 0.0 copy-done.12
  56.2 7.6 %smooth.1 = f32[24,64,64]{2,1,0:T(8,128)} custom-call(s32[3]{0:T(128)S(1)} %pad_add_fusion.where_ref, s32[96,4]{1,0:T(8,128)S(1)} %copy.17.adj_ref, f32[256,512]{1,0:T(8,128)S(1)} %copy-done.1, f32[64,64]{1,0:T(8,128)S(1)} %copy-done.4, f32[128,128]{1,0:T(8,128)S(1)} %copy-done.2, f32[64,128]{1,0:T(8,128)S(1)} %copy-done.6, f32[8,64]{1,0:T(8,128)S(1)} %copy-done.12, ...), custom_call_target="tpu_custom_call" | custom-call | tf_op jit(solution)/shard_map/smooth/pallas_call | solution.py:641
  (5 shorter events, 0.0 us)
Async XLA Ops:
  0.6 16.5 %copy-start = (f32[4096,128]{1,0:T(8,128)S(1)}, f32[4096,128]{1,0:T(8,128)}, u32[]{:S(2)}) copy-start(f32[4096,128]{1,0:T(8,128)} %fields_in.3) | copy-start | bytes 6291460
  3.0 14.2 %all-to-all-start = ((f32[8,8,160]{2,1,0:T(8,128)}), f32[8,8,160]{2,1,0:T(8,128)S(1)}, u32[]{:S(2)}, u32[]{:S(2)}) async-start(f32[8,8,160]{2,1,0:T(8,128)} %get-tuple-element.10), calls=%async_computation | async-start | bytes 131072 | tf_op jit(solution)/shard_map/all_to_all | solution.py:725
  10.2 13.8 %copy-start.3 = (f32[8,2048]{1,0:T(8,128)S(1)}, f32[8,2048]{1,0:T(8,128)}, u32[]{:S(2)}) copy-start(f32[8,2048]{1,0:T(8,128)} %geom_in.5) | copy-start | bytes 196612
  10.3 13.8 %copy-start.7 = (s32[2048]{0:T(1024)S(1)}, s32[2048]{0:T(1024)}, u32[]{:S(2)}) copy-start(s32[2048]{0:T(1024)} %cell_in.3) | copy-start | bytes 24580
  10.3 13.8 %copy-start.9 = (s32[2048]{0:T(1024)S(1)}, s32[2048]{0:T(1024)}, u32[]{:S(2)}) copy-start(s32[2048]{0:T(1024)} %param.22) | copy-start | bytes 24580
  10.3 13.8 %copy-start.10 = (s32[512]{0:T(512)S(1)}, s32[512]{0:T(512)}, u32[]{:S(2)}) copy-start(s32[512]{0:T(512)} %param.19) | copy-start | bytes 6148
  13.9 10.2 %copy-start.8 = (f32[1,1024]{1,0:T(1,128)S(1)}, f32[1,1024]{1,0:T(1,128)}, u32[]{:S(2)}) copy-start(f32[1,1024]{1,0:T(1,128)} %near_densities.1.dens_in) | copy-start | bytes 12292
  13.9 16.6 %copy-start.2 = (f32[128,128]{1,0:T(8,128)S(1)}, f32[128,128]{1,0:T(8,128)}, u32[]{:S(2)}) copy-start(f32[128,128]{1,0:T(8,128)} %constant.35.clone.pair_ref) | copy-start | bytes 196612
  13.9 16.6 %copy-start.4 = (f32[64,64]{1,0:T(8,128)S(1)}, f32[64,64]{1,0:T(8,128)}, u32[]{:S(2)}) copy-start(f32[64,64]{1,0:T(8,128)} %constant.34.clone.basis_ref) | copy-start | bytes 49156
  13.9 16.6 %copy-start.5 = (f32[8,512]{1,0:T(8,128)S(1)}, f32[8,512]{1,0:T(8,128)}, u32[]{:S(2)}) copy-start(f32[8,512]{1,0:T(8,128)} %geom_ref.1) | copy-start | bytes 49156
  14.0 16.6 %copy-start.13 = (s32[1,512]{1,0:T(1,128)S(1)}, s32[1,512]{1,0:T(1,128)}, u32[]{:S(2)}) copy-start(s32[1,512]{1,0:T(1,128)} %get-tuple-element.12.place_ref) | copy-start | bytes 6148
  20.5 34.3 %copy-start.14 = (s32[96,4]{0,1:T(4,128)S(1)}, s32[96,4]{0,1:T(4,128)}, u32[]{:S(2)}) copy-start(s32[96,4]{0,1:T(4,128)} %param.23) | copy-start | bytes 4612
  20.5 35.7 %copy-start.1 = (f32[256,512]{1,0:T(8,128)S(1)}, f32[256,512]{1,0:T(8,128)}, u32[]{:S(2)}) copy-start(f32[256,512]{1,0:T(8,128)} %constant.39.clone.coupling_ref) | copy-start | bytes 1572868
  20.5 35.7 %copy-start.6 = (f32[64,128]{1,0:T(8,128)S(1)}, f32[64,128]{1,0:T(8,128)}, u32[]{:S(2)}) copy-start(f32[64,128]{1,0:T(8,128)} %constant.38.clone.series_ref) | copy-start | bytes 98308
  20.6 35.7 %copy-start.11 = (f32[8,128]{1,0:T(8,128)S(1)}, f32[8,128]{1,0:T(8,128)}, u32[]{:S(2)}) copy-start(f32[8,128]{1,0:T(8,128)} %constant.37.clone.scale_ref) | copy-start | bytes 12292
  20.6 35.7 %copy-start.12 = (f32[8,64]{1,0:T(8,128)S(1)}, f32[8,64]{1,0:T(8,128)}, u32[]{:S(2)}) copy-start(f32[8,64]{1,0:T(8,128)} %constant.36.clone.edge_ref) | copy-start | bytes 6148
  20.6 9.9 %all-to-all-start.1 = ((f32[8,1,160]{2,1,0:T(1,128)}), f32[8,1,160]{2,1,0:T(1,128)S(1)}, u32[]{:S(2)}, u32[]{:S(2)}) async-start(f32[8,1,160]{2,1,0:T(1,128)} %far_answers.1), calls=%async_computation.1 | async-start | bytes 16384 | tf_op jit(solution)/shard_map/all_to_all | solution.py:729
  32.1 6.2 %collective-permute-start.2 = (f32[136,128]{1,0:T(8,128)S(1)}, f32[136,128]{1,0:T(8,128)S(1)}, u32[]{:S(2)}, u32[]{:S(2)}) collective-permute-start(f32[136,128]{1,0:T(8,128)S(1)} %get-tuple-element.17.refs_0_), channel_id=1, source_target_pairs={{0,24},{4,28},{8,16},{12,20},{16,8},{20,12},{24,0},{28,4},{1,25},{... | collective-permute-start | bytes 208904 | tf_op jit(solution)/shard_map/ppermute | solution.py:700
  32.9 6.7 %collective-permute-start.1 = (f32[136,128]{1,0:T(8,128)S(1)}, f32[136,128]{1,0:T(8,128)S(1)}, u32[]{:S(2)}, u32[]{:S(2)}) collective-permute-start(f32[136,128]{1,0:T(8,128)S(1)} %get-tuple-element.17.refs_0_), channel_id=1, source_target_pairs={{0,16},{4,20},{8,24},{12,28},{16,0},{20,4},{24,8},{28,12},{1,17},{... | collective-permute-start | bytes 208904 | tf_op jit(solution)/shard_map/ppermute | solution.py:700
  34.1 5.6 %collective-permute-start = (f32[136,128]{1,0:T(8,128)S(1)}, f32[136,128]{1,0:T(8,128)S(1)}, u32[]{:S(2)}, u32[]{:S(2)}) collective-permute-start(f32[136,128]{1,0:T(8,128)S(1)} %get-tuple-element.17.refs_0_), channel_id=1, source_target_pairs={{0,8},{4,12},{8,0},{12,4},{16,24},{20,28},{24,16},{28,20},{1,9},{5... | collective-permute-start | bytes 208904 | tf_op jit(solution)/shard_map/ppermute | solution.py:700
  40.6 6.9 %collective-permute-start.6 = (f32[544,128]{1,0:T(8,128)S(1)}, f32[544,128]{1,0:T(8,128)S(1)}, u32[]{:S(2)}, u32[]{:S(2)}) collective-permute-start(f32[544,128]{1,0:T(8,128)S(1)} %join.1.rest_0_), channel_id=1, source_target_pairs={{0,4},{4,0},{8,12},{12,8},{16,20},{20,16},{24,28},{28,24},{1,5},{5... | collective-permute-start | bytes 835592 | tf_op jit(solution)/shard_map/ppermute | solution.py:700
  41.3 8.4 %collective-permute-start.4 = (f32[544,128]{1,0:T(8,128)S(1)}, f32[544,128]{1,0:T(8,128)S(1)}, u32[]{:S(2)}, u32[]{:S(2)}) collective-permute-start(f32[544,128]{1,0:T(8,128)S(1)} %join.1.rest_0_), channel_id=1, source_target_pairs={{0,2},{1,3},{2,0},{3,1},{4,6},{5,7},{6,4},{7,5},{8,10},{9,11},{10,... | collective-permute-start | bytes 835592 | tf_op jit(solution)/shard_map/ppermute | solution.py:700
  42.8 12.2 %collective-permute-start.3 = (f32[544,128]{1,0:T(8,128)S(1)}, f32[544,128]{1,0:T(8,128)S(1)}, u32[]{:S(2)}, u32[]{:S(2)}) collective-permute-start(f32[544,128]{1,0:T(8,128)S(1)} %join.1.rest_0_), channel_id=1, source_target_pairs={{0,1},{1,0},{2,3},{3,2},{4,5},{5,4},{6,7},{7,6},{8,9},{9,8},{10,11... | collective-permute-start | bytes 835592 | tf_op jit(solution)/shard_map/ppermute | solution.py:700
  47.6 5.2 %collective-permute-start.8 = (f32[272,128]{1,0:T(8,128)S(1)}, f32[272,128]{1,0:T(8,128)S(1)}, u32[]{:S(2)}, u32[]{:S(2)}) collective-permute-start(f32[272,128]{1,0:T(8,128)S(1)} %slice.8), channel_id=1, source_target_pairs={{0,2},{1,3},{2,0},{3,1},{4,6},{5,7},{6,4},{7,5},{8,10},{9,11},{10,... | collective-permute-start | bytes 417800 | tf_op jit(solution)/shard_map/ppermute | solution.py:700
  49.7 5.1 %collective-permute-start.9 = (f32[272,128]{1,0:T(8,128)S(1)}, f32[272,128]{1,0:T(8,128)S(1)}, u32[]{:S(2)}, u32[]{:S(2)}) collective-permute-start(f32[272,128]{1,0:T(8,128)S(1)} %slice.9), channel_id=1, source_target_pairs={{0,4},{4,0},{8,12},{12,8},{16,20},{20,16},{24,28},{28,24},{1,5},{5... | collective-permute-start | bytes 417800 | tf_op jit(solution)/shard_map/ppermute | solution.py:700
  50.9 4.1 %collective-permute-start.7 = (f32[544,128]{1,0:T(8,128)S(1)}, f32[544,128]{1,0:T(8,128)S(1)}, u32[]{:S(2)}, u32[]{:S(2)}) collective-permute-start(f32[544,128]{1,0:T(8,128)S(1)} %collective-permute-done.6.rest_4_), channel_id=1, source_target_pairs={{0,1},{1,0},{2,3},{3,2},{4,5},{5,4},{6,7},{7,6},{8,9},{9,8},{10,11... | collective-permute-start | bytes 835592 | tf_op jit(solution)/shard_map/ppermute | solution.py:700
  50.9 5.3 %collective-permute-start.5 = (f32[544,128]{1,0:T(8,128)S(1)}, f32[544,128]{1,0:T(8,128)S(1)}, u32[]{:S(2)}, u32[]{:S(2)}) collective-permute-start(f32[544,128]{1,0:T(8,128)S(1)} %collective-permute-done.4.rest_2_), channel_id=1, source_target_pairs={{0,1},{1,0},{2,3},{3,2},{4,5},{5,4},{6,7},{7,6},{8,9},{9,8},{10,11... | collective-permute-start | bytes 835592 | tf_op jit(solution)/shard_map/ppermute | solution.py:700
  52.7 2.2 %collective-permute-start.10 = (f32[272,128]{1,0:T(8,128)S(1)}, f32[272,128]{1,0:T(8,128)S(1)}, u32[]{:S(2)}, u32[]{:S(2)}) collective-permute-start(f32[272,128]{1,0:T(8,128)S(1)} %collective-permute-done.8.rest_6_), channel_id=1, source_target_pairs={{0,1},{1,0},{2,3},{3,2},{4,5},{5,4},{6,7},{7,6},{8,9},{9,8},{10,11... | collective-permute-start | bytes 417800 | tf_op jit(solution)/shard_map/ppermute | solution.py:700
  54.8 1.4 %collective-permute-start.11 = (f32[272,128]{1,0:T(8,128)S(1)}, f32[272,128]{1,0:T(8,128)S(1)}, u32[]{:S(2)}, u32[]{:S(2)}) collective-permute-start(f32[272,128]{1,0:T(8,128)S(1)} %collective-permute-done.9.rest_7_), channel_id=1, source_target_pairs={{0,1},{1,0},{2,3},{3,2},{4,5},{5,4},{6,7},{7,6},{8,9},{9,8},{10,11... | collective-permute-start | bytes 417800 | tf_op jit(solution)/shard_map/ppermute | solution.py:700

commit v5 on v3

--- a/solution.py
+++ b/solution.py
@@ -16,6 +16,9 @@
 NO_PATCH = 1.0e6
 GRID_ROWS = GROUP // 2 * CTRL
 PAYLOAD_ROWS = GRID_ROWS + 2 * GROUP
+LINES = 4
+CHUNKS = 3
+NEAR_ROWS = PAYLOAD_ROWS + 4 * LINES
 F32 = jnp.float32
 BF16 = jnp.bfloat16
 EXACT = lax.Precision.HIGHEST
@@ -140,7 +143,8 @@
     place = place.astype(jnp.int32)
     place_ref[...] = place
     row = iota((8, count), 0)
-    values = jnp.where(row < 6, geom_ref[...], jnp.where(row == 6, cell_ref[...].astype(F32), 0.0))
+    number = (iota((8, count), 1) + 1).astype(F32)
+    values = jnp.where(row < 6, geom_ref[...], jnp.where(row == 6, cell_ref[...].astype(F32), number))
     high, mid, low = split3(values)
     parts = jnp.concatenate([high, mid, low], 0).astype(BF16)
     put = jnp.where(iota((owners * capacity, count), 0) == place, 1.0, 0.0).astype(BF16)
@@ -250,35 +254,10 @@
     densities(rows_ref, geom_ref, out_ref, count)
 
 
-def near_scratch(fields, count):
-    return [
-        pltpu.SMEM((count,), jnp.int32),
-        pltpu.VMEM(fields.shape, F32),
-        pltpu.VMEM((8, count), F32),
-        pltpu.VMEM((count, LANES), F32),
-        pltpu.SemaphoreType.DMA((3,)),
-    ]
-
-
-def near_densities(near_cell, fields, near_geom, count):
-    return pl.pallas_call(
-        functools.partial(near_kernel, 0),
-        out_shape=jax.ShapeDtypeStruct((1, count), F32),
-        in_specs=[HBM] * 3,
-        out_specs=VMEM,
-        scratch_shapes=near_scratch(fields, count),
-        compiler_params=params(60),
-        cost_estimate=pl.CostEstimate(flops=20_000_000, bytes_accessed=4_000_000, transcendentals=0),
-        name="near_densities",
-    )(near_cell, fields, near_geom)
-
-
-def far_kernel(
-    request_in, fields_ref, out_ref, request_ref, query_ref, cell_v, cell_s, rows_ref, dens_ref, sems, sem
-):
+def far_densities(request_in, fields_ref, request_ref, query_ref, cell_v, cell_s, rows_ref, dens_ref, sems, sem):
     owners, _, capacity = request_in.shape
+    count = owners * capacity
     fetch([(request_in, request_ref)], sems)
-    count = owners * capacity
     for o in range(owners):
         query_ref[:, o * capacity : (o + 1) * capacity] = request_ref[o]
     cell_v[...] = query_ref[6:7, :].astype(jnp.int32)
@@ -287,34 +266,85 @@
     copy.wait()
     gather_rows(lambda p: cell_s[0, p], fields_ref, rows_ref, count)
     densities(rows_ref, query_ref, dens_ref, count)
+
+
+def far_kernel(request_in, fields_ref, out_ref, *scratch):
+    owners, _, capacity = request_in.shape
+    far_densities(request_in, fields_ref, *scratch)
+    dens_ref = scratch[5]
     for o in range(owners):
         out_ref[o] = dens_ref[:, o * capacity : (o + 1) * capacity]
 
 
+def in_rows(x):
+    return jnp.concatenate([x[:, i : i + LANES] for i in range(0, x.shape[1], LANES)], 0)
+
+
+def in_line(x):
+    return jnp.concatenate([x[i : i + 1, :] for i in range(x.shape[0])], 1)
+
+
+def far_spread_kernel(request_in, fields_ref, out_ref, *scratch):
+    owners, _, capacity = request_in.shape
+    far_densities(request_in, fields_ref, *scratch)
+    query_ref, dens_ref = scratch[1], scratch[5]
+    number = iota((LINES * LANES, capacity), 0) + 1
+    found = []
+    for o in range(owners):
+        part = slice(o * capacity, (o + 1) * capacity)
+        place = jnp.where(number == query_ref[7:8, part].astype(jnp.int32), 1.0, 0.0).astype(BF16)
+        high, mid, low = split3(dens_ref[:, part])
+        parts = jnp.concatenate([high, mid, low, jnp.zeros((5, capacity), F32)], 0).astype(BF16)
+        got = nt(parts, place)
+        found.append(in_rows((got[2:3] + got[1:2]) + got[0:1]))
+    lines = [jnp.concatenate(found[y::2], 0) for y in range(2)]
+    for o in range(owners):
+        out_ref[o] = lines[o % 2]
+
+
+def far_scratch(requests):
+    owners, _, capacity = requests.shape
+    count = owners * capacity
+    return [
+        pltpu.VMEM(requests.shape, F32),
+        pltpu.VMEM((8, count), F32),
+        pltpu.VMEM((1, count), jnp.int32),
+        pltpu.SMEM((1, count), jnp.int32),
+        pltpu.VMEM((count, LANES), F32),
+        pltpu.VMEM((1, count), F32),
+        pltpu.SemaphoreType.DMA((1,)),
+        pltpu.SemaphoreType.DMA,
+    ]
+
+
 def far_answers(requests, fields):
     owners, _, capacity = requests.shape
-    count = owners * capacity
     return pl.pallas_call(
         far_kernel,
         out_shape=jax.ShapeDtypeStruct((owners, 1, capacity), F32),
         in_specs=[ANY, VMEM],
         out_specs=VMEM,
-        scratch_shapes=[
-            pltpu.VMEM(requests.shape, F32),
-            pltpu.VMEM((8, count), F32),
-            pltpu.VMEM((1, count), jnp.int32),
-            pltpu.SMEM((1, count), jnp.int32),
-            pltpu.VMEM((count, LANES), F32),
-            pltpu.VMEM((1, count), F32),
-            pltpu.SemaphoreType.DMA((1,)),
-            pltpu.SemaphoreType.DMA,
-        ],
+        scratch_shapes=far_scratch(requests),
         compiler_params=params(24),
         name="far_answers",
     )(requests, fields)
 
 
-def spline_columns(param):
+def far_spread(requests, fields):
+    owners = requests.shape[0]
+    return pl.pallas_call(
+        far_spread_kernel,
+        out_shape=jax.ShapeDtypeStruct((owners, owners // 2 * LINES, LANES), F32),
+        in_specs=[ANY, VMEM],
+        out_specs=VMEM,
+        scratch_shapes=far_scratch(requests),
+        compiler_params=params(24),
+        cost_estimate=pl.CostEstimate(flops=40_000_000, bytes_accessed=4_000_000, transcendentals=0),
+        name="far_spread",
+    )(requests, fields)
+
+
+def spline_weights(param):
     scaled = param * float(CTRL - 3)
     start = jnp.clip(jnp.floor(scaled), 0.0, float(CTRL - 4))
     x = scaled - start
@@ -326,7 +356,11 @@
         (-3.0 * cubed + 3.0 * squared + 3.0 * x + 1.0) * (1.0 / 6.0),
         cubed * (1.0 / 6.0),
     ]
-    off = iota((CTRL, param.shape[1]), 0) - start.astype(jnp.int32)
+    return start.astype(jnp.int32), weights
+
+
+def spline_columns(start, weights):
+    off = iota((CTRL, start.shape[1]), 0) - start
     out = jnp.zeros(off.shape, F32)
     for m in range(4):
         out = jnp.where(off == m, weights[m], out)
@@ -334,32 +368,38 @@
 
 
 def slot_grids(density, s, t, patch, slots):
-    left_high, left_low = halves(spline_columns(s))
-    right_high, right_low = halves(spline_columns(t) * density)
+    start, weights = spline_weights(t)
+    right = spline_columns(start, [w * density for w in weights])
+    return grids_of(spline_columns(*spline_weights(s)), right, patch, slots)
+
+
+def grids_of(left, right, patch, slots):
+    left_high, left_low = halves(left)
+    right_high, right_low = halves(right)
     masks = [jnp.where(patch == slot, 1.0, 0.0).astype(BF16) for slot in slots]
     high = jnp.concatenate([left_high * m for m in masks], 0)
     low = jnp.concatenate([left_low * m for m in masks], 0)
-    return nt(high, right_high) + (nt(high, right_low) + nt(low, right_high))
-
-
-def near_grid_kernel(
-    dens_in, cell_in, fields_in, geom_in, near_in, far_in, grid_ref, slot_ref,
-    dens_ref, spline_ref, near_ref, far_ref, rest_ref, cell_ref, fields_ref, geom_ref, rows_ref, more, sem,
+    return fold(nt(high, jnp.concatenate([right_high, right_low], 0))) + nt(low, right_high)
+
+
+def side_by_side(grids):
+    return [
+        jnp.concatenate([grids[a * CTRL : (a + 1) * CTRL], grids[(a + 1) * CTRL : (a + 2) * CTRL]], 1)
+        for a in range(0, GROUP, 2)
+    ]
+
+
+def near_payload_kernel(
+    cell_in, fields_in, geom_in, near_in, far_in, far_geom_in, out_ref, slot_ref,
+    near_ref, far_ref, far_geom_ref, dens_ref, cell_ref, fields_ref, geom_ref, rows_ref, more, sem,
 ):
-    count, done = near_in.shape[1], dens_in.shape[1]
-    others = [
-        (dens_in, dens_ref.at[:, pl.ds(0, done)]),
-        (geom_in, spline_ref),
-        (near_in, near_ref),
-        (far_in, far_ref),
-    ]
+    others = [(near_in, near_ref), (far_in, far_ref), (far_geom_in, far_geom_ref)]
     others = [pltpu.make_async_copy(a, b, more.at[i]) for i, (a, b) in enumerate(others)]
     for copy in others:
         copy.start()
-    near_kernel(done, cell_in, fields_in, geom_in, rest_ref, cell_ref, fields_ref, geom_ref, rows_ref, sem)
+    near_kernel(0, cell_in, fields_in, geom_in, dens_ref, cell_ref, fields_ref, geom_ref, rows_ref, sem)
     for copy in others:
         copy.wait()
-    dens_ref[:, done:count] = rest_ref[...]
     near, far = near_ref[...].astype(F32), far_ref[...].astype(F32)
     slots = []
     last = jnp.full((1, 1), -1.0, F32)
@@ -368,40 +408,56 @@
         b = jnp.min(jnp.where(far > last, far, NO_PATCH), axis=1, keepdims=True)
         last = jnp.minimum(a, b)
         slots.append(last)
-    slot_ref[...] = jnp.concatenate([jnp.broadcast_to(s, (1, LANES)) for s in slots + slots], 0)
-    grid_ref[...] = slot_grids(dens_ref[...], spline_ref[6:7, :], spline_ref[7:8, :], near, slots)
-
-
-def near_grids(dens, near_cell, fields, near_geom, near_patch, far_patch):
-    count, done = near_geom.shape[1], dens.shape[1]
+    grids = slot_grids(dens_ref[...], geom_ref[6:7, :], geom_ref[7:8, :], near, slots)
+    lane = iota((1, LANES), 1)
+    names = jnp.zeros((1, LANES), F32)
+    for s in range(GROUP):
+        names = jnp.where(lane == s, slots[s], names)
+    slots = [jnp.broadcast_to(s, (1, LANES)) for s in slots]
+    slot_ref[...] = jnp.concatenate(slots + slots, 0)
+    out_ref[0:PAYLOAD_ROWS, :] = jnp.concatenate(side_by_side(grids) + slots + [names] * GROUP, 0)
+    if out_ref.shape[0] > PAYLOAD_ROWS:
+        held = [in_rows(x) for x in (far_geom_ref[6:7, :], far_geom_ref[7:8, :], far)]
+        out_ref[PAYLOAD_ROWS:, :] = jnp.concatenate(held + [jnp.zeros((LINES, LANES), F32)], 0)
+
+
+def near_payload(near_cell, fields, near_geom, near_patch, far_patch, far_geom, rows):
+    count = near_geom.shape[1]
     return pl.pallas_call(
-        near_grid_kernel,
+        near_payload_kernel,
         out_shape=(
-            jax.ShapeDtypeStruct((GROUP * CTRL, CTRL), F32),
+            jax.ShapeDtypeStruct((rows, LANES), F32),
             jax.ShapeDtypeStruct((8, LANES), F32),
         ),
-        in_specs=[ANY] * 6,
+        in_specs=[HBM] * 6,
         out_specs=(VMEM, VMEM),
         scratch_shapes=[
+            pltpu.VMEM(near_patch.shape, jnp.int32),
+            pltpu.VMEM(far_patch.shape, jnp.int32),
+            pltpu.VMEM(far_geom.shape, F32),
             pltpu.VMEM((1, count), F32),
+            pltpu.SMEM((count,), jnp.int32),
+            pltpu.VMEM(fields.shape, F32),
             pltpu.VMEM((8, count), F32),
-            pltpu.VMEM((1, count), jnp.int32),
-            pltpu.VMEM(far_patch.shape, jnp.int32),
-            pltpu.VMEM((1, count - done), F32),
-            *near_scratch(fields, count - done)[:-1],
-            pltpu.SemaphoreType.DMA((4,)),
+            pltpu.VMEM((count, LANES), F32),
+            pltpu.SemaphoreType.DMA((3,)),
             pltpu.SemaphoreType.DMA((3,)),
         ],
-        compiler_params=params(24),
+        compiler_params=params(60),
         cost_estimate=pl.CostEstimate(flops=100_000_000, bytes_accessed=4_000_000, transcendentals=0),
-        name="near_grids",
-    )(dens, near_cell, fields, near_geom, near_patch, far_patch)
+        name="near_payload",
+    )(near_cell, fields, near_geom, near_patch, far_patch, far_geom)
+
+
+def to_spectral(blocks, basis, basis_pair):
+    turned = product(blocks, basis_pair)
+    parts = range(0, blocks.shape[0], CTRL)
+    turned = product(basis, jnp.concatenate([turned[at : at + CTRL] for at in parts], 1))
+    return jnp.concatenate([turned[:, 2 * at : 2 * at + LANES] for at in parts], 0)
 
 
 def payload_kernel(
-    reply_ref, place_ref, geom_ref, far_ref, slot_ref, near_ref,
-    basis_ref, pair_ref,
-    dens_ref, out_ref, flat_ref,
+    reply_ref, place_ref, geom_ref, far_ref, slot_ref, near_ref, basis_ref, pair_ref, dens_ref, out_ref, flat_ref
 ):
     owners, _, capacity = reply_ref.shape
     count = geom_ref.shape[1]
@@ -414,27 +470,13 @@
     dens = (got[2:3] + got[1:2]) + got[0:1]
     dens_ref[...] = dens
     slots = [slot_ref[s : s + 1, 0:1] for s in range(GROUP)]
-    grids = near_ref[...] + slot_grids(
-        dens, geom_ref[6:7, :], geom_ref[7:8, :], far_ref[...].astype(F32), slots
-    )
-    lane = iota((1, LANES), 1)
-    names = jnp.zeros((1, LANES), F32)
-    for s in range(GROUP):
-        names = jnp.where(lane == s, slot_ref[s : s + 1, :], names)
-    out_ref[GRID_ROWS : GRID_ROWS + GROUP, :] = slot_ref[0:GROUP, :]
-    out_ref[GRID_ROWS + GROUP : PAYLOAD_ROWS, :] = jnp.broadcast_to(names, (GROUP, LANES))
-    blocks = [
-        jnp.concatenate([grids[a * CTRL : (a + 1) * CTRL], grids[(a + 1) * CTRL : (a + 2) * CTRL]], 1)
-        for a in range(0, GROUP, 2)
-    ]
-    turned = product(jnp.concatenate(blocks, 0), pair_ref[...])
-    turned = jnp.concatenate([turned[:CTRL], turned[CTRL:]], 1)
-    spectral = product(basis_ref[...], turned)
-    for pair in range(GROUP // 2):
-        out_ref[pair * CTRL : (pair + 1) * CTRL, :] = spectral[:, pair * LANES : (pair + 1) * LANES]
-
-
-def make_payload(reply, place, far_geom, far_patch, slots, near_grid, const):
+    grids = slot_grids(dens, geom_ref[6:7, :], geom_ref[7:8, :], far_ref[...].astype(F32), slots)
+    out_ref[GRID_ROWS:PAYLOAD_ROWS, :] = near_ref[GRID_ROWS:PAYLOAD_ROWS, :]
+    blocks = near_ref[0:GRID_ROWS, :] + jnp.concatenate(side_by_side(grids), 0)
+    out_ref[0:GRID_ROWS, :] = to_spectral(blocks, basis_ref[...], pair_ref[...])
+
+
+def make_payload(reply, place, far_geom, far_patch, slots, near, const):
     owners, _, capacity = reply.shape
     count = far_geom.shape[1]
     return pl.pallas_call(
@@ -443,15 +485,12 @@
             jax.ShapeDtypeStruct((1, count), F32),
             jax.ShapeDtypeStruct((PAYLOAD_ROWS, LANES), F32),
         ),
-        in_specs=[VMEM] * 2 + [WHOLE] * 2 + [VMEM] * 2 + [WHOLE] * 2,
+        in_specs=[VMEM] * 6 + [WHOLE] * 2,
         out_specs=(VMEM, VMEM),
         scratch_shapes=[pltpu.VMEM((1, owners * capacity), F32)],
         compiler_params=params(24),
         name="make_payload",
-    )(
-        reply, place, far_geom, far_patch, slots, near_grid,
-        const["basis"], const["basis_pair"],
-    )
+    )(reply, place, far_geom, far_patch, slots, near, const["basis"], const["basis_pair"])
 
 
 def pair_rows(edge):
@@ -462,12 +501,13 @@
 def absorb(first_own, y_at, per_owner, items, sums, groups, edge, scale, name_v, name_s, edges, where_to, name_sem):
     patches = groups.shape[1]
     low8 = iota((8, LANES), 1) < CTRL
+    spare = per_owner + iota((1, LANES), 1) // 2 % 2
     at = 0
     for ref, parts, _, _ in items:
         for p in range(parts):
             last = (p + 1) * PAYLOAD_ROWS - 1
             patch = ref[last : last + 1, :].astype(jnp.int32) - first_own
-            name_v[at : at + 1, :] = jnp.where((patch >= 0) & (patch < per_owner), patch, -1)
+            name_v[at : at + 1, :] = jnp.where((patch >= 0) & (patch < per_owner), patch, spare)
             at += 1
     names = pltpu.make_async_copy(name_v, name_s, name_sem)
     names.start()
@@ -515,19 +555,16 @@
         for ref, parts, dy, _ in items:
 
             def add_payload(p, carry, ref=ref, at=at):
+                places = [pl.ds(pl.multiple_of(name_s[at + p, s] * CTRL, CTRL), CTRL) for s in range(GROUP)]
+                first = pl.multiple_of(p * PAYLOAD_ROWS, 8)
+                blocks = [ref[pl.ds(first + q * CTRL, CTRL), :] for q in range(GROUP // 2)]
+                held = [sums[s % 2, places[s], :] + blocks[s // 2] for s in range(GROUP)]
                 for s in range(GROUP):
-                    patch = name_s[at + p, s]
-
-                    @pl.when(patch >= 0)
-                    def _():
-                        row = pl.multiple_of(p * PAYLOAD_ROWS + (s // 2) * CTRL, 8)
-                        own = pl.multiple_of(patch * CTRL, CTRL)
-                        sums[s % 2, pl.ds(own, CTRL), :] = sums[s % 2, pl.ds(own, CTRL), :] + ref[pl.ds(row, CTRL), :]
-
+                    sums[s % 2, places[s], :] = held[s]
                 return carry
 
             if dy == wanted:
-                lax.fori_loop(0, parts, add_payload, 0)
+                lax.fori_loop(0, parts, add_payload, 0, unroll=2)
             at += parts
 
     @pl.when(y_at == 0)
@@ -545,7 +582,7 @@
     items, per_owner, where_ref, adj_ref, coupling_ref, basis_ref, pair_ref, series_ref, edge_ref, scale_ref, *rest
 ):
     refs, rest = rest[: len(items)], rest[len(items) :]
-    out_ref, sums, groups, halo_all, halo_rows, *scratch = rest
+    out_ref, sums, groups, halo_all, halo_rows, out_v, out_sem, *scratch = rest
     patches = adj_ref.shape[0]
     first_own = pl.multiple_of(where_ref[0] * per_owner, 8)
     items = [(ref, *item) for ref, item in zip(refs, items)]
@@ -613,20 +650,29 @@
     low16 = iota((16, LANES), 1) < CTRL
     along_cols = [jnp.where(low16, x, y) for x, y in zip(along_cols[::2], along_cols[1::2])]
     from_cols = tn_product(jnp.concatenate(along_cols, 1), both)
-    turned = []
-    for pair in range(pairs):
-        a, b = [slice(patch * CTRL, (patch + 1) * CTRL) for patch in (2 * pair, 2 * pair + 1)]
-        left = sums[0, a, :] + pltpu.roll(sums[1, a, :], CTRL, 1)
-        right = pltpu.roll(sums[0, b, :], CTRL, 1) + sums[1, b, :]
-        spectral = jnp.where(low_half, left, right) * series_ref[...]
-        spectral = spectral + from_rows[:, pair * LANES : (pair + 1) * LANES]
-        turned.append(spectral + from_cols[pair * CTRL : (pair + 1) * CTRL, :])
-    turned = product(jnp.concatenate(turned, 0), basis_both)
-    flat = jnp.concatenate([turned[pair * CTRL : (pair + 1) * CTRL] for pair in range(pairs)], 1)
-    done = product(basis_ref[...], flat)
-    for pair in range(pairs):
-        out_ref[2 * pair] = done[:, pair * LANES : pair * LANES + CTRL]
-        out_ref[2 * pair + 1] = done[:, pair * LANES + CTRL : (pair + 1) * LANES]
+    step = pairs // CHUNKS if pairs % CHUNKS == 0 else pairs
+    stores = []
+    for start in range(0, pairs, step):
+        turned = []
+        for pair in range(start, start + step):
+            a, b = [slice(patch * CTRL, (patch + 1) * CTRL) for patch in (2 * pair, 2 * pair + 1)]
+            left = sums[0, a, :] + pltpu.roll(sums[1, a, :], CTRL, 1)
+            right = pltpu.roll(sums[0, b, :], CTRL, 1) + sums[1, b, :]
+            spectral = jnp.where(low_half, left, right) * series_ref[...]
+            spectral = spectral + from_rows[:, pair * LANES : (pair + 1) * LANES]
+            turned.append(spectral + from_cols[pair * CTRL : (pair + 1) * CTRL, :])
+        turned = product(jnp.concatenate(turned, 0), basis_both)
+        flat = jnp.concatenate([turned[at : at + CTRL] for at in range(0, step * CTRL, CTRL)], 1)
+        done = product(basis_ref[...], flat)
+        for pair in range(start, start + step):
+            at = (pair - start) * LANES
+            out_v[2 * pair] = done[:, at : at + CTRL]
+            out_v[2 * pair + 1] = done[:, at + CTRL : at + LANES]
+        part = pl.ds(2 * start, 2 * step)
+        stores.append(pltpu.make_async_copy(out_v.at[part], out_ref.at[part], out_sem.at[len(stores)]))
+        stores[-1].start()
+    for store in stores:
+        store.wait()
 
 
 def tn_product(x, y):
@@ -642,12 +688,14 @@
         functools.partial(smooth_kernel, items, per_owner),
         out_shape=jax.ShapeDtypeStruct((per_owner, CTRL, CTRL), F32),
         in_specs=[SMEM] + [WHOLE] * 7 + [VMEM] * len(payloads),
-        out_specs=VMEM,
+        out_specs=HBM,
         scratch_shapes=[
-            pltpu.VMEM((2, per_owner * CTRL, LANES), F32),
+            pltpu.VMEM((2, (per_owner + 2) * CTRL, LANES), F32),
             pltpu.VMEM((2, patches, 12 * CTRL), F32),
             pltpu.VMEM((2, patches, 4 * CTRL), F32),
             pltpu.VMEM((per_owner * 8, LANES), F32),
+            pltpu.VMEM((per_owner, CTRL, CTRL), F32),
+            pltpu.SemaphoreType.DMA((CHUNKS,)),
             pltpu.VMEM((total, LANES), jnp.int32),
             pltpu.SMEM((total, LANES), jnp.int32),
             pltpu.VMEM((total * GROUP * 8, LANES), F32),
@@ -662,26 +710,59 @@
     )
 
 
-def gather_and_smooth(payload, adjacency, vol_count, dsg_count, const):
-    patches = adjacency.shape[0]
-    per_owner = patches // dsg_count
-    y_at = lax.axis_index("vol") % 2 if (vol_count, dsg_count) == (8, 4) else 0
-    where = jnp.stack([lax.axis_index("dsg"), y_at]).astype(jnp.int32)
-    if vol_count != 8 or dsg_count != 4:
-        whole = lax.all_gather(payload, ("vol", "dsg"), axis=0, tiled=True)
-        items = ((vol_count * dsg_count, 0, 0),)
-        return smooth([whole], items, where, adjacency, per_owner, const)
-
-    def over(axis, array, bit):
-        count = vol_count if axis == "vol" else dsg_count
-        return lax.ppermute(array, axis, [(i, i ^ bit) for i in range(count)])
-
-    copies = jnp.broadcast_to(payload[None], (vol_count // 2,) + payload.shape)
-    along_z = lax.all_to_all(
-        copies, "vol", split_axis=0, concat_axis=0, tiled=True,
-        axis_index_groups=[list(range(y, vol_count, 2)) for y in range(2)],
-    )
-    here = along_z.reshape(-1, LANES)
+def join_kernel(where_ref, spread_ref, basis_ref, pair_ref, *refs):
+    *parts, out_ref, own_ref, total_ref, near_ref = refs
+    z_at = where_ref[2] // 2
+    total = spread_ref[0]
+    for o in range(1, spread_ref.shape[0]):
+        total = total + spread_ref[o]
+    total_ref[...] = total
+    own_ref[...] = total_ref[pl.ds(z_at * LINES, LINES), :]
+    for k, part in enumerate(parts):
+        near_ref[z_at ^ k] = part[...]
+    blocks = []
+    for z in range(len(parts)):
+        part = near_ref.at[z]
+        dens = total_ref[z * LINES : (z + 1) * LINES, :]
+        s, t, patch = [part[PAYLOAD_ROWS + i * LINES : PAYLOAD_ROWS + (i + 1) * LINES, :] for i in range(3)]
+        start_s, weights_s = spline_weights(s)
+        start_t, weights_t = spline_weights(t)
+        left = spline_columns(in_line(start_s), [in_line(w) for w in weights_s])
+        right = spline_columns(in_line(start_t), [in_line(w * dens) for w in weights_t])
+        slots = [part[GRID_ROWS + i : GRID_ROWS + i + 1, 0:1] for i in range(GROUP)]
+        far = side_by_side(grids_of(left, right, in_line(patch), slots))
+        blocks.append(part[0:GRID_ROWS, :] + jnp.concatenate(far, 0))
+    blocks = to_spectral(jnp.concatenate(blocks, 0), basis_ref[...], pair_ref[...])
+    for z in range(len(parts)):
+        at = z * PAYLOAD_ROWS
+        out_ref[at : at + GRID_ROWS, :] = blocks[z * GRID_ROWS : (z + 1) * GRID_ROWS]
+        out_ref[at + GRID_ROWS : at + PAYLOAD_ROWS, :] = near_ref[z, GRID_ROWS:PAYLOAD_ROWS, :]
+
+
+def join(parts, spread, where, const):
+    return pl.pallas_call(
+        join_kernel,
+        out_shape=(
+            jax.ShapeDtypeStruct((len(parts) * PAYLOAD_ROWS, LANES), F32),
+            jax.ShapeDtypeStruct((LINES, LANES), F32),
+        ),
+        in_specs=[SMEM, VMEM, WHOLE, WHOLE] + [VMEM] * len(parts),
+        out_specs=(VMEM, VMEM),
+        scratch_shapes=[
+            pltpu.VMEM((len(parts) * LINES, LANES), F32),
+            pltpu.VMEM((len(parts), NEAR_ROWS, LANES), F32),
+        ],
+        compiler_params=params(16),
+        name="join",
+    )(where, spread, const["basis"], const["basis_pair"], *parts)
+
+
+def over(axis, array, bit):
+    count = lax.axis_size(axis)
+    return lax.ppermute(array, axis, [(i, i ^ bit) for i in range(count)])
+
+
+def gather_in_plane(here):
     half = here.shape[0] // 2
     beside_y = over("vol", here, 1)
     beside_x = over("dsg", here, 2)
@@ -690,7 +771,7 @@
     arrays = [x for array in arrays for x in (array, over("dsg", array, 1))]
     arrays += corner + [over("dsg", c, 1) for c in corner]
     items = ((4, 0, 0), (4, 0, 0), (4, 0, 1), (4, 0, 1), (4, 1, 0), (4, 1, 0)) + ((2, 1, 1),) * 4
-    return smooth(arrays, items, where, adjacency, per_owner, const)
+    return arrays, items
 
 
 def per_device(
@@ -701,19 +782,31 @@
     capacity = 5 * far_count // (2 * vol_count)
     const = {name: jnp.asarray(value) for name, value in constants().items()}
 
+    per_owner = adjacency.shape[0] // dsg_count
+    staged = vol_count == 8 and dsg_count == 4 and far_count == LINES * LANES
+    vol_at = lax.axis_index("vol")
+    where = jnp.stack([lax.axis_index("dsg"), vol_at % 2 if staged else 0, vol_at]).astype(jnp.int32)
     request, place = pack_requests(
         far_geom, far_block.reshape(1, -1), far_cell.reshape(1, -1), vol_count, capacity
     )
     asked = lax.all_to_all(request, "vol", split_axis=0, concat_axis=0, tiled=True)
-    near_dens = near_densities(near_cell, fields, near_geom, near_cell.shape[0] // 2)
-    asked, near_dens = lax.optimization_barrier((asked, near_dens))
-    answer = far_answers(asked, fields)
-    reply = lax.all_to_all(answer, "vol", split_axis=0, concat_axis=0, tiled=True)
     near_patch, far_patch = near_patch.reshape(1, -1), far_patch.reshape(1, -1)
-    near_grid, slots = near_grids(near_dens, near_cell, fields, near_geom, near_patch, far_patch)
-    far_dens, payload = make_payload(reply, place, far_geom, far_patch, slots, near_grid, const)
-
-    design = gather_and_smooth(payload, adjacency, vol_count, dsg_count, const)
+    near, slots = near_payload(
+        near_cell, fields, near_geom, near_patch, far_patch, far_geom, NEAR_ROWS if staged else PAYLOAD_ROWS
+    )
+    asked, near, slots = lax.optimization_barrier((asked, near, slots))
+    if staged:
+        spread = far_spread(asked, fields)
+        spread = lax.all_to_all(spread, "vol", split_axis=0, concat_axis=0, tiled=True)
+        parts = [near] + [over("vol", near, 2 * k) for k in (1, 2, 3)]
+        here, far_dens = join(parts, spread, where, const)
+        arrays, items = gather_in_plane(here)
+    else:
+        reply = lax.all_to_all(far_answers(asked, fields), "vol", split_axis=0, concat_axis=0, tiled=True)
+        far_dens, payload = make_payload(reply, place, far_geom, far_patch, slots, near, const)
+        arrays = [lax.all_gather(payload, ("vol", "dsg"), axis=0, tiled=True)]
+        items = ((vol_count * dsg_count, 0, 0),)
+    design = smooth(arrays, items, where, adjacency, per_owner, const)
     return far_dens.reshape(-1), design
 
 

time: 65.7 us -> 62.6 us (0.953)
  blocking collectives: 10.1 us -> 0 us
  starting transfers between devices: 16.4 us -> 23.5 us
    all_to_all x1 -> x0, blocking collectives: 10.1 us -> none  [gather_and_smooth(): lax.all_to_all(copies, 'vol', split_axis=0, concat_axis=0, tiled=True, ax...]
    ppermute x9 -> x12, waiting for transfers between devices: 9.72 us -> 15.4 us  [over(): return lax.ppermute(array, axis, [(i, i ^ bit) for i in range(count)])]
    ppermute x9 -> x12, starting transfers between devices: 5.65 us -> 10.7 us  [over(): return lax.ppermute(array, axis, [(i, i ^ bit) for i in range(count)])]
    all_to_all x1, waiting for transfers between devices: 2.91 us -> 0.01 us  [per_device(): lax.all_to_all(spread, 'vol', split_axis=0, concat_axis=0, tiled=True)]
    all_to_all x1, waiting for transfers between devices: 3.2 us -> 0.54 us  [per_device(): lax.all_to_all(request, 'vol', split_axis=0, concat_axis=0, tiled=True)]
    all_to_all x1, starting transfers between devices: 3.48 us -> 5.49 us  [per_device(): lax.all_to_all(spread, 'vol', split_axis=0, concat_axis=0, tiled=True)]
    pallas_call x1, Pallas kernels: 7.58 us -> 6.56 us  [smooth(): pl.pallas_call(functools.partial(smooth_kernel, items, per_owner), out_sh...]
    pallas_call x4 -> x3, Pallas kernels: 12 us -> 12.9 us  [the longest x1 6.26 us: near_payload(): pl.pallas_call(near_payload_kernel, out_shape=(jax.ShapeDtypeStruct((rows...]
  transfers between devices with their start and end apart: 11 -> 14, of which waited for: 7 -> 8; matrix products, arithmetic and copies ran while one was open for 0% -> 0% of each run, Pallas kernels for 11% -> 10%
where the time goes in v5:
time: 62.6 us; the launch traced here: 62.2 us
  starting transfers between devices  23.5 us (38%)
  Pallas kernels  21.7 us (35%)
  waiting for transfers between devices  16 us (26%)
  between operations  0.8 us (1%)
    ppermute x12, waiting for transfers between devices, over(): return lax.ppermute(array, axis, [(i, i ^ bit) for i in range(count)])  15.4 us
    ppermute x12, starting transfers between devices, over(): return lax.ppermute(array, axis, [(i, i ^ bit) for i in range(count)])  10.7 us
    all_to_all x1, starting transfers between devices, per_device(): lax.all_to_all(request, 'vol', split_axis=0, concat_axis=0, tiled=True)  7.29 us
    pallas_call x1, Pallas kernels, smooth(): pl.pallas_call(functools.partial(smooth_kernel, items, per_owner), out_sh...  6.56 us
    pallas_call x1, Pallas kernels, near_payload(): pl.pallas_call(near_payload_kernel, out_shape=(jax.ShapeDtypeStruct((rows...  6.26 us
    all_to_all x1, starting transfers between devices, per_device(): lax.all_to_all(spread, 'vol', split_axis=0, concat_axis=0, tiled=True)  5.49 us
    pallas_call x1, Pallas kernels, far_spread(): pl.pallas_call(far_spread_kernel, out_shape=jax.ShapeDtypeStruct((owners,...  4 us
    pallas_call x1, Pallas kernels, join(): pl.pallas_call(join_kernel, out_shape=(jax.ShapeDtypeStruct((len(parts) *...  2.59 us
  transfers between devices with their start and end apart: 14, of which 8 were waited for; matrix products, arithmetic and copies ran while one was open for 0% of the time, Pallas kernels for 10%

profile of v5, /device:TPU:0, one launch (start us, length us, event | category | flops | bytes accessed | tf_op | source)
XLA Modules:
  0.0 62.2 jit_solution(16514972870144780714)
XLA Ops:
  0.6 0.0 copy-start
  0.6 2.3 %pack_requests.1 = (f32[8,8,160]{2,1,0:T(8,128)}, s32[1,512]{1,0:T(1,128)}) custom-call(f32[8,512]{1,0:T(8,128)} %far_geom_in.1, s32[1,512]{1,0:T(1,128)} %bitcast.10, s32[1,512]{1,0:T(1,128)} %bitcast.11), custom_call_target="tpu_custom_call" | custom-call | tf_op jit(solution)/shard_map/pack_requests/pallas_call | solution.py:159
  2.9 7.3 %all-to-all-start = ((f32[8,8,160]{2,1,0:T(8,128)}), f32[8,8,160]{2,1,0:T(8,128)S(1)}, u32[]{:S(2)}, u32[]{:S(2)}) async-start(f32[8,8,160]{2,1,0:T(8,128)} %get-tuple-element.8), calls=%async_computation | async-start | bytes 131072 | tf_op jit(solution)/shard_map/all_to_all | solution.py:792
  10.2 0.0 copy-start.2
  10.2 0.0 copy-start.3
  10.3 6.3 %near_payload.1 = (f32[152,128]{1,0:T(8,128)}, f32[8,128]{1,0:T(8,128)}) custom-call(s32[2048]{0:T(1024)} %cell_in.1, f32[4096,128]{1,0:T(8,128)} %fields_ref.1, f32[8,2048]{1,0:T(8,128)} %geom_in.3, s32[1,2048]{1,0:T(1,128)} %bitcast.8, s32[1,512]{1,0:T(1,128)} %bitcast.9, f32[8,512]{1,0:T(8,128)} %far_geom_in.1), custom_call_target="tpu_custom_call" | custom-call | flops 100000000 | bytes 4000000 | tf_op jit(solution)/shard_map/near_payload/pallas_call | solution.py:426
  16.5 0.0 copy-start.4
  16.5 0.0 copy-start.8
  16.5 0.0 copy-start.1
  16.6 0.0 copy-start.5
  16.6 0.0 copy-start.6
  16.6 0.0 copy-start.7
  16.6 0.5 all-to-all-done.request_in
  17.1 0.0 copy-done
  17.1 4.0 %far_spread.1 = f32[8,16,128]{2,1,0:T(8,128)} custom-call(f32[8,8,160]{2,1,0:T(8,128)S(1)} %all-to-all-done.request_in, f32[4096,128]{1,0:T(8,128)S(1)} %copy-done), custom_call_target="tpu_custom_call" | custom-call | flops 40000000 | bytes 4000000 | tf_op jit(solution)/shard_map/far_spread/pallas_call | solution.py:335
  21.1 5.5 %all-to-all-start.1 = ((f32[8,16,128]{2,1,0:T(8,128)}), f32[8,16,128]{2,1,0:T(8,128)S(1)}, u32[]{:S(2)}, u32[]{:S(2)}) async-start(f32[8,16,128]{2,1,0:T(8,128)} %far_spread.1), calls=%async_computation.1 | async-start | bytes 131072 | tf_op jit(solution)/shard_map/all_to_all | solution.py:800
  26.6 0.0 copy-done.4
  26.6 3.8 %collective-permute-start.2 = (f32[152,128]{1,0:T(8,128)S(1)}, f32[152,128]{1,0:T(8,128)S(1)}, u32[]{:S(2)}, u32[]{:S(2)}) collective-permute-start(f32[152,128]{1,0:T(8,128)S(1)} %copy-done.4), channel_id=1, source_target_pairs={{0,24},{4,28},{8,16},{12,20},{16,8},{20,12},{24,0},{28,4},{1,25},{... | collective-permute-start | bytes 233480 | tf_op jit(solution)/shard_map/ppermute | solution.py:762
  30.5 0.0 collective-permute-start.1
  30.5 0.6 %collective-permute-start = (f32[152,128]{1,0:T(8,128)S(1)}, f32[152,128]{1,0:T(8,128)S(1)}, u32[]{:S(2)}, u32[]{:S(2)}) collective-permute-start(f32[152,128]{1,0:T(8,128)S(1)} %copy-done.4), channel_id=1, source_target_pairs={{0,8},{4,12},{8,0},{12,4},{16,24},{20,28},{24,16},{28,20},{1,9},{5... | collective-permute-start | bytes 233480 | tf_op jit(solution)/shard_map/ppermute | solution.py:762
  31.1 0.1 pad_add_fusion.where_ref
  31.2 2.8 %collective-permute-done.2.refs_3_ = f32[152,128]{1,0:T(8,128)S(1)} collective-permute-done((f32[152,128]{1,0:T(8,128)S(1)}, f32[152,128]{1,0:T(8,128)S(1)}, u32[]{:S(2)}, u32[]{:S(2)}) %collective-permute-start.2) | collective-permute-done | bytes 77856 | tf_op jit(solution)/shard_map/ppermute | solution.py:762
  33.9 3.5 %collective-permute-done.1.refs_2_ = f32[152,128]{1,0:T(8,128)S(1)} collective-permute-done((f32[152,128]{1,0:T(8,128)S(1)}, f32[152,128]{1,0:T(8,128)S(1)}, u32[]{:S(2)}, u32[]{:S(2)}) %collective-permute-start.1) | collective-permute-done | bytes 77856 | tf_op jit(solution)/shard_map/ppermute | solution.py:762
  37.4 0.0 collective-permute-done.refs_1_
  37.4 0.0 all-to-all-done.1.spread_ref
  37.4 0.0 copy-done.2
  37.4 0.0 copy-done.3
  37.4 2.6 %join.1 = (f32[544,128]{1,0:T(8,128)S(1)}, f32[4,128]{1,0:T(4,128)}) custom-call(s32[3]{0:T(128)S(1)} %pad_add_fusion.where_ref, f32[8,16,128]{2,1,0:T(8,128)S(1)} %all-to-all-done.1.spread_ref, f32[64,64]{1,0:T(8,128)S(1)} %copy-done.3, f32[128,128]{1,0:T(8,128)S(1)} %copy-done.2, f32[152,128]{1,0:T(8,128)S(1)} %copy-done.4, ...), custom_call_target="tpu_custom_call" | custom-call | tf_op jit(solution)/shard_map/join/pallas_call | solution.py:743
  40.0 1.5 %collective-permute-start.6 = (f32[544,128]{1,0:T(8,128)S(1)}, f32[544,128]{1,0:T(8,128)S(1)}, u32[]{:S(2)}, u32[]{:S(2)}) collective-permute-start(f32[544,128]{1,0:T(8,128)S(1)} %get-tuple-element.13.rest_0_), channel_id=1, source_target_pairs={{0,4},{4,0},{8,12},{12,8},{16,20},{20,16},{24,28},{28,24},{1,5},{5... | collective-permute-start | bytes 835592 | tf_op jit(solution)/shard_map/ppermute | solution.py:762
  41.5 1.5 %collective-permute-start.4 = (f32[544,128]{1,0:T(8,128)S(1)}, f32[544,128]{1,0:T(8,128)S(1)}, u32[]{:S(2)}, u32[]{:S(2)}) collective-permute-start(f32[544,128]{1,0:T(8,128)S(1)} %get-tuple-element.13.rest_0_), channel_id=1, source_target_pairs={{0,2},{1,3},{2,0},{3,1},{4,6},{5,7},{6,4},{7,5},{8,10},{9,11},{10,... | collective-permute-start | bytes 835592 | tf_op jit(solution)/shard_map/ppermute | solution.py:762
  43.0 0.0 collective-permute-start.3
  43.0 4.2 %collective-permute-done.6.rest_4_ = f32[544,128]{1,0:T(8,128)S(1)} collective-permute-done((f32[544,128]{1,0:T(8,128)S(1)}, f32[544,128]{1,0:T(8,128)S(1)}, u32[]{:S(2)}, u32[]{:S(2)}) %collective-permute-start.6) | collective-permute-done | bytes 278560 | tf_op jit(solution)/shard_map/ppermute | solution.py:762
  47.2 1.6 %collective-permute-start.8 = (f32[272,128]{1,0:T(8,128)S(1)}, f32[272,128]{1,0:T(8,128)S(1)}, u32[]{:S(2)}, u32[]{:S(2)}) collective-permute-start(f32[272,128]{1,0:T(8,128)S(1)} %slice.8), channel_id=1, source_target_pairs={{0,2},{1,3},{2,0},{3,1},{4,6},{5,7},{6,4},{7,5},{8,10},{9,11},{10,... | collective-permute-start | bytes 417800 | tf_op jit(solution)/shard_map/ppermute | solution.py:762
  48.8 0.3 collective-permute-done.4.rest_2_
  49.1 1.2 %collective-permute-start.9 = (f32[272,128]{1,0:T(8,128)S(1)}, f32[272,128]{1,0:T(8,128)S(1)}, u32[]{:S(2)}, u32[]{:S(2)}) collective-permute-start(f32[272,128]{1,0:T(8,128)S(1)} %slice.9), channel_id=1, source_target_pairs={{0,4},{4,0},{8,12},{12,8},{16,20},{20,16},{24,28},{28,24},{1,5},{5... | collective-permute-start | bytes 417800 | tf_op jit(solution)/shard_map/ppermute | solution.py:762
  50.3 0.0 collective-permute-start.7
  50.3 0.5 collective-permute-start.5
  50.8 1.5 %collective-permute-done.8.rest_6_ = f32[272,128]{1,0:T(8,128)S(1)} collective-permute-done((f32[272,128]{1,0:T(8,128)S(1)}, f32[272,128]{1,0:T(8,128)S(1)}, u32[]{:S(2)}, u32[]{:S(2)}) %collective-permute-start.8) | collective-permute-done | bytes 139296 | tf_op jit(solution)/shard_map/ppermute | solution.py:762
  52.3 0.0 collective-permute-start.10
  52.3 1.9 %collective-permute-done.9.rest_7_ = f32[272,128]{1,0:T(8,128)S(1)} collective-permute-done((f32[272,128]{1,0:T(8,128)S(1)}, f32[272,128]{1,0:T(8,128)S(1)}, u32[]{:S(2)}, u32[]{:S(2)}) %collective-permute-start.9) | collective-permute-done | bytes 139296 | tf_op jit(solution)/shard_map/ppermute | solution.py:762
  54.3 0.0 collective-permute-start.11
  54.3 0.0 copy-done.8
  54.3 0.1 copy.17.adj_ref
  54.4 0.0 collective-permute-done.3.rest_1_
  54.4 0.0 collective-permute-done.10.rest_8_
  54.4 0.0 collective-permute-done.7.rest_5_
  54.4 1.2 %collective-permute-done.11.rest_9_ = f32[272,128]{1,0:T(8,128)S(1)} collective-permute-done((f32[272,128]{1,0:T(8,128)S(1)}, f32[272,128]{1,0:T(8,128)S(1)}, u32[]{:S(2)}, u32[]{:S(2)}) %collective-permute-start.11) | collective-permute-done | bytes 139296 | tf_op jit(solution)/shard_map/ppermute | solution.py:762
  55.6 0.0 collective-permute-done.5.rest_3_
  55.6 0.0 copy-done.1
  55.6 0.0 copy-done.5
  55.6 0.0 copy-done.6
  55.6 0.0 copy-done.7
  55.7 6.6 %smooth.1 = f32[24,64,64]{2,1,0:T(8,128)} custom-call(s32[3]{0:T(128)S(1)} %pad_add_fusion.where_ref, s32[96,4]{1,0:T(8,128)S(1)} %copy.17.adj_ref, f32[256,512]{1,0:T(8,128)S(1)} %copy-done.1, f32[64,64]{1,0:T(8,128)S(1)} %copy-done.3, f32[128,128]{1,0:T(8,128)S(1)} %copy-done.2, f32[64,128]{1,0:T(8,128)S(1)} %copy-done.5, f32[8,64]{1,0:T(8,128)S(1)} %copy-done.7, ...), custom_call_target="tpu_custom_call" | custom-call | tf_op jit(solution)/shard_map/smooth/pallas_call | solution.py:687
  (2 shorter events, 0.0 us)
Async XLA Ops:
  0.6 16.5 %copy-start = (f32[4096,128]{1,0:T(8,128)S(1)}, f32[4096,128]{1,0:T(8,128)}, u32[]{:S(2)}) copy-start(f32[4096,128]{1,0:T(8,128)} %fields_ref.1) | copy-start | bytes 6291460
  2.9 14.2 %all-to-all-start = ((f32[8,8,160]{2,1,0:T(8,128)}), f32[8,8,160]{2,1,0:T(8,128)S(1)}, u32[]{:S(2)}, u32[]{:S(2)}) async-start(f32[8,8,160]{2,1,0:T(8,128)} %get-tuple-element.8), calls=%async_computation | async-start | bytes 131072 | tf_op jit(solution)/shard_map/all_to_all | solution.py:792
  10.2 27.2 %copy-start.2 = (f32[128,128]{1,0:T(8,128)S(1)}, f32[128,128]{1,0:T(8,128)}, u32[]{:S(2)}) copy-start(f32[128,128]{1,0:T(8,128)} %constant.35.clone.pair_ref) | copy-start | bytes 196612
  10.2 27.2 %copy-start.3 = (f32[64,64]{1,0:T(8,128)S(1)}, f32[64,64]{1,0:T(8,128)}, u32[]{:S(2)}) copy-start(f32[64,64]{1,0:T(8,128)} %constant.34.clone.basis_ref) | copy-start | bytes 49156
  16.5 10.1 %copy-start.4 = (f32[152,128]{1,0:T(8,128)S(1)}, f32[152,128]{1,0:T(8,128)}, u32[]{:S(2)}) copy-start(f32[152,128]{1,0:T(8,128)} %get-tuple-element.11.refs_0_) | copy-start | bytes 233476
  16.5 37.7 %copy-start.8 = (s32[96,4]{0,1:T(4,128)S(1)}, s32[96,4]{0,1:T(4,128)}, u32[]{:S(2)}) copy-start(s32[96,4]{0,1:T(4,128)} %param.23) | copy-start | bytes 4612
  16.5 39.1 %copy-start.1 = (f32[256,512]{1,0:T(8,128)S(1)}, f32[256,512]{1,0:T(8,128)}, u32[]{:S(2)}) copy-start(f32[256,512]{1,0:T(8,128)} %constant.39.clone.coupling_ref) | copy-start | bytes 1572868
  16.6 39.1 %copy-start.5 = (f32[64,128]{1,0:T(8,128)S(1)}, f32[64,128]{1,0:T(8,128)}, u32[]{:S(2)}) copy-start(f32[64,128]{1,0:T(8,128)} %constant.38.clone.series_ref) | copy-start | bytes 98308
  16.6 39.1 %copy-start.6 = (f32[8,128]{1,0:T(8,128)S(1)}, f32[8,128]{1,0:T(8,128)}, u32[]{:S(2)}) copy-start(f32[8,128]{1,0:T(8,128)} %constant.37.clone.scale_ref) | copy-start | bytes 12292
  16.6 39.1 %copy-start.7 = (f32[8,64]{1,0:T(8,128)S(1)}, f32[8,64]{1,0:T(8,128)}, u32[]{:S(2)}) copy-start(f32[8,64]{1,0:T(8,128)} %constant.36.clone.edge_ref) | copy-start | bytes 6148
  21.1 16.3 %all-to-all-start.1 = ((f32[8,16,128]{2,1,0:T(8,128)}), f32[8,16,128]{2,1,0:T(8,128)S(1)}, u32[]{:S(2)}, u32[]{:S(2)}) async-start(f32[8,16,128]{2,1,0:T(8,128)} %far_spread.1), calls=%async_computation.1 | async-start | bytes 131072 | tf_op jit(solution)/shard_map/all_to_all | solution.py:800
  26.6 7.3 %collective-permute-start.2 = (f32[152,128]{1,0:T(8,128)S(1)}, f32[152,128]{1,0:T(8,128)S(1)}, u32[]{:S(2)}, u32[]{:S(2)}) collective-permute-start(f32[152,128]{1,0:T(8,128)S(1)} %copy-done.4), channel_id=1, source_target_pairs={{0,24},{4,28},{8,16},{12,20},{16,8},{20,12},{24,0},{28,4},{1,25},{... | collective-permute-start | bytes 233480 | tf_op jit(solution)/shard_map/ppermute | solution.py:762
  30.5 6.9 %collective-permute-start.1 = (f32[152,128]{1,0:T(8,128)S(1)}, f32[152,128]{1,0:T(8,128)S(1)}, u32[]{:S(2)}, u32[]{:S(2)}) collective-permute-start(f32[152,128]{1,0:T(8,128)S(1)} %copy-done.4), channel_id=1, source_target_pairs={{0,16},{4,20},{8,24},{12,28},{16,0},{20,4},{24,8},{28,12},{1,17},{... | collective-permute-start | bytes 233480 | tf_op jit(solution)/shard_map/ppermute | solution.py:762
  30.5 6.9 %collective-permute-start = (f32[152,128]{1,0:T(8,128)S(1)}, f32[152,128]{1,0:T(8,128)S(1)}, u32[]{:S(2)}, u32[]{:S(2)}) collective-permute-start(f32[152,128]{1,0:T(8,128)S(1)} %copy-done.4), channel_id=1, source_target_pairs={{0,8},{4,12},{8,0},{12,4},{16,24},{20,28},{24,16},{28,20},{1,9},{5... | collective-permute-start | bytes 233480 | tf_op jit(solution)/shard_map/ppermute | solution.py:762
  40.0 7.2 %collective-permute-start.6 = (f32[544,128]{1,0:T(8,128)S(1)}, f32[544,128]{1,0:T(8,128)S(1)}, u32[]{:S(2)}, u32[]{:S(2)}) collective-permute-start(f32[544,128]{1,0:T(8,128)S(1)} %get-tuple-element.13.rest_0_), channel_id=1, source_target_pairs={{0,4},{4,0},{8,12},{12,8},{16,20},{20,16},{24,28},{28,24},{1,5},{5... | collective-permute-start | bytes 835592 | tf_op jit(solution)/shard_map/ppermute | solution.py:762
  41.5 7.6 %collective-permute-start.4 = (f32[544,128]{1,0:T(8,128)S(1)}, f32[544,128]{1,0:T(8,128)S(1)}, u32[]{:S(2)}, u32[]{:S(2)}) collective-permute-start(f32[544,128]{1,0:T(8,128)S(1)} %get-tuple-element.13.rest_0_), channel_id=1, source_target_pairs={{0,2},{1,3},{2,0},{3,1},{4,6},{5,7},{6,4},{7,5},{8,10},{9,11},{10,... | collective-permute-start | bytes 835592 | tf_op jit(solution)/shard_map/ppermute | solution.py:762
  43.0 11.4 %collective-permute-start.3 = (f32[544,128]{1,0:T(8,128)S(1)}, f32[544,128]{1,0:T(8,128)S(1)}, u32[]{:S(2)}, u32[]{:S(2)}) collective-permute-start(f32[544,128]{1,0:T(8,128)S(1)} %get-tuple-element.13.rest_0_), channel_id=1, source_target_pairs={{0,1},{1,0},{2,3},{3,2},{4,5},{5,4},{6,7},{7,6},{8,9},{9,8},{10,11... | collective-permute-start | bytes 835592 | tf_op jit(solution)/shard_map/ppermute | solution.py:762
  47.2 5.1 %collective-permute-start.8 = (f32[272,128]{1,0:T(8,128)S(1)}, f32[272,128]{1,0:T(8,128)S(1)}, u32[]{:S(2)}, u32[]{:S(2)}) collective-permute-start(f32[272,128]{1,0:T(8,128)S(1)} %slice.8), channel_id=1, source_target_pairs={{0,2},{1,3},{2,0},{3,1},{4,6},{5,7},{6,4},{7,5},{8,10},{9,11},{10,... | collective-permute-start | bytes 417800 | tf_op jit(solution)/shard_map/ppermute | solution.py:762
  49.1 5.1 %collective-permute-start.9 = (f32[272,128]{1,0:T(8,128)S(1)}, f32[272,128]{1,0:T(8,128)S(1)}, u32[]{:S(2)}, u32[]{:S(2)}) collective-permute-start(f32[272,128]{1,0:T(8,128)S(1)} %slice.9), channel_id=1, source_target_pairs={{0,4},{4,0},{8,12},{12,8},{16,20},{20,16},{24,28},{28,24},{1,5},{5... | collective-permute-start | bytes 417800 | tf_op jit(solution)/shard_map/ppermute | solution.py:762
  50.3 4.1 %collective-permute-start.7 = (f32[544,128]{1,0:T(8,128)S(1)}, f32[544,128]{1,0:T(8,128)S(1)}, u32[]{:S(2)}, u32[]{:S(2)}) collective-permute-start(f32[544,128]{1,0:T(8,128)S(1)} %collective-permute-done.6.rest_4_), channel_id=1, source_target_pairs={{0,1},{1,0},{2,3},{3,2},{4,5},{5,4},{6,7},{7,6},{8,9},{9,8},{10,11... | collective-permute-start | bytes 835592 | tf_op jit(solution)/shard_map/ppermute | solution.py:762
  50.3 5.3 %collective-permute-start.5 = (f32[544,128]{1,0:T(8,128)S(1)}, f32[544,128]{1,0:T(8,128)S(1)}, u32[]{:S(2)}, u32[]{:S(2)}) collective-permute-start(f32[544,128]{1,0:T(8,128)S(1)} %collective-permute-done.4.rest_2_), channel_id=1, source_target_pairs={{0,1},{1,0},{2,3},{3,2},{4,5},{5,4},{6,7},{7,6},{8,9},{9,8},{10,11... | collective-permute-start | bytes 835592 | tf_op jit(solution)/shard_map/ppermute | solution.py:762
  52.3 2.0 %collective-permute-start.10 = (f32[272,128]{1,0:T(8,128)S(1)}, f32[272,128]{1,0:T(8,128)S(1)}, u32[]{:S(2)}, u32[]{:S(2)}) collective-permute-start(f32[272,128]{1,0:T(8,128)S(1)} %collective-permute-done.8.rest_6_), channel_id=1, source_target_pairs={{0,1},{1,0},{2,3},{3,2},{4,5},{5,4},{6,7},{7,6},{8,9},{9,8},{10,11... | collective-permute-start | bytes 417800 | tf_op jit(solution)/shard_map/ppermute | solution.py:762
  54.3 1.4 %collective-permute-start.11 = (f32[272,128]{1,0:T(8,128)S(1)}, f32[272,128]{1,0:T(8,128)S(1)}, u32[]{:S(2)}, u32[]{:S(2)}) collective-permute-start(f32[272,128]{1,0:T(8,128)S(1)} %collective-permute-done.9.rest_7_), channel_id=1, source_target_pairs={{0,1},{1,0},{2,3},{3,2},{4,5},{5,4},{6,7},{7,6},{8,9},{9,8},{10,11... | collective-permute-start | bytes 417800 | tf_op jit(solution)/shard_map/ppermute | solution.py:762

commit v6 on v5

--- a/solution.py
+++ b/solution.py
@@ -18,7 +18,6 @@
 PAYLOAD_ROWS = GRID_ROWS + 2 * GROUP
 LINES = 4
 CHUNKS = 3
-NEAR_ROWS = PAYLOAD_ROWS + 4 * LINES
 F32 = jnp.float32
 BF16 = jnp.bfloat16
 EXACT = lax.Precision.HIGHEST
@@ -130,8 +129,20 @@
         copy.wait()
 
 
-def pack_kernel(capacity, geom_in, block_in, cell_in, request_ref, place_ref, geom_ref, block_ref, cell_ref, sem):
-    fetch([(geom_in, geom_ref), (block_in, block_ref), (cell_in, cell_ref)], sem)
+def pack_kernel(
+    capacity, geom_in, block_in, cell_in, near_in, far_in, request_ref, place_ref, slot_ref,
+    geom_ref, block_ref, cell_ref, near_ref, far_ref, sem,
+):
+    fetch([(geom_in, geom_ref), (block_in, block_ref), (cell_in, cell_ref), (near_in, near_ref), (far_in, far_ref)], sem)
+    near, far = near_ref[...].astype(F32), far_ref[...].astype(F32)
+    slots = []
+    last = jnp.full((1, 1), -1.0, F32)
+    for _ in range(GROUP):
+        a = jnp.min(jnp.where(near > last, near, NO_PATCH), axis=1, keepdims=True)
+        b = jnp.min(jnp.where(far > last, far, NO_PATCH), axis=1, keepdims=True)
+        last = jnp.minimum(a, b)
+        slots.append(jnp.broadcast_to(last, (1, LANES)))
+    slot_ref[...] = jnp.concatenate(slots + slots, 0)
     owners = request_ref.shape[0]
     count = geom_ref.shape[1]
     block = block_ref[...]
@@ -151,28 +162,37 @@
     packed = nt(parts, put)
     packed = (packed[16:24] + packed[8:16]) + packed[0:8]
     for owner in range(owners):
-        request_ref[owner] = packed[:, owner * capacity : (owner + 1) * capacity]
-
-
-def pack_requests(far_geom, far_block, far_cell, owners, capacity):
+        request_ref[owner, 0:8, :] = packed[:, owner * capacity : (owner + 1) * capacity]
+    if request_ref.shape[1] > 8:
+        own = [in_rows(x) for x in (geom_ref[6:7, :], geom_ref[7:8, :], far)] + [slot_ref[0:GROUP, :]]
+        own = jnp.concatenate(own, 0)
+        for owner in range(owners):
+            request_ref[owner, 8:, 0:LANES] = own
+            request_ref[owner, 8:, LANES:] = jnp.zeros((own.shape[0], capacity - LANES), F32)
+
+
+def pack_requests(far_geom, far_block, far_cell, near_patch, far_patch, owners, capacity, staged):
     count = far_geom.shape[1]
     return pl.pallas_call(
         functools.partial(pack_kernel, capacity),
         out_shape=(
-            jax.ShapeDtypeStruct((owners, 8, capacity), F32),
+            jax.ShapeDtypeStruct((owners, 8 + staged * (3 * LINES + GROUP), capacity), F32),
             jax.ShapeDtypeStruct((1, count), jnp.int32),
+            jax.ShapeDtypeStruct((8, LANES), F32),
         ),
-        in_specs=[HBM] * 3,
-        out_specs=(VMEM, VMEM),
+        in_specs=[HBM] * 5,
+        out_specs=(VMEM, VMEM, VMEM),
         scratch_shapes=[
             pltpu.VMEM((8, count), F32),
             pltpu.VMEM((1, count), jnp.int32),
             pltpu.VMEM((1, count), jnp.int32),
-            pltpu.SemaphoreType.DMA((3,)),
+            pltpu.VMEM(near_patch.shape, jnp.int32),
+            pltpu.VMEM(far_patch.shape, jnp.int32),
+            pltpu.SemaphoreType.DMA((5,)),
         ],
         compiler_params=params(60),
         name="pack_requests",
-    )(far_geom, far_block, far_cell)
+    )(far_geom, far_block, far_cell, near_patch, far_patch)
 
 
 def gather_rows(cells, fields_ref, rows_ref, count):
@@ -257,7 +277,7 @@
 def far_densities(request_in, fields_ref, request_ref, query_ref, cell_v, cell_s, rows_ref, dens_ref, sems, sem):
     owners, _, capacity = request_in.shape
     count = owners * capacity
-    fetch([(request_in, request_ref)], sems)
+    fetch([(request_in.at[:, pl.ds(0, 8), :], request_ref)], sems)
     for o in range(owners):
         query_ref[:, o * capacity : (o + 1) * capacity] = request_ref[o]
     cell_v[...] = query_ref[6:7, :].astype(jnp.int32)
@@ -306,7 +326,7 @@
     owners, _, capacity = requests.shape
     count = owners * capacity
     return [
-        pltpu.VMEM(requests.shape, F32),
+        pltpu.VMEM((owners, 8, capacity), F32),
         pltpu.VMEM((8, count), F32),
         pltpu.VMEM((1, count), jnp.int32),
         pltpu.SMEM((1, count), jnp.int32),
@@ -390,63 +410,48 @@
 
 
 def near_payload_kernel(
-    cell_in, fields_in, geom_in, near_in, far_in, far_geom_in, out_ref, slot_ref,
-    near_ref, far_ref, far_geom_ref, dens_ref, cell_ref, fields_ref, geom_ref, rows_ref, more, sem,
+    cell_in, fields_in, geom_in, near_in, slot_in, out_ref,
+    near_ref, slot_ref, dens_ref, cell_ref, fields_ref, geom_ref, rows_ref, more, sem,
 ):
-    others = [(near_in, near_ref), (far_in, far_ref), (far_geom_in, far_geom_ref)]
+    others = [(near_in, near_ref), (slot_in, slot_ref)]
     others = [pltpu.make_async_copy(a, b, more.at[i]) for i, (a, b) in enumerate(others)]
     for copy in others:
         copy.start()
     near_kernel(0, cell_in, fields_in, geom_in, dens_ref, cell_ref, fields_ref, geom_ref, rows_ref, sem)
     for copy in others:
         copy.wait()
-    near, far = near_ref[...].astype(F32), far_ref[...].astype(F32)
-    slots = []
-    last = jnp.full((1, 1), -1.0, F32)
-    for _ in range(GROUP):
-        a = jnp.min(jnp.where(near > last, near, NO_PATCH), axis=1, keepdims=True)
-        b = jnp.min(jnp.where(far > last, far, NO_PATCH), axis=1, keepdims=True)
-        last = jnp.minimum(a, b)
-        slots.append(last)
+    slots = [slot_ref[s : s + 1, 0:1] for s in range(GROUP)]
+    near = near_ref[...].astype(F32)
     grids = slot_grids(dens_ref[...], geom_ref[6:7, :], geom_ref[7:8, :], near, slots)
     lane = iota((1, LANES), 1)
     names = jnp.zeros((1, LANES), F32)
     for s in range(GROUP):
         names = jnp.where(lane == s, slots[s], names)
-    slots = [jnp.broadcast_to(s, (1, LANES)) for s in slots]
-    slot_ref[...] = jnp.concatenate(slots + slots, 0)
-    out_ref[0:PAYLOAD_ROWS, :] = jnp.concatenate(side_by_side(grids) + slots + [names] * GROUP, 0)
-    if out_ref.shape[0] > PAYLOAD_ROWS:
-        held = [in_rows(x) for x in (far_geom_ref[6:7, :], far_geom_ref[7:8, :], far)]
-        out_ref[PAYLOAD_ROWS:, :] = jnp.concatenate(held + [jnp.zeros((LINES, LANES), F32)], 0)
-
-
-def near_payload(near_cell, fields, near_geom, near_patch, far_patch, far_geom, rows):
+    out_ref[...] = jnp.concatenate(side_by_side(grids) + [slot_ref[0:GROUP, :]] + [names] * GROUP, 0)
+
+
+def near_payload(near_cell, fields, near_geom, near_patch, slots):
     count = near_geom.shape[1]
     return pl.pallas_call(
         near_payload_kernel,
-        out_shape=(
-            jax.ShapeDtypeStruct((rows, LANES), F32),
-            jax.ShapeDtypeStruct((8, LANES), F32),
-        ),
-        in_specs=[HBM] * 6,
-        out_specs=(VMEM, VMEM),
+        out_shape=jax.ShapeDtypeStruct((PAYLOAD_ROWS, LANES), F32),
+        in_specs=[HBM] * 5,
+        out_specs=VMEM,
         scratch_shapes=[
             pltpu.VMEM(near_patch.shape, jnp.int32),
-            pltpu.VMEM(far_patch.shape, jnp.int32),
-            pltpu.VMEM(far_geom.shape, F32),
+            pltpu.VMEM(slots.shape, F32),
             pltpu.VMEM((1, count), F32),
             pltpu.SMEM((count,), jnp.int32),
             pltpu.VMEM(fields.shape, F32),
             pltpu.VMEM((8, count), F32),
             pltpu.VMEM((count, LANES), F32),
-            pltpu.SemaphoreType.DMA((3,)),
+            pltpu.SemaphoreType.DMA((2,)),
             pltpu.SemaphoreType.DMA((3,)),
         ],
         compiler_params=params(60),
         cost_estimate=pl.CostEstimate(flops=100_000_000, bytes_accessed=4_000_000, transcendentals=0),
         name="near_payload",
-    )(near_cell, fields, near_geom, near_patch, far_patch, far_geom)
+    )(near_cell, fields, near_geom, near_patch, slots)
 
 
 def to_spectral(blocks, basis, basis_pair):
@@ -710,28 +715,49 @@
     )
 
 
-def join_kernel(where_ref, spread_ref, basis_ref, pair_ref, *refs):
-    *parts, out_ref, own_ref, total_ref, near_ref = refs
-    z_at = where_ref[2] // 2
+def far_line_kernel(where_ref, spread_ref, asked_ref, out_ref, own_ref, total_ref):
+    owners = spread_ref.shape[0]
+    line = owners // 2
     total = spread_ref[0]
-    for o in range(1, spread_ref.shape[0]):
+    for o in range(1, owners):
         total = total + spread_ref[o]
     total_ref[...] = total
-    own_ref[...] = total_ref[pl.ds(z_at * LINES, LINES), :]
-    for k, part in enumerate(parts):
-        near_ref[z_at ^ k] = part[...]
-    blocks = []
-    for z in range(len(parts)):
-        part = near_ref.at[z]
-        dens = total_ref[z * LINES : (z + 1) * LINES, :]
-        s, t, patch = [part[PAYLOAD_ROWS + i * LINES : PAYLOAD_ROWS + (i + 1) * LINES, :] for i in range(3)]
+    own_ref[...] = total_ref[pl.ds(where_ref[2] // 2 * LINES, LINES), :]
+    for z in range(line):
+        dens = total[z * LINES : (z + 1) * LINES]
+        held = asked_ref[2 * z + where_ref[1], 8:, 0:LANES]
+        s, t, patch = [held[i * LINES : (i + 1) * LINES] for i in range(3)]
         start_s, weights_s = spline_weights(s)
         start_t, weights_t = spline_weights(t)
         left = spline_columns(in_line(start_s), [in_line(w) for w in weights_s])
         right = spline_columns(in_line(start_t), [in_line(w * dens) for w in weights_t])
-        slots = [part[GRID_ROWS + i : GRID_ROWS + i + 1, 0:1] for i in range(GROUP)]
+        slots = [held[3 * LINES + i : 3 * LINES + i + 1, 0:1] for i in range(GROUP)]
         far = side_by_side(grids_of(left, right, in_line(patch), slots))
-        blocks.append(part[0:GRID_ROWS, :] + jnp.concatenate(far, 0))
+        out_ref[z * GRID_ROWS : (z + 1) * GRID_ROWS, :] = jnp.concatenate(far, 0)
+
+
+def far_line(spread, asked, where):
+    line = spread.shape[0] // 2
+    return pl.pallas_call(
+        far_line_kernel,
+        out_shape=(
+            jax.ShapeDtypeStruct((line * GRID_ROWS, LANES), F32),
+            jax.ShapeDtypeStruct((LINES, LANES), F32),
+        ),
+        in_specs=[SMEM, VMEM, VMEM],
+        out_specs=(VMEM, VMEM),
+        scratch_shapes=[pltpu.VMEM((line * LINES, LANES), F32)],
+        compiler_params=params(16),
+        cost_estimate=pl.CostEstimate(flops=100_000_000, bytes_accessed=1_000_000, transcendentals=0),
+        name="far_line",
+    )(where, spread, asked)
+
+
+def join_kernel(where_ref, far_ref, basis_ref, pair_ref, *refs):
+    *parts, out_ref, near_ref = refs
+    for k, part in enumerate(parts):
+        near_ref[where_ref[2] // 2 ^ k] = part[...]
+    blocks = [near_ref[z, 0:GRID_ROWS, :] + far_ref[z * GRID_ROWS : (z + 1) * GRID_ROWS, :] for z in range(len(parts))]
     blocks = to_spectral(jnp.concatenate(blocks, 0), basis_ref[...], pair_ref[...])
     for z in range(len(parts)):
         at = z * PAYLOAD_ROWS
@@ -739,22 +765,16 @@
         out_ref[at + GRID_ROWS : at + PAYLOAD_ROWS, :] = near_ref[z, GRID_ROWS:PAYLOAD_ROWS, :]
 
 
-def join(parts, spread, where, const):
+def join(parts, far, where, const):
     return pl.pallas_call(
         join_kernel,
-        out_shape=(
-            jax.ShapeDtypeStruct((len(parts) * PAYLOAD_ROWS, LANES), F32),
-            jax.ShapeDtypeStruct((LINES, LANES), F32),
-        ),
+        out_shape=jax.ShapeDtypeStruct((len(parts) * PAYLOAD_ROWS, LANES), F32),
         in_specs=[SMEM, VMEM, WHOLE, WHOLE] + [VMEM] * len(parts),
-        out_specs=(VMEM, VMEM),
-        scratch_shapes=[
-            pltpu.VMEM((len(parts) * LINES, LANES), F32),
-            pltpu.VMEM((len(parts), NEAR_ROWS, LANES), F32),
-        ],
+        out_specs=VMEM,
+        scratch_shapes=[pltpu.VMEM((len(parts), PAYLOAD_ROWS, LANES), F32)],
         compiler_params=params(16),
         name="join",
-    )(where, spread, const["basis"], const["basis_pair"], *parts)
+    )(where, far, const["basis"], const["basis_pair"], *parts)
 
 
 def over(axis, array, bit):
@@ -786,20 +806,19 @@
     staged = vol_count == 8 and dsg_count == 4 and far_count == LINES * LANES
     vol_at = lax.axis_index("vol")
     where = jnp.stack([lax.axis_index("dsg"), vol_at % 2 if staged else 0, vol_at]).astype(jnp.int32)
-    request, place = pack_requests(
-        far_geom, far_block.reshape(1, -1), far_cell.reshape(1, -1), vol_count, capacity
+    near_patch, far_patch = near_patch.reshape(1, -1), far_patch.reshape(1, -1)
+    request, place, slots = pack_requests(
+        far_geom, far_block.reshape(1, -1), far_cell.reshape(1, -1), near_patch, far_patch, vol_count, capacity, staged
     )
     asked = lax.all_to_all(request, "vol", split_axis=0, concat_axis=0, tiled=True)
-    near_patch, far_patch = near_patch.reshape(1, -1), far_patch.reshape(1, -1)
-    near, slots = near_payload(
-        near_cell, fields, near_geom, near_patch, far_patch, far_geom, NEAR_ROWS if staged else PAYLOAD_ROWS
-    )
-    asked, near, slots = lax.optimization_barrier((asked, near, slots))
+    near = near_payload(near_cell, fields, near_geom, near_patch, slots)
+    asked, near = lax.optimization_barrier((asked, near))
     if staged:
         spread = far_spread(asked, fields)
         spread = lax.all_to_all(spread, "vol", split_axis=0, concat_axis=0, tiled=True)
         parts = [near] + [over("vol", near, 2 * k) for k in (1, 2, 3)]
-        here, far_dens = join(parts, spread, where, const)
+        far, far_dens = far_line(spread, asked, where)
+        here = join(parts, far, where, const)
         arrays, items = gather_in_plane(here)
     else:
         reply = lax.all_to_all(far_answers(asked, fields), "vol", split_axis=0, concat_axis=0, tiled=True)

time: 62.6 us -> 60.2 us (0.962)
  waiting for transfers between devices: 16 us -> 14.3 us
  starting transfers between devices: 23.5 us -> 22.4 us
    ppermute x12, waiting for transfers between devices: 15.4 us -> 9.6 us  [over(): return lax.ppermute(array, axis, [(i, i ^ bit) for i in range(count)])]
    all_to_all x1, waiting for transfers between devices: 0.01 us -> 2.82 us  [per_device(): lax.all_to_all(spread, 'vol', split_axis=0, concat_axis=0, tiled=True)]
    all_to_all x1, starting transfers between devices: 5.49 us -> 4.16 us  [per_device(): lax.all_to_all(spread, 'vol', split_axis=0, concat_axis=0, tiled=True)]
    all_to_all x1, waiting for transfers between devices: 0.54 us -> 1.85 us  [per_device(): lax.all_to_all(request, 'vol', split_axis=0, concat_axis=0, tiled=True)]
    pallas_call x2 -> x3, Pallas kernels: 8.85 us -> 9.25 us  [the longest x1 6 us: near_payload(): pl.pallas_call(near_payload_kernel, out_shape=jax.ShapeDtypeStruct((PAYLO...]
  transfers between devices with their start and end apart: 14 -> 14, of which waited for: 8 -> 8; matrix products, arithmetic and copies ran while one was open for 0% -> 0% of each run, Pallas kernels for 10% -> 13%
where the time goes in v6:
time: 60.2 us; the launch traced here: 59.9 us
  starting transfers between devices  22.4 us (37%)
  Pallas kernels  22.2 us (37%)
  waiting for transfers between devices  14.3 us (24%)
  between operations  0.8 us (1%)
    ppermute x12, starting transfers between devices, over(): return lax.ppermute(array, axis, [(i, i ^ bit) for i in range(count)])  10.9 us
    ppermute x12, waiting for transfers between devices, over(): return lax.ppermute(array, axis, [(i, i ^ bit) for i in range(count)])  9.6 us
    all_to_all x1, starting transfers between devices, per_device(): lax.all_to_all(request, 'vol', split_axis=0, concat_axis=0, tiled=True)  7.29 us
    pallas_call x1, Pallas kernels, smooth(): pl.pallas_call(functools.partial(smooth_kernel, items, per_owner), out_sh...  6.57 us
    pallas_call x1, Pallas kernels, near_payload(): pl.pallas_call(near_payload_kernel, out_shape=jax.ShapeDtypeStruct((PAYLO...  6 us
    all_to_all x1, starting transfers between devices, per_device(): lax.all_to_all(spread, 'vol', split_axis=0, concat_axis=0, tiled=True)  4.16 us
    pallas_call x1, Pallas kernels, far_spread(): pl.pallas_call(far_spread_kernel, out_shape=jax.ShapeDtypeStruct((owners,...  3.96 us
    all_to_all x1, waiting for transfers between devices, per_device(): lax.all_to_all(spread, 'vol', split_axis=0, concat_axis=0, tiled=True)  2.82 us
  transfers between devices with their start and end apart: 14, of which 8 were waited for; matrix products, arithmetic and copies ran while one was open for 0% of the time, Pallas kernels for 13%

profile of v6, /device:TPU:0, one launch (start us, length us, event | category | flops | bytes accessed | tf_op | source)
XLA Modules:
  0.0 59.9 jit_solution(14359595400352718308)
XLA Ops:
  0.6 0.0 copy-start
  0.6 2.4 %pack_requests.1 = (f32[8,24,160]{2,1,0:T(8,128)}, s32[1,512]{1,0:T(1,128)}, f32[8,128]{1,0:T(8,128)}) custom-call(f32[8,512]{1,0:T(8,128)} %geom_in.2, s32[1,512]{1,0:T(1,128)} %bitcast.10, s32[1,512]{1,0:T(1,128)} %bitcast.11, s32[1,2048]{1,0:T(1,128)} %bitcast.8, s32[1,512]{1,0:T(1,128)} %bitcast.12), custom_call_target="tpu_custom_call" | custom-call | tf_op jit(solution)/shard_map/pack_requests/pallas_call | solution.py:176
  3.1 7.3 %all-to-all-start = ((f32[8,24,160]{2,1,0:T(8,128)}), f32[8,24,160]{2,1,0:T(8,128)S(1)}, u32[]{:S(2)}, u32[]{:S(2)}) async-start(f32[8,24,160]{2,1,0:T(8,128)} %get-tuple-element.8), calls=%async_computation | async-start | bytes 393216 | tf_op jit(solution)/shard_map/all_to_all | solution.py:813
  10.4 0.0 copy-start.3
  10.4 0.0 copy-start.4
  10.4 6.0 %near_payload.1.refs_0_ = f32[136,128]{1,0:T(8,128)} custom-call(s32[2048]{0:T(1024)} %cell_in.1, f32[4096,128]{1,0:T(8,128)} %fields_ref.1, f32[8,2048]{1,0:T(8,128)} %geom_in.3, s32[1,2048]{1,0:T(1,128)} %bitcast.9, f32[8,128]{1,0:T(8,128)} %get-tuple-element.9.slot_in), custom_call_target="tpu_custom_call" | custom-call | flops 100000000 | bytes 4000000 | tf_op jit(solution)/shard_map/near_payload/pallas_call | solution.py:435
  16.4 0.0 copy-start.2
  16.4 0.0 copy-start.8
  16.4 0.0 copy-start.1
  16.4 0.0 copy-start.5
  16.4 0.0 copy-start.6
  16.4 0.0 copy-start.7
  16.5 1.9 %all-to-all-done.request_in.asked_ref = f32[8,24,160]{2,1,0:T(8,128)S(1)} async-done(((f32[8,24,160]{2,1,0:T(8,128)}), f32[8,24,160]{2,1,0:T(8,128)S(1)}, u32[]{:S(2)}, u32[]{:S(2)}) %all-to-all-start) | async-done | bytes 122912 | tf_op jit(solution)/shard_map/all_to_all | solution.py:813
  18.3 0.0 copy-done
  18.3 4.0 %far_spread.1 = f32[8,16,128]{2,1,0:T(8,128)} custom-call(f32[8,24,160]{2,1,0:T(8,128)S(1)} %all-to-all-done.request_in.asked_ref, f32[4096,128]{1,0:T(8,128)S(1)} %copy-done), custom_call_target="tpu_custom_call" | custom-call | flops 40000000 | bytes 4000000 | tf_op jit(solution)/shard_map/far_spread/pallas_call | solution.py:355
  22.3 4.2 %all-to-all-start.1 = ((f32[8,16,128]{2,1,0:T(8,128)}), f32[8,16,128]{2,1,0:T(8,128)S(1)}, u32[]{:S(2)}, u32[]{:S(2)}) async-start(f32[8,16,128]{2,1,0:T(8,128)} %far_spread.1), calls=%async_computation.1 | async-start | bytes 131072 | tf_op jit(solution)/shard_map/all_to_all | solution.py:818
  26.4 0.0 copy-done.2
  26.4 3.8 %collective-permute-start.2 = (f32[136,128]{1,0:T(8,128)S(1)}, f32[136,128]{1,0:T(8,128)S(1)}, u32[]{:S(2)}, u32[]{:S(2)}) collective-permute-start(f32[136,128]{1,0:T(8,128)S(1)} %copy-done.2), channel_id=1, source_target_pairs={{0,24},{4,28},{8,16},{12,20},{16,8},{20,12},{24,0},{28,4},{1,25},{... | collective-permute-start | bytes 208904 | tf_op jit(solution)/shard_map/ppermute | solution.py:782
  30.3 0.0 collective-permute-start.1
  30.3 0.6 %collective-permute-start = (f32[136,128]{1,0:T(8,128)S(1)}, f32[136,128]{1,0:T(8,128)S(1)}, u32[]{:S(2)}, u32[]{:S(2)}) collective-permute-start(f32[136,128]{1,0:T(8,128)S(1)} %copy-done.2), channel_id=1, source_target_pairs={{0,8},{4,12},{8,0},{12,4},{16,24},{20,28},{24,16},{28,20},{1,9},{5... | collective-permute-start | bytes 208904 | tf_op jit(solution)/shard_map/ppermute | solution.py:782
  30.9 0.1 pad_add_fusion.where_ref
  31.0 2.8 %all-to-all-done.1.spread_ref = f32[8,16,128]{2,1,0:T(8,128)S(1)} async-done(((f32[8,16,128]{2,1,0:T(8,128)}), f32[8,16,128]{2,1,0:T(8,128)S(1)}, u32[]{:S(2)}, u32[]{:S(2)}) %all-to-all-start.1) | async-done | bytes 65568 | tf_op jit(solution)/shard_map/all_to_all | solution.py:818
  33.8 2.1 %far_line.1 = (f32[512,128]{1,0:T(8,128)S(1)}, f32[4,128]{1,0:T(4,128)}) custom-call(s32[3]{0:T(128)S(1)} %pad_add_fusion.where_ref, f32[8,16,128]{2,1,0:T(8,128)S(1)} %all-to-all-done.1.spread_ref, f32[8,24,160]{2,1,0:T(8,128)S(1)} %all-to-all-done.request_in.asked_ref), custom_call_target="tpu_custom_call" | custom-call | flops 100000000 | bytes 1000000 | tf_op jit(solution)/shard_map/far_line/pallas_call | solution.py:741
  35.9 0.0 collective-permute-done.2.refs_3_
  35.9 0.6 %collective-permute-done.1.refs_2_ = f32[136,128]{1,0:T(8,128)S(1)} collective-permute-done((f32[136,128]{1,0:T(8,128)S(1)}, f32[136,128]{1,0:T(8,128)S(1)}, u32[]{:S(2)}, u32[]{:S(2)}) %collective-permute-start.1) | collective-permute-done | bytes 69664 | tf_op jit(solution)/shard_map/ppermute | solution.py:782
  36.5 0.0 collective-permute-done.refs_1_
  36.5 0.0 copy-done.3
  36.5 0.0 copy-done.4
  36.5 1.2 %join.1.rest_0_ = f32[544,128]{1,0:T(8,128)S(1)} custom-call(s32[3]{0:T(128)S(1)} %pad_add_fusion.where_ref, f32[512,128]{1,0:T(8,128)S(1)} %get-tuple-element.12.far_ref, f32[64,64]{1,0:T(8,128)S(1)} %copy-done.4, f32[128,128]{1,0:T(8,128)S(1)} %copy-done.3, f32[136,128]{1,0:T(8,128)S(1)} %copy-done.2, f32[136,128]{1,0:T(8,128)S(1)} %collective-permute-done.refs_1_, ...), custom_call_target="tpu_custom_call" | custom-call | tf_op jit(solution)/shard_map/join/pallas_call | solution.py:769
  37.7 1.5 %collective-permute-start.6 = (f32[544,128]{1,0:T(8,128)S(1)}, f32[544,128]{1,0:T(8,128)S(1)}, u32[]{:S(2)}, u32[]{:S(2)}) collective-permute-start(f32[544,128]{1,0:T(8,128)S(1)} %join.1.rest_0_), channel_id=1, source_target_pairs={{0,4},{4,0},{8,12},{12,8},{16,20},{20,16},{24,28},{28,24},{1,5},{5... | collective-permute-start | bytes 835592 | tf_op jit(solution)/shard_map/ppermute | solution.py:782
  39.2 1.5 %collective-permute-start.4 = (f32[544,128]{1,0:T(8,128)S(1)}, f32[544,128]{1,0:T(8,128)S(1)}, u32[]{:S(2)}, u32[]{:S(2)}) collective-permute-start(f32[544,128]{1,0:T(8,128)S(1)} %join.1.rest_0_), channel_id=1, source_target_pairs={{0,2},{1,3},{2,0},{3,1},{4,6},{5,7},{6,4},{7,5},{8,10},{9,11},{10,... | collective-permute-start | bytes 835592 | tf_op jit(solution)/shard_map/ppermute | solution.py:782
  40.7 0.0 collective-permute-start.3
  40.7 4.4 %collective-permute-done.6.rest_4_ = f32[544,128]{1,0:T(8,128)S(1)} collective-permute-done((f32[544,128]{1,0:T(8,128)S(1)}, f32[544,128]{1,0:T(8,128)S(1)}, u32[]{:S(2)}, u32[]{:S(2)}) %collective-permute-start.6) | collective-permute-done | bytes 278560 | tf_op jit(solution)/shard_map/ppermute | solution.py:782
  45.1 1.6 %collective-permute-start.8 = (f32[272,128]{1,0:T(8,128)S(1)}, f32[272,128]{1,0:T(8,128)S(1)}, u32[]{:S(2)}, u32[]{:S(2)}) collective-permute-start(f32[272,128]{1,0:T(8,128)S(1)} %slice.8), channel_id=1, source_target_pairs={{0,2},{1,3},{2,0},{3,1},{4,6},{5,7},{6,4},{7,5},{8,10},{9,11},{10,... | collective-permute-start | bytes 417800 | tf_op jit(solution)/shard_map/ppermute | solution.py:782
  46.7 0.1 collective-permute-done.4.rest_2_
  46.8 1.4 %collective-permute-start.9 = (f32[272,128]{1,0:T(8,128)S(1)}, f32[272,128]{1,0:T(8,128)S(1)}, u32[]{:S(2)}, u32[]{:S(2)}) collective-permute-start(f32[272,128]{1,0:T(8,128)S(1)} %slice.9), channel_id=1, source_target_pairs={{0,4},{4,0},{8,12},{12,8},{16,20},{20,16},{24,28},{28,24},{1,5},{5... | collective-permute-start | bytes 417800 | tf_op jit(solution)/shard_map/ppermute | solution.py:782
  48.2 0.0 collective-permute-start.7
  48.2 0.5 collective-permute-start.5
  48.7 1.6 %collective-permute-done.8.rest_6_ = f32[272,128]{1,0:T(8,128)S(1)} collective-permute-done((f32[272,128]{1,0:T(8,128)S(1)}, f32[272,128]{1,0:T(8,128)S(1)}, u32[]{:S(2)}, u32[]{:S(2)}) %collective-permute-start.8) | collective-permute-done | bytes 139296 | tf_op jit(solution)/shard_map/ppermute | solution.py:782
  50.2 0.0 collective-permute-start.10
  50.2 1.7 %collective-permute-done.9.rest_7_ = f32[272,128]{1,0:T(8,128)S(1)} collective-permute-done((f32[272,128]{1,0:T(8,128)S(1)}, f32[272,128]{1,0:T(8,128)S(1)}, u32[]{:S(2)}, u32[]{:S(2)}) %collective-permute-start.9) | collective-permute-done | bytes 139296 | tf_op jit(solution)/shard_map/ppermute | solution.py:782
  51.9 0.0 collective-permute-start.11
  51.9 0.0 copy-done.8
  51.9 0.1 copy.17.adj_ref
  52.0 0.0 collective-permute-done.3.rest_1_
  52.0 0.0 collective-permute-done.10.rest_8_
  52.1 0.0 collective-permute-done.7.rest_5_
  52.1 1.2 %collective-permute-done.11.rest_9_ = f32[272,128]{1,0:T(8,128)S(1)} collective-permute-done((f32[272,128]{1,0:T(8,128)S(1)}, f32[272,128]{1,0:T(8,128)S(1)}, u32[]{:S(2)}, u32[]{:S(2)}) %collective-permute-start.11) | collective-permute-done | bytes 139296 | tf_op jit(solution)/shard_map/ppermute | solution.py:782
  53.3 0.0 collective-permute-done.5.rest_3_
  53.3 0.0 copy-done.1
  53.3 0.0 copy-done.5
  53.3 0.0 copy-done.6
  53.3 0.0 copy-done.7
  53.3 6.6 %smooth.1 = f32[24,64,64]{2,1,0:T(8,128)} custom-call(s32[3]{0:T(128)S(1)} %pad_add_fusion.where_ref, s32[96,4]{1,0:T(8,128)S(1)} %copy.17.adj_ref, f32[256,512]{1,0:T(8,128)S(1)} %copy-done.1, f32[64,64]{1,0:T(8,128)S(1)} %copy-done.4, f32[128,128]{1,0:T(8,128)S(1)} %copy-done.3, f32[64,128]{1,0:T(8,128)S(1)} %copy-done.5, f32[8,64]{1,0:T(8,128)S(1)} %copy-done.7, ...), custom_call_target="tpu_custom_call" | custom-call | tf_op jit(solution)/shard_map/smooth/pallas_call | solution.py:692
  (2 shorter events, 0.0 us)
Async XLA Ops:
  0.6 17.7 %copy-start = (f32[4096,128]{1,0:T(8,128)S(1)}, f32[4096,128]{1,0:T(8,128)}, u32[]{:S(2)}) copy-start(f32[4096,128]{1,0:T(8,128)} %fields_ref.1) | copy-start | bytes 6291460
  3.1 15.2 %all-to-all-start = ((f32[8,24,160]{2,1,0:T(8,128)}), f32[8,24,160]{2,1,0:T(8,128)S(1)}, u32[]{:S(2)}, u32[]{:S(2)}) async-start(f32[8,24,160]{2,1,0:T(8,128)} %get-tuple-element.8), calls=%async_computation | async-start | bytes 393216 | tf_op jit(solution)/shard_map/all_to_all | solution.py:813
  10.4 26.2 %copy-start.3 = (f32[128,128]{1,0:T(8,128)S(1)}, f32[128,128]{1,0:T(8,128)}, u32[]{:S(2)}) copy-start(f32[128,128]{1,0:T(8,128)} %constant.35.clone.pair_ref) | copy-start | bytes 196612
  10.4 26.2 %copy-start.4 = (f32[64,64]{1,0:T(8,128)S(1)}, f32[64,64]{1,0:T(8,128)}, u32[]{:S(2)}) copy-start(f32[64,64]{1,0:T(8,128)} %constant.34.clone.basis_ref) | copy-start | bytes 49156
  16.4 10.1 %copy-start.2 = (f32[136,128]{1,0:T(8,128)S(1)}, f32[136,128]{1,0:T(8,128)}, u32[]{:S(2)}) copy-start(f32[136,128]{1,0:T(8,128)} %near_payload.1.refs_0_) | copy-start | bytes 208900
  16.4 35.5 %copy-start.8 = (s32[96,4]{0,1:T(4,128)S(1)}, s32[96,4]{0,1:T(4,128)}, u32[]{:S(2)}) copy-start(s32[96,4]{0,1:T(4,128)} %param.23) | copy-start | bytes 4612
  16.4 36.9 %copy-start.1 = (f32[256,512]{1,0:T(8,128)S(1)}, f32[256,512]{1,0:T(8,128)}, u32[]{:S(2)}) copy-start(f32[256,512]{1,0:T(8,128)} %constant.39.clone.coupling_ref) | copy-start | bytes 1572868
  16.4 36.9 %copy-start.5 = (f32[64,128]{1,0:T(8,128)S(1)}, f32[64,128]{1,0:T(8,128)}, u32[]{:S(2)}) copy-start(f32[64,128]{1,0:T(8,128)} %constant.38.clone.series_ref) | copy-start | bytes 98308
  16.4 36.9 %copy-start.6 = (f32[8,128]{1,0:T(8,128)S(1)}, f32[8,128]{1,0:T(8,128)}, u32[]{:S(2)}) copy-start(f32[8,128]{1,0:T(8,128)} %constant.37.clone.scale_ref) | copy-start | bytes 12292
  16.4 36.9 %copy-start.7 = (f32[8,64]{1,0:T(8,128)S(1)}, f32[8,64]{1,0:T(8,128)}, u32[]{:S(2)}) copy-start(f32[8,64]{1,0:T(8,128)} %constant.36.clone.edge_ref) | copy-start | bytes 6148
  22.3 11.5 %all-to-all-start.1 = ((f32[8,16,128]{2,1,0:T(8,128)}), f32[8,16,128]{2,1,0:T(8,128)S(1)}, u32[]{:S(2)}, u32[]{:S(2)}) async-start(f32[8,16,128]{2,1,0:T(8,128)} %far_spread.1), calls=%async_computation.1 | async-start | bytes 131072 | tf_op jit(solution)/shard_map/all_to_all | solution.py:818
  26.4 9.4 %collective-permute-start.2 = (f32[136,128]{1,0:T(8,128)S(1)}, f32[136,128]{1,0:T(8,128)S(1)}, u32[]{:S(2)}, u32[]{:S(2)}) collective-permute-start(f32[136,128]{1,0:T(8,128)S(1)} %copy-done.2), channel_id=1, source_target_pairs={{0,24},{4,28},{8,16},{12,20},{16,8},{20,12},{24,0},{28,4},{1,25},{... | collective-permute-start | bytes 208904 | tf_op jit(solution)/shard_map/ppermute | solution.py:782
  30.3 6.2 %collective-permute-start.1 = (f32[136,128]{1,0:T(8,128)S(1)}, f32[136,128]{1,0:T(8,128)S(1)}, u32[]{:S(2)}, u32[]{:S(2)}) collective-permute-start(f32[136,128]{1,0:T(8,128)S(1)} %copy-done.2), channel_id=1, source_target_pairs={{0,16},{4,20},{8,24},{12,28},{16,0},{20,4},{24,8},{28,12},{1,17},{... | collective-permute-start | bytes 208904 | tf_op jit(solution)/shard_map/ppermute | solution.py:782
  30.3 6.2 %collective-permute-start = (f32[136,128]{1,0:T(8,128)S(1)}, f32[136,128]{1,0:T(8,128)S(1)}, u32[]{:S(2)}, u32[]{:S(2)}) collective-permute-start(f32[136,128]{1,0:T(8,128)S(1)} %copy-done.2), channel_id=1, source_target_pairs={{0,8},{4,12},{8,0},{12,4},{16,24},{20,28},{24,16},{28,20},{1,9},{5... | collective-permute-start | bytes 208904 | tf_op jit(solution)/shard_map/ppermute | solution.py:782
  37.7 7.4 %collective-permute-start.6 = (f32[544,128]{1,0:T(8,128)S(1)}, f32[544,128]{1,0:T(8,128)S(1)}, u32[]{:S(2)}, u32[]{:S(2)}) collective-permute-start(f32[544,128]{1,0:T(8,128)S(1)} %join.1.rest_0_), channel_id=1, source_target_pairs={{0,4},{4,0},{8,12},{12,8},{16,20},{20,16},{24,28},{28,24},{1,5},{5... | collective-permute-start | bytes 835592 | tf_op jit(solution)/shard_map/ppermute | solution.py:782
  39.2 7.6 %collective-permute-start.4 = (f32[544,128]{1,0:T(8,128)S(1)}, f32[544,128]{1,0:T(8,128)S(1)}, u32[]{:S(2)}, u32[]{:S(2)}) collective-permute-start(f32[544,128]{1,0:T(8,128)S(1)} %join.1.rest_0_), channel_id=1, source_target_pairs={{0,2},{1,3},{2,0},{3,1},{4,6},{5,7},{6,4},{7,5},{8,10},{9,11},{10,... | collective-permute-start | bytes 835592 | tf_op jit(solution)/shard_map/ppermute | solution.py:782
  40.7 11.3 %collective-permute-start.3 = (f32[544,128]{1,0:T(8,128)S(1)}, f32[544,128]{1,0:T(8,128)S(1)}, u32[]{:S(2)}, u32[]{:S(2)}) collective-permute-start(f32[544,128]{1,0:T(8,128)S(1)} %join.1.rest_0_), channel_id=1, source_target_pairs={{0,1},{1,0},{2,3},{3,2},{4,5},{5,4},{6,7},{7,6},{8,9},{9,8},{10,11... | collective-permute-start | bytes 835592 | tf_op jit(solution)/shard_map/ppermute | solution.py:782
  45.1 5.1 %collective-permute-start.8 = (f32[272,128]{1,0:T(8,128)S(1)}, f32[272,128]{1,0:T(8,128)S(1)}, u32[]{:S(2)}, u32[]{:S(2)}) collective-permute-start(f32[272,128]{1,0:T(8,128)S(1)} %slice.8), channel_id=1, source_target_pairs={{0,2},{1,3},{2,0},{3,1},{4,6},{5,7},{6,4},{7,5},{8,10},{9,11},{10,... | collective-permute-start | bytes 417800 | tf_op jit(solution)/shard_map/ppermute | solution.py:782
  46.8 5.1 %collective-permute-start.9 = (f32[272,128]{1,0:T(8,128)S(1)}, f32[272,128]{1,0:T(8,128)S(1)}, u32[]{:S(2)}, u32[]{:S(2)}) collective-permute-start(f32[272,128]{1,0:T(8,128)S(1)} %slice.9), channel_id=1, source_target_pairs={{0,4},{4,0},{8,12},{12,8},{16,20},{20,16},{24,28},{28,24},{1,5},{5... | collective-permute-start | bytes 417800 | tf_op jit(solution)/shard_map/ppermute | solution.py:782
  48.2 3.9 %collective-permute-start.7 = (f32[544,128]{1,0:T(8,128)S(1)}, f32[544,128]{1,0:T(8,128)S(1)}, u32[]{:S(2)}, u32[]{:S(2)}) collective-permute-start(f32[544,128]{1,0:T(8,128)S(1)} %collective-permute-done.6.rest_4_), channel_id=1, source_target_pairs={{0,1},{1,0},{2,3},{3,2},{4,5},{5,4},{6,7},{7,6},{8,9},{9,8},{10,11... | collective-permute-start | bytes 835592 | tf_op jit(solution)/shard_map/ppermute | solution.py:782
  48.2 5.1 %collective-permute-start.5 = (f32[544,128]{1,0:T(8,128)S(1)}, f32[544,128]{1,0:T(8,128)S(1)}, u32[]{:S(2)}, u32[]{:S(2)}) collective-permute-start(f32[544,128]{1,0:T(8,128)S(1)} %collective-permute-done.4.rest_2_), channel_id=1, source_target_pairs={{0,1},{1,0},{2,3},{3,2},{4,5},{5,4},{6,7},{7,6},{8,9},{9,8},{10,11... | collective-permute-start | bytes 835592 | tf_op jit(solution)/shard_map/ppermute | solution.py:782
  50.2 1.8 %collective-permute-start.10 = (f32[272,128]{1,0:T(8,128)S(1)}, f32[272,128]{1,0:T(8,128)S(1)}, u32[]{:S(2)}, u32[]{:S(2)}) collective-permute-start(f32[272,128]{1,0:T(8,128)S(1)} %collective-permute-done.8.rest_6_), channel_id=1, source_target_pairs={{0,1},{1,0},{2,3},{3,2},{4,5},{5,4},{6,7},{7,6},{8,9},{9,8},{10,11... | collective-permute-start | bytes 417800 | tf_op jit(solution)/shard_map/ppermute | solution.py:782
  51.9 1.4 %collective-permute-start.11 = (f32[272,128]{1,0:T(8,128)S(1)}, f32[272,128]{1,0:T(8,128)S(1)}, u32[]{:S(2)}, u32[]{:S(2)}) collective-permute-start(f32[272,128]{1,0:T(8,128)S(1)} %collective-permute-done.9.rest_7_), channel_id=1, source_target_pairs={{0,1},{1,0},{2,3},{3,2},{4,5},{5,4},{6,7},{7,6},{8,9},{9,8},{10,11... | collective-permute-start | bytes 417800 | tf_op jit(solution)/shard_map/ppermute | solution.py:782

commit v7 on v6

--- a/solution.py
+++ b/solution.py
@@ -196,7 +196,7 @@
 
 
 def gather_rows(cells, fields_ref, rows_ref, count):
-    unroll = 32
+    unroll = 64
 
     def step(i, carry):
         for u in range(unroll):
@@ -263,7 +263,7 @@
         return carry
 
     tiles = count // LANES
-    lax.fori_loop(0, tiles, step, 0, unroll=4 if tiles % 4 == 0 else 2)
+    lax.fori_loop(0, tiles, step, 0, unroll=next(n for n in (8, 5, 4, 2, 1) if tiles % n == 0))
 
 
 def near_kernel(first, cell_in, fields_in, geom_in, out_ref, cell_ref, fields_ref, geom_ref, rows_ref, sem):

time: 60.2 us -> 59.7 us (level)
  no operation moved by 1% of the time
where the time goes in v7:
time: 59.7 us; the launch traced here: 59.3 us
  starting transfers between devices  22.1 us (37%)
  Pallas kernels  21.6 us (36%)
  waiting for transfers between devices  14.5 us (24%)
  between operations  0.8 us (1%)
    ppermute x12, starting transfers between devices, over(): return lax.ppermute(array, axis, [(i, i ^ bit) for i in range(count)])  10.9 us
    ppermute x12, waiting for transfers between devices, over(): return lax.ppermute(array, axis, [(i, i ^ bit) for i in range(count)])  9.58 us
    all_to_all x1, starting transfers between devices, per_device(): lax.all_to_all(request, 'vol', split_axis=0, concat_axis=0, tiled=True)  7.29 us
    pallas_call x1, Pallas kernels, smooth(): pl.pallas_call(functools.partial(smooth_kernel, items, per_owner), out_sh...  6.57 us
    pallas_call x1, Pallas kernels, near_payload(): pl.pallas_call(near_payload_kernel, out_shape=jax.ShapeDtypeStruct((PAYLO...  5.75 us
    all_to_all x1, starting transfers between devices, per_device(): lax.all_to_all(spread, 'vol', split_axis=0, concat_axis=0, tiled=True)  3.91 us
    pallas_call x1, Pallas kernels, far_spread(): pl.pallas_call(far_spread_kernel, out_shape=jax.ShapeDtypeStruct((owners,...  3.65 us
    all_to_all x1, waiting for transfers between devices, per_device(): lax.all_to_all(spread, 'vol', split_axis=0, concat_axis=0, tiled=True)  2.82 us
  transfers between devices with their start and end apart: 14, of which 8 were waited for; matrix products, arithmetic and copies ran while one was open for 0% of the time, Pallas kernels for 13%

profile of v7, /device:TPU:0, one launch (start us, length us, event | category | flops | bytes accessed | tf_op | source)
XLA Modules:
  0.0 59.3 jit_solution(14279158067203707457)
XLA Ops:
  0.6 0.0 copy-start
  0.6 2.4 %pack_requests.1 = (f32[8,24,160]{2,1,0:T(8,128)}, s32[1,512]{1,0:T(1,128)}, f32[8,128]{1,0:T(8,128)}) custom-call(f32[8,512]{1,0:T(8,128)} %geom_in.2, s32[1,512]{1,0:T(1,128)} %bitcast.10, s32[1,512]{1,0:T(1,128)} %bitcast.11, s32[1,2048]{1,0:T(1,128)} %bitcast.8, s32[1,512]{1,0:T(1,128)} %bitcast.12), custom_call_target="tpu_custom_call" | custom-call | tf_op jit(solution)/shard_map/pack_requests/pallas_call | solution.py:176
  3.1 7.3 %all-to-all-start = ((f32[8,24,160]{2,1,0:T(8,128)}), f32[8,24,160]{2,1,0:T(8,128)S(1)}, u32[]{:S(2)}, u32[]{:S(2)}) async-start(f32[8,24,160]{2,1,0:T(8,128)} %get-tuple-element.8), calls=%async_computation | async-start | bytes 393216 | tf_op jit(solution)/shard_map/all_to_all | solution.py:813
  10.4 0.0 copy-start.3
  10.4 0.0 copy-start.4
  10.4 5.8 %near_payload.1.refs_0_ = f32[136,128]{1,0:T(8,128)} custom-call(s32[2048]{0:T(1024)} %cell_in.1, f32[4096,128]{1,0:T(8,128)} %fields_ref.1, f32[8,2048]{1,0:T(8,128)} %geom_in.3, s32[1,2048]{1,0:T(1,128)} %bitcast.9, f32[8,128]{1,0:T(8,128)} %get-tuple-element.9.slot_in), custom_call_target="tpu_custom_call" | custom-call | flops 100000000 | bytes 4000000 | tf_op jit(solution)/shard_map/near_payload/pallas_call | solution.py:435
  16.1 0.0 copy-start.2
  16.1 0.0 copy-start.8
  16.2 0.0 copy-start.1
  16.2 0.0 copy-start.5
  16.2 0.0 copy-start.6
  16.2 0.0 copy-start.7
  16.2 2.1 %all-to-all-done.request_in.asked_ref = f32[8,24,160]{2,1,0:T(8,128)S(1)} async-done(((f32[8,24,160]{2,1,0:T(8,128)}), f32[8,24,160]{2,1,0:T(8,128)S(1)}, u32[]{:S(2)}, u32[]{:S(2)}) %all-to-all-start) | async-done | bytes 122912 | tf_op jit(solution)/shard_map/all_to_all | solution.py:813
  18.3 0.0 copy-done
  18.3 3.7 %far_spread.1 = f32[8,16,128]{2,1,0:T(8,128)} custom-call(f32[8,24,160]{2,1,0:T(8,128)S(1)} %all-to-all-done.request_in.asked_ref, f32[4096,128]{1,0:T(8,128)S(1)} %copy-done), custom_call_target="tpu_custom_call" | custom-call | flops 40000000 | bytes 4000000 | tf_op jit(solution)/shard_map/far_spread/pallas_call | solution.py:355
  22.0 3.9 %all-to-all-start.1 = ((f32[8,16,128]{2,1,0:T(8,128)}), f32[8,16,128]{2,1,0:T(8,128)S(1)}, u32[]{:S(2)}, u32[]{:S(2)}) async-start(f32[8,16,128]{2,1,0:T(8,128)} %far_spread.1), calls=%async_computation.1 | async-start | bytes 131072 | tf_op jit(solution)/shard_map/all_to_all | solution.py:818
  25.9 0.0 copy-done.2
  25.9 3.8 %collective-permute-start.2 = (f32[136,128]{1,0:T(8,128)S(1)}, f32[136,128]{1,0:T(8,128)S(1)}, u32[]{:S(2)}, u32[]{:S(2)}) collective-permute-start(f32[136,128]{1,0:T(8,128)S(1)} %copy-done.2), channel_id=1, source_target_pairs={{0,24},{4,28},{8,16},{12,20},{16,8},{20,12},{24,0},{28,4},{1,25},{... | collective-permute-start | bytes 208904 | tf_op jit(solution)/shard_map/ppermute | solution.py:782
  29.7 0.0 collective-permute-start.1
  29.7 0.6 %collective-permute-start = (f32[136,128]{1,0:T(8,128)S(1)}, f32[136,128]{1,0:T(8,128)S(1)}, u32[]{:S(2)}, u32[]{:S(2)}) collective-permute-start(f32[136,128]{1,0:T(8,128)S(1)} %copy-done.2), channel_id=1, source_target_pairs={{0,8},{4,12},{8,0},{12,4},{16,24},{20,28},{24,16},{28,20},{1,9},{5... | collective-permute-start | bytes 208904 | tf_op jit(solution)/shard_map/ppermute | solution.py:782
  30.3 0.1 pad_add_fusion.where_ref
  30.4 2.8 %all-to-all-done.1.spread_ref = f32[8,16,128]{2,1,0:T(8,128)S(1)} async-done(((f32[8,16,128]{2,1,0:T(8,128)}), f32[8,16,128]{2,1,0:T(8,128)S(1)}, u32[]{:S(2)}, u32[]{:S(2)}) %all-to-all-start.1) | async-done | bytes 65568 | tf_op jit(solution)/shard_map/all_to_all | solution.py:818
  33.2 2.1 %far_line.1 = (f32[512,128]{1,0:T(8,128)S(1)}, f32[4,128]{1,0:T(4,128)}) custom-call(s32[3]{0:T(128)S(1)} %pad_add_fusion.where_ref, f32[8,16,128]{2,1,0:T(8,128)S(1)} %all-to-all-done.1.spread_ref, f32[8,24,160]{2,1,0:T(8,128)S(1)} %all-to-all-done.request_in.asked_ref), custom_call_target="tpu_custom_call" | custom-call | flops 100000000 | bytes 1000000 | tf_op jit(solution)/shard_map/far_line/pallas_call | solution.py:741
  35.3 0.0 collective-permute-done.2.refs_3_
  35.3 0.6 %collective-permute-done.1.refs_2_ = f32[136,128]{1,0:T(8,128)S(1)} collective-permute-done((f32[136,128]{1,0:T(8,128)S(1)}, f32[136,128]{1,0:T(8,128)S(1)}, u32[]{:S(2)}, u32[]{:S(2)}) %collective-permute-start.1) | collective-permute-done | bytes 69664 | tf_op jit(solution)/shard_map/ppermute | solution.py:782
  36.0 0.0 collective-permute-done.refs_1_
  36.0 0.0 copy-done.3
  36.0 0.0 copy-done.4
  36.0 1.2 %join.1.rest_0_ = f32[544,128]{1,0:T(8,128)S(1)} custom-call(s32[3]{0:T(128)S(1)} %pad_add_fusion.where_ref, f32[512,128]{1,0:T(8,128)S(1)} %get-tuple-element.12.far_ref, f32[64,64]{1,0:T(8,128)S(1)} %copy-done.4, f32[128,128]{1,0:T(8,128)S(1)} %copy-done.3, f32[136,128]{1,0:T(8,128)S(1)} %copy-done.2, f32[136,128]{1,0:T(8,128)S(1)} %collective-permute-done.refs_1_, ...), custom_call_target="tpu_custom_call" | custom-call | tf_op jit(solution)/shard_map/join/pallas_call | solution.py:769
  37.1 1.5 %collective-permute-start.6 = (f32[544,128]{1,0:T(8,128)S(1)}, f32[544,128]{1,0:T(8,128)S(1)}, u32[]{:S(2)}, u32[]{:S(2)}) collective-permute-start(f32[544,128]{1,0:T(8,128)S(1)} %join.1.rest_0_), channel_id=1, source_target_pairs={{0,4},{4,0},{8,12},{12,8},{16,20},{20,16},{24,28},{28,24},{1,5},{5... | collective-permute-start | bytes 835592 | tf_op jit(solution)/shard_map/ppermute | solution.py:782
  38.7 1.5 %collective-permute-start.4 = (f32[544,128]{1,0:T(8,128)S(1)}, f32[544,128]{1,0:T(8,128)S(1)}, u32[]{:S(2)}, u32[]{:S(2)}) collective-permute-start(f32[544,128]{1,0:T(8,128)S(1)} %join.1.rest_0_), channel_id=1, source_target_pairs={{0,2},{1,3},{2,0},{3,1},{4,6},{5,7},{6,4},{7,5},{8,10},{9,11},{10,... | collective-permute-start | bytes 835592 | tf_op jit(solution)/shard_map/ppermute | solution.py:782
  40.2 0.0 collective-permute-start.3
  40.2 4.4 %collective-permute-done.6.rest_4_ = f32[544,128]{1,0:T(8,128)S(1)} collective-permute-done((f32[544,128]{1,0:T(8,128)S(1)}, f32[544,128]{1,0:T(8,128)S(1)}, u32[]{:S(2)}, u32[]{:S(2)}) %collective-permute-start.6) | collective-permute-done | bytes 278560 | tf_op jit(solution)/shard_map/ppermute | solution.py:782
  44.6 1.6 %collective-permute-start.8 = (f32[272,128]{1,0:T(8,128)S(1)}, f32[272,128]{1,0:T(8,128)S(1)}, u32[]{:S(2)}, u32[]{:S(2)}) collective-permute-start(f32[272,128]{1,0:T(8,128)S(1)} %slice.8), channel_id=1, source_target_pairs={{0,2},{1,3},{2,0},{3,1},{4,6},{5,7},{6,4},{7,5},{8,10},{9,11},{10,... | collective-permute-start | bytes 417800 | tf_op jit(solution)/shard_map/ppermute | solution.py:782
  46.1 0.1 collective-permute-done.4.rest_2_
  46.3 1.4 %collective-permute-start.9 = (f32[272,128]{1,0:T(8,128)S(1)}, f32[272,128]{1,0:T(8,128)S(1)}, u32[]{:S(2)}, u32[]{:S(2)}) collective-permute-start(f32[272,128]{1,0:T(8,128)S(1)} %slice.9), channel_id=1, source_target_pairs={{0,4},{4,0},{8,12},{12,8},{16,20},{20,16},{24,28},{28,24},{1,5},{5... | collective-permute-start | bytes 417800 | tf_op jit(solution)/shard_map/ppermute | solution.py:782
  47.6 0.0 collective-permute-start.7
  47.6 0.5 collective-permute-start.5
  48.1 1.5 %collective-permute-done.8.rest_6_ = f32[272,128]{1,0:T(8,128)S(1)} collective-permute-done((f32[272,128]{1,0:T(8,128)S(1)}, f32[272,128]{1,0:T(8,128)S(1)}, u32[]{:S(2)}, u32[]{:S(2)}) %collective-permute-start.8) | collective-permute-done | bytes 139296 | tf_op jit(solution)/shard_map/ppermute | solution.py:782
  49.7 0.0 collective-permute-start.10
  49.7 1.7 %collective-permute-done.9.rest_7_ = f32[272,128]{1,0:T(8,128)S(1)} collective-permute-done((f32[272,128]{1,0:T(8,128)S(1)}, f32[272,128]{1,0:T(8,128)S(1)}, u32[]{:S(2)}, u32[]{:S(2)}) %collective-permute-start.9) | collective-permute-done | bytes 139296 | tf_op jit(solution)/shard_map/ppermute | solution.py:782
  51.4 0.0 collective-permute-start.11
  51.4 0.0 copy-done.8
  51.4 0.1 copy.17.adj_ref
  51.5 0.0 collective-permute-done.3.rest_1_
  51.5 0.0 collective-permute-done.10.rest_8_
  51.5 0.0 collective-permute-done.7.rest_5_
  51.5 1.2 %collective-permute-done.11.rest_9_ = f32[272,128]{1,0:T(8,128)S(1)} collective-permute-done((f32[272,128]{1,0:T(8,128)S(1)}, f32[272,128]{1,0:T(8,128)S(1)}, u32[]{:S(2)}, u32[]{:S(2)}) %collective-permute-start.11) | collective-permute-done | bytes 139296 | tf_op jit(solution)/shard_map/ppermute | solution.py:782
  52.7 0.0 collective-permute-done.5.rest_3_
  52.7 0.0 copy-done.1
  52.7 0.0 copy-done.5
  52.7 0.0 copy-done.6
  52.8 0.0 copy-done.7
  52.8 6.6 %smooth.1 = f32[24,64,64]{2,1,0:T(8,128)} custom-call(s32[3]{0:T(128)S(1)} %pad_add_fusion.where_ref, s32[96,4]{1,0:T(8,128)S(1)} %copy.17.adj_ref, f32[256,512]{1,0:T(8,128)S(1)} %copy-done.1, f32[64,64]{1,0:T(8,128)S(1)} %copy-done.4, f32[128,128]{1,0:T(8,128)S(1)} %copy-done.3, f32[64,128]{1,0:T(8,128)S(1)} %copy-done.5, f32[8,64]{1,0:T(8,128)S(1)} %copy-done.7, ...), custom_call_target="tpu_custom_call" | custom-call | tf_op jit(solution)/shard_map/smooth/pallas_call | solution.py:692
  (2 shorter events, 0.0 us)
Async XLA Ops:
  0.6 17.7 %copy-start = (f32[4096,128]{1,0:T(8,128)S(1)}, f32[4096,128]{1,0:T(8,128)}, u32[]{:S(2)}) copy-start(f32[4096,128]{1,0:T(8,128)} %fields_ref.1) | copy-start | bytes 6291460
  3.1 15.2 %all-to-all-start = ((f32[8,24,160]{2,1,0:T(8,128)}), f32[8,24,160]{2,1,0:T(8,128)S(1)}, u32[]{:S(2)}, u32[]{:S(2)}) async-start(f32[8,24,160]{2,1,0:T(8,128)} %get-tuple-element.8), calls=%async_computation | async-start | bytes 393216 | tf_op jit(solution)/shard_map/all_to_all | solution.py:813
  10.4 25.6 %copy-start.3 = (f32[128,128]{1,0:T(8,128)S(1)}, f32[128,128]{1,0:T(8,128)}, u32[]{:S(2)}) copy-start(f32[128,128]{1,0:T(8,128)} %constant.35.clone.pair_ref) | copy-start | bytes 196612
  10.4 25.6 %copy-start.4 = (f32[64,64]{1,0:T(8,128)S(1)}, f32[64,64]{1,0:T(8,128)}, u32[]{:S(2)}) copy-start(f32[64,64]{1,0:T(8,128)} %constant.34.clone.basis_ref) | copy-start | bytes 49156
  16.1 9.8 %copy-start.2 = (f32[136,128]{1,0:T(8,128)S(1)}, f32[136,128]{1,0:T(8,128)}, u32[]{:S(2)}) copy-start(f32[136,128]{1,0:T(8,128)} %near_payload.1.refs_0_) | copy-start | bytes 208900
  16.1 35.2 %copy-start.8 = (s32[96,4]{0,1:T(4,128)S(1)}, s32[96,4]{0,1:T(4,128)}, u32[]{:S(2)}) copy-start(s32[96,4]{0,1:T(4,128)} %param.23) | copy-start | bytes 4612
  16.2 36.6 %copy-start.1 = (f32[256,512]{1,0:T(8,128)S(1)}, f32[256,512]{1,0:T(8,128)}, u32[]{:S(2)}) copy-start(f32[256,512]{1,0:T(8,128)} %constant.39.clone.coupling_ref) | copy-start | bytes 1572868
  16.2 36.6 %copy-start.5 = (f32[64,128]{1,0:T(8,128)S(1)}, f32[64,128]{1,0:T(8,128)}, u32[]{:S(2)}) copy-start(f32[64,128]{1,0:T(8,128)} %constant.38.clone.series_ref) | copy-start | bytes 98308
  16.2 36.6 %copy-start.6 = (f32[8,128]{1,0:T(8,128)S(1)}, f32[8,128]{1,0:T(8,128)}, u32[]{:S(2)}) copy-start(f32[8,128]{1,0:T(8,128)} %constant.37.clone.scale_ref) | copy-start | bytes 12292
  16.2 36.6 %copy-start.7 = (f32[8,64]{1,0:T(8,128)S(1)}, f32[8,64]{1,0:T(8,128)}, u32[]{:S(2)}) copy-start(f32[8,64]{1,0:T(8,128)} %constant.36.clone.edge_ref) | copy-start | bytes 6148
  22.0 11.3 %all-to-all-start.1 = ((f32[8,16,128]{2,1,0:T(8,128)}), f32[8,16,128]{2,1,0:T(8,128)S(1)}, u32[]{:S(2)}, u32[]{:S(2)}) async-start(f32[8,16,128]{2,1,0:T(8,128)} %far_spread.1), calls=%async_computation.1 | async-start | bytes 131072 | tf_op jit(solution)/shard_map/all_to_all | solution.py:818
  25.9 9.4 %collective-permute-start.2 = (f32[136,128]{1,0:T(8,128)S(1)}, f32[136,128]{1,0:T(8,128)S(1)}, u32[]{:S(2)}, u32[]{:S(2)}) collective-permute-start(f32[136,128]{1,0:T(8,128)S(1)} %copy-done.2), channel_id=1, source_target_pairs={{0,24},{4,28},{8,16},{12,20},{16,8},{20,12},{24,0},{28,4},{1,25},{... | collective-permute-start | bytes 208904 | tf_op jit(solution)/shard_map/ppermute | solution.py:782
  29.7 6.2 %collective-permute-start.1 = (f32[136,128]{1,0:T(8,128)S(1)}, f32[136,128]{1,0:T(8,128)S(1)}, u32[]{:S(2)}, u32[]{:S(2)}) collective-permute-start(f32[136,128]{1,0:T(8,128)S(1)} %copy-done.2), channel_id=1, source_target_pairs={{0,16},{4,20},{8,24},{12,28},{16,0},{20,4},{24,8},{28,12},{1,17},{... | collective-permute-start | bytes 208904 | tf_op jit(solution)/shard_map/ppermute | solution.py:782
  29.7 6.2 %collective-permute-start = (f32[136,128]{1,0:T(8,128)S(1)}, f32[136,128]{1,0:T(8,128)S(1)}, u32[]{:S(2)}, u32[]{:S(2)}) collective-permute-start(f32[136,128]{1,0:T(8,128)S(1)} %copy-done.2), channel_id=1, source_target_pairs={{0,8},{4,12},{8,0},{12,4},{16,24},{20,28},{24,16},{28,20},{1,9},{5... | collective-permute-start | bytes 208904 | tf_op jit(solution)/shard_map/ppermute | solution.py:782
  37.1 7.4 %collective-permute-start.6 = (f32[544,128]{1,0:T(8,128)S(1)}, f32[544,128]{1,0:T(8,128)S(1)}, u32[]{:S(2)}, u32[]{:S(2)}) collective-permute-start(f32[544,128]{1,0:T(8,128)S(1)} %join.1.rest_0_), channel_id=1, source_target_pairs={{0,4},{4,0},{8,12},{12,8},{16,20},{20,16},{24,28},{28,24},{1,5},{5... | collective-permute-start | bytes 835592 | tf_op jit(solution)/shard_map/ppermute | solution.py:782
  38.7 7.6 %collective-permute-start.4 = (f32[544,128]{1,0:T(8,128)S(1)}, f32[544,128]{1,0:T(8,128)S(1)}, u32[]{:S(2)}, u32[]{:S(2)}) collective-permute-start(f32[544,128]{1,0:T(8,128)S(1)} %join.1.rest_0_), channel_id=1, source_target_pairs={{0,2},{1,3},{2,0},{3,1},{4,6},{5,7},{6,4},{7,5},{8,10},{9,11},{10,... | collective-permute-start | bytes 835592 | tf_op jit(solution)/shard_map/ppermute | solution.py:782
  40.2 11.3 %collective-permute-start.3 = (f32[544,128]{1,0:T(8,128)S(1)}, f32[544,128]{1,0:T(8,128)S(1)}, u32[]{:S(2)}, u32[]{:S(2)}) collective-permute-start(f32[544,128]{1,0:T(8,128)S(1)} %join.1.rest_0_), channel_id=1, source_target_pairs={{0,1},{1,0},{2,3},{3,2},{4,5},{5,4},{6,7},{7,6},{8,9},{9,8},{10,11... | collective-permute-start | bytes 835592 | tf_op jit(solution)/shard_map/ppermute | solution.py:782
  44.6 5.1 %collective-permute-start.8 = (f32[272,128]{1,0:T(8,128)S(1)}, f32[272,128]{1,0:T(8,128)S(1)}, u32[]{:S(2)}, u32[]{:S(2)}) collective-permute-start(f32[272,128]{1,0:T(8,128)S(1)} %slice.8), channel_id=1, source_target_pairs={{0,2},{1,3},{2,0},{3,1},{4,6},{5,7},{6,4},{7,5},{8,10},{9,11},{10,... | collective-permute-start | bytes 417800 | tf_op jit(solution)/shard_map/ppermute | solution.py:782
  46.3 5.1 %collective-permute-start.9 = (f32[272,128]{1,0:T(8,128)S(1)}, f32[272,128]{1,0:T(8,128)S(1)}, u32[]{:S(2)}, u32[]{:S(2)}) collective-permute-start(f32[272,128]{1,0:T(8,128)S(1)} %slice.9), channel_id=1, source_target_pairs={{0,4},{4,0},{8,12},{12,8},{16,20},{20,16},{24,28},{28,24},{1,5},{5... | collective-permute-start | bytes 417800 | tf_op jit(solution)/shard_map/ppermute | solution.py:782
  47.6 3.9 %collective-permute-start.7 = (f32[544,128]{1,0:T(8,128)S(1)}, f32[544,128]{1,0:T(8,128)S(1)}, u32[]{:S(2)}, u32[]{:S(2)}) collective-permute-start(f32[544,128]{1,0:T(8,128)S(1)} %collective-permute-done.6.rest_4_), channel_id=1, source_target_pairs={{0,1},{1,0},{2,3},{3,2},{4,5},{5,4},{6,7},{7,6},{8,9},{9,8},{10,11... | collective-permute-start | bytes 835592 | tf_op jit(solution)/shard_map/ppermute | solution.py:782
  47.6 5.1 %collective-permute-start.5 = (f32[544,128]{1,0:T(8,128)S(1)}, f32[544,128]{1,0:T(8,128)S(1)}, u32[]{:S(2)}, u32[]{:S(2)}) collective-permute-start(f32[544,128]{1,0:T(8,128)S(1)} %collective-permute-done.4.rest_2_), channel_id=1, source_target_pairs={{0,1},{1,0},{2,3},{3,2},{4,5},{5,4},{6,7},{7,6},{8,9},{9,8},{10,11... | collective-permute-start | bytes 835592 | tf_op jit(solution)/shard_map/ppermute | solution.py:782
  49.7 1.8 %collective-permute-start.10 = (f32[272,128]{1,0:T(8,128)S(1)}, f32[272,128]{1,0:T(8,128)S(1)}, u32[]{:S(2)}, u32[]{:S(2)}) collective-permute-start(f32[272,128]{1,0:T(8,128)S(1)} %collective-permute-done.8.rest_6_), channel_id=1, source_target_pairs={{0,1},{1,0},{2,3},{3,2},{4,5},{5,4},{6,7},{7,6},{8,9},{9,8},{10,11... | collective-permute-start | bytes 417800 | tf_op jit(solution)/shard_map/ppermute | solution.py:782
  51.4 1.4 %collective-permute-start.11 = (f32[272,128]{1,0:T(8,128)S(1)}, f32[272,128]{1,0:T(8,128)S(1)}, u32[]{:S(2)}, u32[]{:S(2)}) collective-permute-start(f32[272,128]{1,0:T(8,128)S(1)} %collective-permute-done.9.rest_7_), channel_id=1, source_target_pairs={{0,1},{1,0},{2,3},{3,2},{4,5},{5,4},{6,7},{7,6},{8,9},{9,8},{10,11... | collective-permute-start | bytes 417800 | tf_op jit(solution)/shard_map/ppermute | solution.py:782

commit v8 on v7

--- a/solution.py
+++ b/solution.py
@@ -263,7 +263,7 @@
         return carry
 
     tiles = count // LANES
-    lax.fori_loop(0, tiles, step, 0, unroll=next(n for n in (8, 5, 4, 2, 1) if tiles % n == 0))
+    lax.fori_loop(0, tiles, step, 0, unroll=next(n for n in (16, 10, 8, 5, 4, 2, 1) if tiles % n == 0))
 
 
 def near_kernel(first, cell_in, fields_in, geom_in, out_ref, cell_ref, fields_ref, geom_ref, rows_ref, sem):

time: 59.7 us -> 59.6 us (level)
  no operation moved by 1% of the time
where the time goes in v8:
time: 59.6 us; the launch traced here: 59.3 us
  starting transfers between devices  22.1 us (37%)
  Pallas kernels  21.6 us (36%)
  waiting for transfers between devices  14.6 us (24%)
  between operations  0.8 us (1%)
    ppermute x12, starting transfers between devices, over(): return lax.ppermute(array, axis, [(i, i ^ bit) for i in range(count)])  10.9 us
    ppermute x12, waiting for transfers between devices, over(): return lax.ppermute(array, axis, [(i, i ^ bit) for i in range(count)])  9.58 us
    all_to_all x1, starting transfers between devices, per_device(): lax.all_to_all(request, 'vol', split_axis=0, concat_axis=0, tiled=True)  7.29 us
    pallas_call x1, Pallas kernels, smooth(): pl.pallas_call(functools.partial(smooth_kernel, items, per_owner), out_sh...  6.56 us
    pallas_call x1, Pallas kernels, near_payload(): pl.pallas_call(near_payload_kernel, out_shape=jax.ShapeDtypeStruct((PAYLO...  5.69 us
    all_to_all x1, starting transfers between devices, per_device(): lax.all_to_all(spread, 'vol', split_axis=0, concat_axis=0, tiled=True)  3.85 us
    pallas_call x1, Pallas kernels, far_spread(): pl.pallas_call(far_spread_kernel, out_shape=jax.ShapeDtypeStruct((owners,...  3.64 us
    all_to_all x1, waiting for transfers between devices, per_device(): lax.all_to_all(spread, 'vol', split_axis=0, concat_axis=0, tiled=True)  2.82 us
  transfers between devices with their start and end apart: 14, of which 8 were waited for; matrix products, arithmetic and copies ran while one was open for 0% of the time, Pallas kernels for 13%

profile of v8, /device:TPU:0, one launch (start us, length us, event | category | flops | bytes accessed | tf_op | source)
XLA Modules:
  0.0 59.3 jit_solution(6346482174158951733)
XLA Ops:
  0.6 0.0 copy-start
  0.6 2.4 %pack_requests.1 = (f32[8,24,160]{2,1,0:T(8,128)}, s32[1,512]{1,0:T(1,128)}, f32[8,128]{1,0:T(8,128)}) custom-call(f32[8,512]{1,0:T(8,128)} %geom_in.2, s32[1,512]{1,0:T(1,128)} %bitcast.10, s32[1,512]{1,0:T(1,128)} %bitcast.11, s32[1,2048]{1,0:T(1,128)} %bitcast.8, s32[1,512]{1,0:T(1,128)} %bitcast.12), custom_call_target="tpu_custom_call" | custom-call | tf_op jit(solution)/shard_map/pack_requests/pallas_call | solution.py:176
  3.1 7.3 %all-to-all-start = ((f32[8,24,160]{2,1,0:T(8,128)}), f32[8,24,160]{2,1,0:T(8,128)S(1)}, u32[]{:S(2)}, u32[]{:S(2)}) async-start(f32[8,24,160]{2,1,0:T(8,128)} %get-tuple-element.8), calls=%async_computation | async-start | bytes 393216 | tf_op jit(solution)/shard_map/all_to_all | solution.py:813
  10.4 0.0 copy-start.3
  10.4 0.0 copy-start.4
  10.4 5.7 %near_payload.1.refs_0_ = f32[136,128]{1,0:T(8,128)} custom-call(s32[2048]{0:T(1024)} %cell_in.1, f32[4096,128]{1,0:T(8,128)} %fields_ref.1, f32[8,2048]{1,0:T(8,128)} %geom_in.3, s32[1,2048]{1,0:T(1,128)} %bitcast.9, f32[8,128]{1,0:T(8,128)} %get-tuple-element.9.slot_in), custom_call_target="tpu_custom_call" | custom-call | flops 100000000 | bytes 4000000 | tf_op jit(solution)/shard_map/near_payload/pallas_call | solution.py:435
  16.1 0.0 copy-start.2
  16.1 0.0 copy-start.8
  16.1 0.0 copy-start.1
  16.1 0.0 copy-start.5
  16.1 0.0 copy-start.6
  16.1 0.0 copy-start.7
  16.1 2.2 %all-to-all-done.request_in.asked_ref = f32[8,24,160]{2,1,0:T(8,128)S(1)} async-done(((f32[8,24,160]{2,1,0:T(8,128)}), f32[8,24,160]{2,1,0:T(8,128)S(1)}, u32[]{:S(2)}, u32[]{:S(2)}) %all-to-all-start) | async-done | bytes 122912 | tf_op jit(solution)/shard_map/all_to_all | solution.py:813
  18.3 0.0 copy-done
  18.3 3.6 %far_spread.1 = f32[8,16,128]{2,1,0:T(8,128)} custom-call(f32[8,24,160]{2,1,0:T(8,128)S(1)} %all-to-all-done.request_in.asked_ref, f32[4096,128]{1,0:T(8,128)S(1)} %copy-done), custom_call_target="tpu_custom_call" | custom-call | flops 40000000 | bytes 4000000 | tf_op jit(solution)/shard_map/far_spread/pallas_call | solution.py:355
  22.0 3.9 %all-to-all-start.1 = ((f32[8,16,128]{2,1,0:T(8,128)}), f32[8,16,128]{2,1,0:T(8,128)S(1)}, u32[]{:S(2)}, u32[]{:S(2)}) async-start(f32[8,16,128]{2,1,0:T(8,128)} %far_spread.1), calls=%async_computation.1 | async-start | bytes 131072 | tf_op jit(solution)/shard_map/all_to_all | solution.py:818
  25.8 0.0 copy-done.2
  25.8 3.8 %collective-permute-start.2 = (f32[136,128]{1,0:T(8,128)S(1)}, f32[136,128]{1,0:T(8,128)S(1)}, u32[]{:S(2)}, u32[]{:S(2)}) collective-permute-start(f32[136,128]{1,0:T(8,128)S(1)} %copy-done.2), channel_id=1, source_target_pairs={{0,24},{4,28},{8,16},{12,20},{16,8},{20,12},{24,0},{28,4},{1,25},{... | collective-permute-start | bytes 208904 | tf_op jit(solution)/shard_map/ppermute | solution.py:782
  29.6 0.0 collective-permute-start.1
  29.6 0.6 %collective-permute-start = (f32[136,128]{1,0:T(8,128)S(1)}, f32[136,128]{1,0:T(8,128)S(1)}, u32[]{:S(2)}, u32[]{:S(2)}) collective-permute-start(f32[136,128]{1,0:T(8,128)S(1)} %copy-done.2), channel_id=1, source_target_pairs={{0,8},{4,12},{8,0},{12,4},{16,24},{20,28},{24,16},{28,20},{1,9},{5... | collective-permute-start | bytes 208904 | tf_op jit(solution)/shard_map/ppermute | solution.py:782
  30.3 0.1 pad_add_fusion.where_ref
  30.4 2.8 %all-to-all-done.1.spread_ref = f32[8,16,128]{2,1,0:T(8,128)S(1)} async-done(((f32[8,16,128]{2,1,0:T(8,128)}), f32[8,16,128]{2,1,0:T(8,128)S(1)}, u32[]{:S(2)}, u32[]{:S(2)}) %all-to-all-start.1) | async-done | bytes 65568 | tf_op jit(solution)/shard_map/all_to_all | solution.py:818
  33.2 2.1 %far_line.1 = (f32[512,128]{1,0:T(8,128)S(1)}, f32[4,128]{1,0:T(4,128)}) custom-call(s32[3]{0:T(128)S(1)} %pad_add_fusion.where_ref, f32[8,16,128]{2,1,0:T(8,128)S(1)} %all-to-all-done.1.spread_ref, f32[8,24,160]{2,1,0:T(8,128)S(1)} %all-to-all-done.request_in.asked_ref), custom_call_target="tpu_custom_call" | custom-call | flops 100000000 | bytes 1000000 | tf_op jit(solution)/shard_map/far_line/pallas_call | solution.py:741
  35.2 0.0 collective-permute-done.2.refs_3_
  35.3 0.6 %collective-permute-done.1.refs_2_ = f32[136,128]{1,0:T(8,128)S(1)} collective-permute-done((f32[136,128]{1,0:T(8,128)S(1)}, f32[136,128]{1,0:T(8,128)S(1)}, u32[]{:S(2)}, u32[]{:S(2)}) %collective-permute-start.1) | collective-permute-done | bytes 69664 | tf_op jit(solution)/shard_map/ppermute | solution.py:782
  35.9 0.0 collective-permute-done.refs_1_
  35.9 0.0 copy-done.3
  35.9 0.0 copy-done.4
  35.9 1.2 %join.1.rest_0_ = f32[544,128]{1,0:T(8,128)S(1)} custom-call(s32[3]{0:T(128)S(1)} %pad_add_fusion.where_ref, f32[512,128]{1,0:T(8,128)S(1)} %get-tuple-element.12.far_ref, f32[64,64]{1,0:T(8,128)S(1)} %copy-done.4, f32[128,128]{1,0:T(8,128)S(1)} %copy-done.3, f32[136,128]{1,0:T(8,128)S(1)} %copy-done.2, f32[136,128]{1,0:T(8,128)S(1)} %collective-permute-done.refs_1_, ...), custom_call_target="tpu_custom_call" | custom-call | tf_op jit(solution)/shard_map/join/pallas_call | solution.py:769
  37.1 1.5 %collective-permute-start.6 = (f32[544,128]{1,0:T(8,128)S(1)}, f32[544,128]{1,0:T(8,128)S(1)}, u32[]{:S(2)}, u32[]{:S(2)}) collective-permute-start(f32[544,128]{1,0:T(8,128)S(1)} %join.1.rest_0_), channel_id=1, source_target_pairs={{0,4},{4,0},{8,12},{12,8},{16,20},{20,16},{24,28},{28,24},{1,5},{5... | collective-permute-start | bytes 835592 | tf_op jit(solution)/shard_map/ppermute | solution.py:782
  38.6 1.5 %collective-permute-start.4 = (f32[544,128]{1,0:T(8,128)S(1)}, f32[544,128]{1,0:T(8,128)S(1)}, u32[]{:S(2)}, u32[]{:S(2)}) collective-permute-start(f32[544,128]{1,0:T(8,128)S(1)} %join.1.rest_0_), channel_id=1, source_target_pairs={{0,2},{1,3},{2,0},{3,1},{4,6},{5,7},{6,4},{7,5},{8,10},{9,11},{10,... | collective-permute-start | bytes 835592 | tf_op jit(solution)/shard_map/ppermute | solution.py:782
  40.1 0.0 collective-permute-start.3
  40.1 4.4 %collective-permute-done.6.rest_4_ = f32[544,128]{1,0:T(8,128)S(1)} collective-permute-done((f32[544,128]{1,0:T(8,128)S(1)}, f32[544,128]{1,0:T(8,128)S(1)}, u32[]{:S(2)}, u32[]{:S(2)}) %collective-permute-start.6) | collective-permute-done | bytes 278560 | tf_op jit(solution)/shard_map/ppermute | solution.py:782
  44.5 1.6 %collective-permute-start.8 = (f32[272,128]{1,0:T(8,128)S(1)}, f32[272,128]{1,0:T(8,128)S(1)}, u32[]{:S(2)}, u32[]{:S(2)}) collective-permute-start(f32[272,128]{1,0:T(8,128)S(1)} %slice.8), channel_id=1, source_target_pairs={{0,2},{1,3},{2,0},{3,1},{4,6},{5,7},{6,4},{7,5},{8,10},{9,11},{10,... | collective-permute-start | bytes 417800 | tf_op jit(solution)/shard_map/ppermute | solution.py:782
  46.1 0.1 collective-permute-done.4.rest_2_
  46.2 1.4 %collective-permute-start.9 = (f32[272,128]{1,0:T(8,128)S(1)}, f32[272,128]{1,0:T(8,128)S(1)}, u32[]{:S(2)}, u32[]{:S(2)}) collective-permute-start(f32[272,128]{1,0:T(8,128)S(1)} %slice.9), channel_id=1, source_target_pairs={{0,4},{4,0},{8,12},{12,8},{16,20},{20,16},{24,28},{28,24},{1,5},{5... | collective-permute-start | bytes 417800 | tf_op jit(solution)/shard_map/ppermute | solution.py:782
  47.6 0.0 collective-permute-start.7
  47.6 0.5 collective-permute-start.5
  48.1 1.5 %collective-permute-done.8.rest_6_ = f32[272,128]{1,0:T(8,128)S(1)} collective-permute-done((f32[272,128]{1,0:T(8,128)S(1)}, f32[272,128]{1,0:T(8,128)S(1)}, u32[]{:S(2)}, u32[]{:S(2)}) %collective-permute-start.8) | collective-permute-done | bytes 139296 | tf_op jit(solution)/shard_map/ppermute | solution.py:782
  49.6 0.0 collective-permute-start.10
  49.6 1.7 %collective-permute-done.9.rest_7_ = f32[272,128]{1,0:T(8,128)S(1)} collective-permute-done((f32[272,128]{1,0:T(8,128)S(1)}, f32[272,128]{1,0:T(8,128)S(1)}, u32[]{:S(2)}, u32[]{:S(2)}) %collective-permute-start.9) | collective-permute-done | bytes 139296 | tf_op jit(solution)/shard_map/ppermute | solution.py:782
  51.3 0.0 collective-permute-start.11
  51.3 0.0 copy-done.8
  51.3 0.1 copy.17.adj_ref
  51.4 0.0 collective-permute-done.3.rest_1_
  51.4 0.0 collective-permute-done.10.rest_8_
  51.4 0.0 collective-permute-done.7.rest_5_
  51.4 1.2 %collective-permute-done.11.rest_9_ = f32[272,128]{1,0:T(8,128)S(1)} collective-permute-done((f32[272,128]{1,0:T(8,128)S(1)}, f32[272,128]{1,0:T(8,128)S(1)}, u32[]{:S(2)}, u32[]{:S(2)}) %collective-permute-start.11) | collective-permute-done | bytes 139296 | tf_op jit(solution)/shard_map/ppermute | solution.py:782
  52.7 0.0 collective-permute-done.5.rest_3_
  52.7 0.0 copy-done.1
  52.7 0.0 copy-done.5
  52.7 0.0 copy-done.6
  52.7 0.0 copy-done.7
  52.7 6.6 %smooth.1 = f32[24,64,64]{2,1,0:T(8,128)} custom-call(s32[3]{0:T(128)S(1)} %pad_add_fusion.where_ref, s32[96,4]{1,0:T(8,128)S(1)} %copy.17.adj_ref, f32[256,512]{1,0:T(8,128)S(1)} %copy-done.1, f32[64,64]{1,0:T(8,128)S(1)} %copy-done.4, f32[128,128]{1,0:T(8,128)S(1)} %copy-done.3, f32[64,128]{1,0:T(8,128)S(1)} %copy-done.5, f32[8,64]{1,0:T(8,128)S(1)} %copy-done.7, ...), custom_call_target="tpu_custom_call" | custom-call | tf_op jit(solution)/shard_map/smooth/pallas_call | solution.py:692
  (2 shorter events, 0.0 us)
Async XLA Ops:
  0.6 17.7 %copy-start = (f32[4096,128]{1,0:T(8,128)S(1)}, f32[4096,128]{1,0:T(8,128)}, u32[]{:S(2)}) copy-start(f32[4096,128]{1,0:T(8,128)} %fields_ref.1) | copy-start | bytes 6291460
  3.1 15.2 %all-to-all-start = ((f32[8,24,160]{2,1,0:T(8,128)}), f32[8,24,160]{2,1,0:T(8,128)S(1)}, u32[]{:S(2)}, u32[]{:S(2)}) async-start(f32[8,24,160]{2,1,0:T(8,128)} %get-tuple-element.8), calls=%async_computation | async-start | bytes 393216 | tf_op jit(solution)/shard_map/all_to_all | solution.py:813
  10.4 25.5 %copy-start.3 = (f32[128,128]{1,0:T(8,128)S(1)}, f32[128,128]{1,0:T(8,128)}, u32[]{:S(2)}) copy-start(f32[128,128]{1,0:T(8,128)} %constant.35.clone.pair_ref) | copy-start | bytes 196612
  10.4 25.5 %copy-start.4 = (f32[64,64]{1,0:T(8,128)S(1)}, f32[64,64]{1,0:T(8,128)}, u32[]{:S(2)}) copy-start(f32[64,64]{1,0:T(8,128)} %constant.34.clone.basis_ref) | copy-start | bytes 49156
  16.1 9.7 %copy-start.2 = (f32[136,128]{1,0:T(8,128)S(1)}, f32[136,128]{1,0:T(8,128)}, u32[]{:S(2)}) copy-start(f32[136,128]{1,0:T(8,128)} %near_payload.1.refs_0_) | copy-start | bytes 208900
  16.1 35.2 %copy-start.8 = (s32[96,4]{0,1:T(4,128)S(1)}, s32[96,4]{0,1:T(4,128)}, u32[]{:S(2)}) copy-start(s32[96,4]{0,1:T(4,128)} %param.23) | copy-start | bytes 4612
  16.1 36.6 %copy-start.1 = (f32[256,512]{1,0:T(8,128)S(1)}, f32[256,512]{1,0:T(8,128)}, u32[]{:S(2)}) copy-start(f32[256,512]{1,0:T(8,128)} %constant.39.clone.coupling_ref) | copy-start | bytes 1572868
  16.1 36.6 %copy-start.5 = (f32[64,128]{1,0:T(8,128)S(1)}, f32[64,128]{1,0:T(8,128)}, u32[]{:S(2)}) copy-start(f32[64,128]{1,0:T(8,128)} %constant.38.clone.series_ref) | copy-start | bytes 98308
  16.1 36.6 %copy-start.6 = (f32[8,128]{1,0:T(8,128)S(1)}, f32[8,128]{1,0:T(8,128)}, u32[]{:S(2)}) copy-start(f32[8,128]{1,0:T(8,128)} %constant.37.clone.scale_ref) | copy-start | bytes 12292
  16.1 36.6 %copy-start.7 = (f32[8,64]{1,0:T(8,128)S(1)}, f32[8,64]{1,0:T(8,128)}, u32[]{:S(2)}) copy-start(f32[8,64]{1,0:T(8,128)} %constant.36.clone.edge_ref) | copy-start | bytes 6148
  22.0 11.2 %all-to-all-start.1 = ((f32[8,16,128]{2,1,0:T(8,128)}), f32[8,16,128]{2,1,0:T(8,128)S(1)}, u32[]{:S(2)}, u32[]{:S(2)}) async-start(f32[8,16,128]{2,1,0:T(8,128)} %far_spread.1), calls=%async_computation.1 | async-start | bytes 131072 | tf_op jit(solution)/shard_map/all_to_all | solution.py:818
  25.8 9.4 %collective-permute-start.2 = (f32[136,128]{1,0:T(8,128)S(1)}, f32[136,128]{1,0:T(8,128)S(1)}, u32[]{:S(2)}, u32[]{:S(2)}) collective-permute-start(f32[136,128]{1,0:T(8,128)S(1)} %copy-done.2), channel_id=1, source_target_pairs={{0,24},{4,28},{8,16},{12,20},{16,8},{20,12},{24,0},{28,4},{1,25},{... | collective-permute-start | bytes 208904 | tf_op jit(solution)/shard_map/ppermute | solution.py:782
  29.6 6.2 %collective-permute-start.1 = (f32[136,128]{1,0:T(8,128)S(1)}, f32[136,128]{1,0:T(8,128)S(1)}, u32[]{:S(2)}, u32[]{:S(2)}) collective-permute-start(f32[136,128]{1,0:T(8,128)S(1)} %copy-done.2), channel_id=1, source_target_pairs={{0,16},{4,20},{8,24},{12,28},{16,0},{20,4},{24,8},{28,12},{1,17},{... | collective-permute-start | bytes 208904 | tf_op jit(solution)/shard_map/ppermute | solution.py:782
  29.6 6.2 %collective-permute-start = (f32[136,128]{1,0:T(8,128)S(1)}, f32[136,128]{1,0:T(8,128)S(1)}, u32[]{:S(2)}, u32[]{:S(2)}) collective-permute-start(f32[136,128]{1,0:T(8,128)S(1)} %copy-done.2), channel_id=1, source_target_pairs={{0,8},{4,12},{8,0},{12,4},{16,24},{20,28},{24,16},{28,20},{1,9},{5... | collective-permute-start | bytes 208904 | tf_op jit(solution)/shard_map/ppermute | solution.py:782
  37.1 7.4 %collective-permute-start.6 = (f32[544,128]{1,0:T(8,128)S(1)}, f32[544,128]{1,0:T(8,128)S(1)}, u32[]{:S(2)}, u32[]{:S(2)}) collective-permute-start(f32[544,128]{1,0:T(8,128)S(1)} %join.1.rest_0_), channel_id=1, source_target_pairs={{0,4},{4,0},{8,12},{12,8},{16,20},{20,16},{24,28},{28,24},{1,5},{5... | collective-permute-start | bytes 835592 | tf_op jit(solution)/shard_map/ppermute | solution.py:782
  38.6 7.6 %collective-permute-start.4 = (f32[544,128]{1,0:T(8,128)S(1)}, f32[544,128]{1,0:T(8,128)S(1)}, u32[]{:S(2)}, u32[]{:S(2)}) collective-permute-start(f32[544,128]{1,0:T(8,128)S(1)} %join.1.rest_0_), channel_id=1, source_target_pairs={{0,2},{1,3},{2,0},{3,1},{4,6},{5,7},{6,4},{7,5},{8,10},{9,11},{10,... | collective-permute-start | bytes 835592 | tf_op jit(solution)/shard_map/ppermute | solution.py:782
  40.1 11.3 %collective-permute-start.3 = (f32[544,128]{1,0:T(8,128)S(1)}, f32[544,128]{1,0:T(8,128)S(1)}, u32[]{:S(2)}, u32[]{:S(2)}) collective-permute-start(f32[544,128]{1,0:T(8,128)S(1)} %join.1.rest_0_), channel_id=1, source_target_pairs={{0,1},{1,0},{2,3},{3,2},{4,5},{5,4},{6,7},{7,6},{8,9},{9,8},{10,11... | collective-permute-start | bytes 835592 | tf_op jit(solution)/shard_map/ppermute | solution.py:782
  44.5 5.1 %collective-permute-start.8 = (f32[272,128]{1,0:T(8,128)S(1)}, f32[272,128]{1,0:T(8,128)S(1)}, u32[]{:S(2)}, u32[]{:S(2)}) collective-permute-start(f32[272,128]{1,0:T(8,128)S(1)} %slice.8), channel_id=1, source_target_pairs={{0,2},{1,3},{2,0},{3,1},{4,6},{5,7},{6,4},{7,5},{8,10},{9,11},{10,... | collective-permute-start | bytes 417800 | tf_op jit(solution)/shard_map/ppermute | solution.py:782
  46.2 5.1 %collective-permute-start.9 = (f32[272,128]{1,0:T(8,128)S(1)}, f32[272,128]{1,0:T(8,128)S(1)}, u32[]{:S(2)}, u32[]{:S(2)}) collective-permute-start(f32[272,128]{1,0:T(8,128)S(1)} %slice.9), channel_id=1, source_target_pairs={{0,4},{4,0},{8,12},{12,8},{16,20},{20,16},{24,28},{28,24},{1,5},{5... | collective-permute-start | bytes 417800 | tf_op jit(solution)/shard_map/ppermute | solution.py:782
  47.6 3.9 %collective-permute-start.7 = (f32[544,128]{1,0:T(8,128)S(1)}, f32[544,128]{1,0:T(8,128)S(1)}, u32[]{:S(2)}, u32[]{:S(2)}) collective-permute-start(f32[544,128]{1,0:T(8,128)S(1)} %collective-permute-done.6.rest_4_), channel_id=1, source_target_pairs={{0,1},{1,0},{2,3},{3,2},{4,5},{5,4},{6,7},{7,6},{8,9},{9,8},{10,11... | collective-permute-start | bytes 835592 | tf_op jit(solution)/shard_map/ppermute | solution.py:782
  47.6 5.1 %collective-permute-start.5 = (f32[544,128]{1,0:T(8,128)S(1)}, f32[544,128]{1,0:T(8,128)S(1)}, u32[]{:S(2)}, u32[]{:S(2)}) collective-permute-start(f32[544,128]{1,0:T(8,128)S(1)} %collective-permute-done.4.rest_2_), channel_id=1, source_target_pairs={{0,1},{1,0},{2,3},{3,2},{4,5},{5,4},{6,7},{7,6},{8,9},{9,8},{10,11... | collective-permute-start | bytes 835592 | tf_op jit(solution)/shard_map/ppermute | solution.py:782
  49.6 1.8 %collective-permute-start.10 = (f32[272,128]{1,0:T(8,128)S(1)}, f32[272,128]{1,0:T(8,128)S(1)}, u32[]{:S(2)}, u32[]{:S(2)}) collective-permute-start(f32[272,128]{1,0:T(8,128)S(1)} %collective-permute-done.8.rest_6_), channel_id=1, source_target_pairs={{0,1},{1,0},{2,3},{3,2},{4,5},{5,4},{6,7},{7,6},{8,9},{9,8},{10,11... | collective-permute-start | bytes 417800 | tf_op jit(solution)/shard_map/ppermute | solution.py:782
  51.3 1.4 %collective-permute-start.11 = (f32[272,128]{1,0:T(8,128)S(1)}, f32[272,128]{1,0:T(8,128)S(1)}, u32[]{:S(2)}, u32[]{:S(2)}) collective-permute-start(f32[272,128]{1,0:T(8,128)S(1)} %collective-permute-done.9.rest_7_), channel_id=1, source_target_pairs={{0,1},{1,0},{2,3},{3,2},{4,5},{5,4},{6,7},{7,6},{8,9},{9,8},{10,11... | collective-permute-start | bytes 417800 | tf_op jit(solution)/shard_map/ppermute | solution.py:782
